TPU v7x, 512 devices: a whole 4x8x8 slice. The times are simulated.
512 devices in a mesh: grp: 32 (over y, x), head: 16 (over z, core).
Axes of the slice: x: 4, y: 8, z: 8, core: 2. Of those that a mesh axis runs over, the one named last changes fastest.
Arguments:
- q_nope: bfloat16 [4, 1024, 128, 128], P(None, 'grp', 'head'), may hold values from -6 to 6
- q_rope: bfloat16 [4, 1024, 128, 64], P(None, 'grp', 'head'), may hold values from -512 to 512
- w_absorb_k: bfloat16 [128, 128, 512], P('head'), may hold values from -0.5 to 0.5
- w_absorb_v: bfloat16 [128, 512, 128], P('head'), may hold values from -0.25 to 0.25
- latent_cache: bfloat16 [1024, 1024, 576], P(('grp', 'head')), may hold values from -4 to 4
- new_latent: bfloat16 [4, 1024, 576], P(None, ('grp', 'head')), may hold values from -6 to 6
- lengths: int32 [1024], replicated, may hold values from 128 to 1020, as said below
- moves: int32 [16, 1], P('head'), may hold values from 1 to 31
Outputs:
- attended: bfloat16 [4, 1024, 128, 128], P(None, 'grp', 'head')
Inputs may be any that keep to these rules, and one draw needn't show every extreme that they name: lengths[r] counts the live rows of latent_cache[r]; its later rows up to 1024 are padding that no query reads.
All inputs are finite; a program needn't handle non-finite values.
Results may differ from a plain program's by a relative error of at most 0.0077.
Values may be sent and summed in bfloat16 or wider, within the bound.
No kernel may reach another device: no remote copies, remote signals or barrier semaphores. Data moves between devices by JAX's collectives and lax.ppermute only.
A program may use at most 64 MiB of HBM per device.

v0:
```python
import math

import jax
import jax.numpy as jnp
from jax import lax
from jax.sharding import PartitionSpec as P

HEAD_DIM = 128
ROPE = 64
LATENT = 512
BLOCK = 128


yarn_gain = (0.1 * math.log(40.0) + 1.0) ** 2


def passed_along(value, axis, steps):
    count = lax.axis_size(axis)
    pairs = [(source, (source + steps) % count) for source in range(count)]
    return lax.ppermute(value, axis, pairs)


def attend(queries, stored, counts, recent, moment, window, score_scale):
    holders = queries.shape[0]
    head_count = queries.shape[1]
    capacity = stored.shape[1]
    longest = jnp.max(counts)
    passes = (longest + window - 1) // window
    positions = jnp.arange(window, dtype=jnp.int32)

    def score_tile(tile_index, buffer):
        begin_at = tile_index * window
        key_rows = lax.dynamic_slice_in_dim(stored, begin_at, window, 1)
        partial_value = (
            jnp.einsum("rhc,rtc->rht", queries, key_rows, preferred_element_type=jnp.float32)
            * score_scale
        )
        inside = (begin_at + positions)[None, None, :] < counts[:, None, None]
        partial_value = jnp.where(inside, partial_value, -jnp.inf)
        return lax.dynamic_update_slice_in_dim(buffer, partial_value, begin_at, 2)

    empty = jnp.full((holders, head_count, capacity), -jnp.inf, jnp.float32)
    scores = lax.fori_loop(0, passes, score_tile, empty)
    extra_scores = (
        jnp.einsum("rhc,rjc->rhj", queries, recent, preferred_element_type=jnp.float32)
        * score_scale
    )
    step_live = jnp.arange(recent.shape[1], dtype=jnp.int32) <= moment
    extra_scores = jnp.where(step_live[None, None, :], extra_scores, -jnp.inf)
    peak = jnp.maximum(jnp.max(scores, axis=2), jnp.max(extra_scores, axis=2))[:, :, None]
    spread = jnp.exp(scores - peak)
    spread_new = jnp.exp(extra_scores - peak)
    softmax_sum = jnp.sum(spread, axis=2, keepdims=True) + jnp.sum(
        spread_new, axis=2, keepdims=True
    )
    weights = (spread / softmax_sum).astype(jnp.bfloat16)
    weights_new = (spread_new / softmax_sum).astype(jnp.bfloat16)
    start_value = jnp.einsum(
        "rhj,rjl->rhl", weights_new, recent[:, :, :LATENT], preferred_element_type=jnp.float32
    )

    def value_tile(tile_index, summed):
        begin_at = tile_index * window
        key_rows = lax.dynamic_slice_in_dim(stored, begin_at, window, 1)[:, :, :LATENT]
        weight_tile = lax.dynamic_slice_in_dim(weights, begin_at, window, 2)
        return summed + jnp.einsum(
            "rht,rtl->rhl", weight_tile, key_rows, preferred_element_type=jnp.float32
        )

    return lax.fori_loop(0, passes, value_tile, start_value).astype(jnp.bfloat16)


def body(q_nope, q_rope, w_absorb_k, w_absorb_v, latent_cache, new_latent, lengths, moves):
    step_count = q_nope.shape[0]
    holders = latent_cache.shape[0]
    capacity = latent_cache.shape[1]
    entries = latent_cache.shape[2]
    movers = moves.shape[1]
    window = min(4 * BLOCK, capacity)
    score_scale = yarn_gain / math.sqrt(HEAD_DIM + ROPE)
    group_count = lax.axis_size("grp")
    column_count = lax.axis_size("head")
    bit_count = group_count.bit_length() - 1
    offsets = moves[0]
    group_here = lax.axis_index("grp")
    column_here = lax.axis_index("head")
    first_slot = (group_here * column_count + column_here) * holders
    counts = lax.dynamic_slice_in_dim(lengths, first_slot, holders)
    recent = jnp.zeros((holders, step_count, entries), jnp.bfloat16)
    results = []
    for moment in range(step_count):
        q_latent = jnp.einsum(
            "rhd,hdl->rhl", q_nope[moment], w_absorb_k, preferred_element_type=jnp.float32
        ).astype(jnp.bfloat16)
        query_rows = jnp.concatenate([q_latent, q_rope[moment]], axis=2)
        owned_rows = lax.all_to_all(query_rows, "head", split_axis=0, concat_axis=1, tiled=True)
        fresh_rows = new_latent[moment]
        if moment >= 2:
            asking = (owned_rows[:movers], fresh_rows[:movers])
            for level in range(bit_count):
                arrived = passed_along((asking[0], asking[1]), "grp", -(1 << level))
                chosen = offsets >> level & 1 == 1
                asking = (
                    jnp.where(chosen[:, None, None], arrived[0], asking[0]),
                    jnp.where(chosen[:, None], arrived[1], asking[1]),
                )
            owned_rows = jnp.concatenate([asking[0], owned_rows[movers:]], axis=0)
            fresh_rows = jnp.concatenate([asking[1], fresh_rows[movers:]], axis=0)
        recent = recent.at[:, moment].set(fresh_rows)
        latent_out = attend(owned_rows, latent_cache, counts, recent, moment, window, score_scale)
        if moment >= 2:
            answer = latent_out[:movers]
            for level in range(bit_count):
                arrived = passed_along(answer, "grp", 1 << level)
                chosen = offsets >> level & 1 == 1
                answer = jnp.where(chosen[:, None, None], arrived, answer)
            latent_out = jnp.concatenate([answer, latent_out[movers:]], axis=0)
        gathered = lax.all_to_all(latent_out, "head", split_axis=1, concat_axis=0, tiled=True)
        results.append(
            jnp.einsum(
                "rhl,hld->rhd", gathered, w_absorb_v, preferred_element_type=jnp.float32
            ).astype(jnp.bfloat16)
        )
    return jnp.stack(results)


def solution(mesh):
    placed = (
        P(None, "grp", "head", None),
        P(None, "grp", "head", None),
        P("head", None, None),
        P("head", None, None),
        P(("grp", "head"), None, None),
        P(None, ("grp", "head"), None),
        P(),
        P("head", None),
    )
    return jax.shard_map(
        body, mesh=mesh, in_specs=placed, out_specs=P(None, "grp", "head", None), check_vma=False
    )
```

profile of v0, /device:TPU:1, one launch (start us, length us, event | category | flops | bytes accessed | tf_op | source)
XLA Modules:
  0.0 334.2 jit_solution(11688088524110400482)
XLA Ops:
  4.5 11.8 %all-to-all-start = ((bf16[32,8,576]{2,1,0:T(8,128)(2,1)}), bf16[32,8,576]{2,1,0:T(8,128)(2,1)}, u32[]{:S(2)}, u32[]{:S(2)}) async-start(bf16[32,8,576]{2,1,0:T(8,128)(2,1)} %copy.115), calls=%async_computation | async-start | bytes 655360 | tf_op jit(solution)/shard_map/all_to_all | solution.py:96
  16.9 7.3 %collective-permute-start.20 = (bf16[1,576]{1,0:T(2,128)(2,1)}, bf16[1,576]{1,0:T(2,128)(2,1)}, u32[]{:S(2)}, u32[]{:S(2)}) collective-permute-start(bf16[1,576]{1,0:T(2,128)(2,1)} %get-tuple-element.609), channel_id=1, source_target_pairs={{0,496},{16,0},{32,16},{48,32},{64,48},{80,64},{96,80},{112,96},{1... | collective-permute-start | bytes 3464 | tf_op jit(solution)/shard_map/ppermute | solution.py:20
  48.9 5.4 %collective-permute-start.21 = (bf16[1,576]{1,0:T(2,128)(2,1)S(1)}, bf16[1,576]{1,0:T(2,128)(2,1)S(1)}, u32[]{:S(2)}, u32[]{:S(2)}) collective-permute-start(bf16[1,576]{1,0:T(2,128)(2,1)S(1)} %get-tuple-element.607), channel_id=1, source_target_pairs={{0,480},{16,496},{32,0},{48,16},{64,32},{80,48},{96,64},{112,80},{... | collective-permute-start | bytes 3464 | tf_op jit(solution)/shard_map/ppermute | solution.py:20
  65.7 6.2 %collective-permute-start.9 = (bf16[1,576]{1,0:T(2,128)(2,1)S(1)}, bf16[1,576]{1,0:T(2,128)(2,1)S(1)}, u32[]{:S(2)}, u32[]{:S(2)}) collective-permute-start(bf16[1,576]{1,0:T(2,128)(2,1)S(1)} %broadcast_select_fusion.27), channel_id=1, source_target_pairs={{0,256},{16,272},{32,288},{48,304},{64,320},{80,336},{96,352},{112... | collective-permute-start | bytes 3464 | tf_op jit(solution)/shard_map/ppermute | solution.py:20
  75.0 5.2 %collective-permute-done.24 = bf16[1,576]{1,0:T(2,128)(2,1)S(1)} collective-permute-done((bf16[1,576]{1,0:T(2,128)(2,1)S(1)}, bf16[1,576]{1,0:T(2,128)(2,1)S(1)}, u32[]{:S(2)}, u32[]{:S(2)}) %collective-permute-start.24) | collective-permute-done | bytes 1184 | tf_op jit(solution)/shard_map/ppermute | solution.py:20
  80.2 10.9 %all-to-all-start.4 = ((bf16[32,8,576]{2,1,0:T(8,128)(2,1)}), bf16[32,8,576]{2,1,0:T(8,128)(2,1)S(1)}, u32[]{:S(2)}, u32[]{:S(2)}) async-start(bf16[32,8,576]{2,1,0:T(8,128)(2,1)} %copy.137), calls=%async_computation.4 | async-start | bytes 655360 | tf_op jit(solution)/shard_map/all_to_all | solution.py:96
  96.6 7.6 %all-to-all-done.4 = bf16[32,8,576]{2,1,0:T(8,128)(2,1)S(1)} async-done(((bf16[32,8,576]{2,1,0:T(8,128)(2,1)}), bf16[32,8,576]{2,1,0:T(8,128)(2,1)S(1)}, u32[]{:S(2)}, u32[]{:S(2)}) %all-to-all-start.4) | async-done | bytes 294944 | tf_op jit(solution)/shard_map/all_to_all | solution.py:96
  111.9 6.3 %collective-permute-start = (bf16[1,128,576]{1,2,0:T(8,128)(2,1)}, bf16[1,128,576]{1,2,0:T(8,128)(2,1)}, u32[]{:S(2)}, u32[]{:S(2)}) collective-permute-start(bf16[1,128,576]{1,2,0:T(8,128)(2,1)} %copy.139), channel_id=1, source_target_pairs={{0,496},{16,0},{32,16},{48,32},{64,48},{80,64},{96,80},{112,96},{1... | collective-permute-start | bytes 442376 | tf_op jit(solution)/shard_map/ppermute | solution.py:20
  127.3 9.4 %all-to-all-done.6 = bf16[32,8,576]{2,1,0:T(8,128)(2,1)S(1)} async-done(((bf16[32,8,576]{2,1,0:T(8,128)(2,1)}), bf16[32,8,576]{2,1,0:T(8,128)(2,1)S(1)}, u32[]{:S(2)}, u32[]{:S(2)}) %all-to-all-start.6) | async-done | bytes 294944 | tf_op jit(solution)/shard_map/all_to_all | solution.py:96
  136.7 4.1 %all-to-all-start.1 = ((bf16[2,128,512]{2,0,1:T(2,128)(2,1)}), bf16[2,128,512]{2,0,1:T(2,128)(2,1)}, u32[]{:S(2)}, u32[]{:S(2)}) async-start(bf16[2,128,512]{2,0,1:T(2,128)(2,1)} %copy.203), calls=%async_computation.1 | async-start | bytes 524288 | tf_op jit(solution)/shard_map/all_to_all | solution.py:118
  141.0 4.2 %collective-permute-start.15 = (bf16[1,128,576]{1,2,0:T(8,128)(2,1)S(1)}, bf16[1,128,576]{1,2,0:T(8,128)(2,1)S(1)}, u32[]{:S(2)}, u32[]{:S(2)}) collective-permute-start(bf16[1,128,576]{1,2,0:T(8,128)(2,1)S(1)} %copy.151), channel_id=1, source_target_pairs={{0,496},{16,0},{32,16},{48,32},{64,48},{80,64},{96,80},{112,96},{1... | collective-permute-start | bytes 442376 | tf_op jit(solution)/shard_map/ppermute | solution.py:20
  149.3 4.5 %collective-permute-start.1 = (bf16[1,128,576]{1,2,0:T(8,128)(2,1)S(1)}, bf16[1,128,576]{1,2,0:T(8,128)(2,1)S(1)}, u32[]{:S(2)}, u32[]{:S(2)}) collective-permute-start(bf16[1,128,576]{1,2,0:T(8,128)(2,1)S(1)} %broadcast_select_fusion.11), channel_id=1, source_target_pairs={{0,480},{16,496},{32,0},{48,16},{64,32},{80,48},{96,64},{112,80},{... | collective-permute-start | bytes 442376 | tf_op jit(solution)/shard_map/ppermute | solution.py:20
  164.9 4.4 %collective-permute-start.3 = (bf16[1,128,576]{1,2,0:T(8,128)(2,1)S(1)}, bf16[1,128,576]{1,2,0:T(8,128)(2,1)S(1)}, u32[]{:S(2)}, u32[]{:S(2)}) collective-permute-start(bf16[1,128,576]{1,2,0:T(8,128)(2,1)S(1)} %broadcast_select_fusion.15), channel_id=1, source_target_pairs={{0,384},{16,400},{32,416},{48,432},{64,448},{80,464},{96,480},{112... | collective-permute-start | bytes 442376 | tf_op jit(solution)/shard_map/ppermute | solution.py:20
  175.3 4.4 %collective-permute-start.4 = (bf16[1,128,576]{1,2,0:T(8,128)(2,1)S(1)}, bf16[1,128,576]{1,2,0:T(8,128)(2,1)S(1)}, u32[]{:S(2)}, u32[]{:S(2)}) collective-permute-start(bf16[1,128,576]{1,2,0:T(8,128)(2,1)S(1)} %broadcast_select_fusion.17), channel_id=1, source_target_pairs={{0,256},{16,272},{32,288},{48,304},{64,320},{80,336},{96,352},{112... | collective-permute-start | bytes 442376 | tf_op jit(solution)/shard_map/ppermute | solution.py:20
  179.7 4.8 %collective-permute-start.19 = (bf16[1,128,576]{1,2,0:T(8,128)(2,1)S(1)}, bf16[1,128,576]{1,2,0:T(8,128)(2,1)}, u32[]{:S(2)}, u32[]{:S(2)}) collective-permute-start(bf16[1,128,576]{1,2,0:T(8,128)(2,1)S(1)} %broadcast_select_fusion.16), channel_id=1, source_target_pairs={{0,256},{16,272},{32,288},{48,304},{64,320},{80,336},{96,352},{112... | collective-permute-start | bytes 442376 | tf_op jit(solution)/shard_map/ppermute | solution.py:20
  188.6 8.1 %collective-permute-done.19 = bf16[1,128,576]{1,2,0:T(8,128)(2,1)} collective-permute-done((bf16[1,128,576]{1,2,0:T(8,128)(2,1)S(1)}, bf16[1,128,576]{1,2,0:T(8,128)(2,1)}, u32[]{:S(2)}, u32[]{:S(2)}) %collective-permute-start.19) | collective-permute-done | bytes 147488 | tf_op jit(solution)/shard_map/ppermute | solution.py:20
  210.2 6.0 %collective-permute-done.10 = bf16[1,128,512]{2,0,1:T(2,128)(2,1)S(1)} collective-permute-done((bf16[1,128,512]{2,0,1:T(2,128)(2,1)S(1)}, bf16[1,128,512]{2,0,1:T(2,128)(2,1)S(1)}, u32[]{:S(2)}, u32[]{:S(2)}) %collective-permute-start.10) | collective-permute-done | bytes 131104 | tf_op jit(solution)/shard_map/ppermute | solution.py:20
  218.7 4.7 %collective-permute-done.25 = bf16[1,128,512]{2,0,1:T(2,128)(2,1)S(1)} collective-permute-done((bf16[1,128,512]{2,0,1:T(2,128)(2,1)S(1)}, bf16[1,128,512]{2,0,1:T(2,128)(2,1)S(1)}, u32[]{:S(2)}, u32[]{:S(2)}) %collective-permute-start.25) | collective-permute-done | bytes 131104 | tf_op jit(solution)/shard_map/ppermute | solution.py:20
  244.2 5.8 %collective-permute-start.28 = (bf16[1,128,512]{2,0,1:T(2,128)(2,1)S(1)}, bf16[1,128,512]{2,0,1:T(2,128)(2,1)S(1)}, u32[]{:S(2)}, u32[]{:S(2)}) collective-permute-start(bf16[1,128,512]{2,0,1:T(2,128)(2,1)S(1)} %broadcast_select_fusion.4), channel_id=1, source_target_pairs={{0,128},{16,144},{32,160},{48,176},{64,192},{80,208},{96,224},{112... | collective-permute-start | bytes 393224 | tf_op jit(solution)/shard_map/ppermute | solution.py:20
  250.4 12.9 %collective-permute-start.14 = (bf16[1,128,512]{2,0,1:T(2,128)(2,1)S(1)}, bf16[1,128,512]{2,0,1:T(2,128)(2,1)S(1)}, u32[]{:S(2)}, u32[]{:S(2)}) collective-permute-start(bf16[1,128,512]{2,0,1:T(2,128)(2,1)S(1)} %broadcast_select_fusion.7), channel_id=1, source_target_pairs={{0,256},{16,272},{32,288},{48,304},{64,320},{80,336},{96,352},{112... | collective-permute-start | bytes 393224 | tf_op jit(solution)/shard_map/ppermute | solution.py:20
  263.4 26.5 %all-to-all-start.3 = ((bf16[2,128,512]{2,0,1:T(2,128)(2,1)}), bf16[2,128,512]{2,0,1:T(2,128)(2,1)S(1)}, u32[]{:S(2)}, u32[]{:S(2)}) async-start(bf16[2,128,512]{2,0,1:T(2,128)(2,1)} %copy.202), calls=%async_computation.3 | async-start | bytes 524288 | tf_op jit(solution)/shard_map/all_to_all | solution.py:118
  294.6 7.3 %all-to-all-done.3 = bf16[2,128,512]{2,0,1:T(2,128)(2,1)S(1)} async-done(((bf16[2,128,512]{2,0,1:T(2,128)(2,1)}), bf16[2,128,512]{2,0,1:T(2,128)(2,1)S(1)}, u32[]{:S(2)}, u32[]{:S(2)}) %all-to-all-start.3) | async-done | bytes 262176 | tf_op jit(solution)/shard_map/all_to_all | solution.py:118
  316.2 4.8 %all-to-all-start.7 = ((bf16[2,128,512]{2,0,1:T(2,128)(2,1)}), bf16[2,128,512]{2,0,1:T(2,128)(2,1)S(1)}, u32[]{:S(2)}, u32[]{:S(2)}) async-start(bf16[2,128,512]{2,0,1:T(2,128)(2,1)} %pad_maximum_fusion.7), calls=%async_computation.7 | async-start | bytes 524288 | tf_op jit(solution)/shard_map/all_to_all | solution.py:118
  322.2 10.6 %all-to-all-done.7 = bf16[2,128,512]{2,0,1:T(2,128)(2,1)S(1)} async-done(((bf16[2,128,512]{2,0,1:T(2,128)(2,1)}), bf16[2,128,512]{2,0,1:T(2,128)(2,1)S(1)}, u32[]{:S(2)}, u32[]{:S(2)}) %all-to-all-start.7) | async-done | bytes 262176 | tf_op jit(solution)/shard_map/all_to_all | solution.py:118
  (241 shorter events, 163.2 us)
Async XLA Ops:
  4.5 75.7 %all-to-all-start = ((bf16[32,8,576]{2,1,0:T(8,128)(2,1)}), bf16[32,8,576]{2,1,0:T(8,128)(2,1)}, u32[]{:S(2)}, u32[]{:S(2)}) async-start(bf16[32,8,576]{2,1,0:T(8,128)(2,1)} %copy.115), calls=%async_computation | async-start | bytes 655360 | tf_op jit(solution)/shard_map/all_to_all | solution.py:96
  16.9 26.1 %collective-permute-start.20 = (bf16[1,576]{1,0:T(2,128)(2,1)}, bf16[1,576]{1,0:T(2,128)(2,1)}, u32[]{:S(2)}, u32[]{:S(2)}) collective-permute-start(bf16[1,576]{1,0:T(2,128)(2,1)} %get-tuple-element.609), channel_id=1, source_target_pairs={{0,496},{16,0},{32,16},{48,32},{64,48},{80,64},{96,80},{112,96},{1... | collective-permute-start | bytes 3464 | tf_op jit(solution)/shard_map/ppermute | solution.py:20
  24.2 18.8 %collective-permute-start.5 = (bf16[1,576]{1,0:T(2,128)(2,1)}, bf16[1,576]{1,0:T(2,128)(2,1)}, u32[]{:S(2)}, u32[]{:S(2)}) collective-permute-start(bf16[1,576]{1,0:T(2,128)(2,1)} %get-tuple-element.611), channel_id=1, source_target_pairs={{0,496},{16,0},{32,16},{48,32},{64,48},{80,64},{96,80},{112,96},{1... | collective-permute-start | bytes 3464 | tf_op jit(solution)/shard_map/ppermute | solution.py:20
  43.1 11.3 %collective-permute-start.6 = (bf16[1,576]{1,0:T(2,128)(2,1)S(1)}, bf16[1,576]{1,0:T(2,128)(2,1)S(1)}, u32[]{:S(2)}, u32[]{:S(2)}) collective-permute-start(bf16[1,576]{1,0:T(2,128)(2,1)S(1)} %get-tuple-element.608), channel_id=1, source_target_pairs={{0,480},{16,496},{32,0},{48,16},{64,32},{80,48},{96,64},{112,80},{... | collective-permute-start | bytes 3464 | tf_op jit(solution)/shard_map/ppermute | solution.py:20
  80.2 24.0 %all-to-all-start.4 = ((bf16[32,8,576]{2,1,0:T(8,128)(2,1)}), bf16[32,8,576]{2,1,0:T(8,128)(2,1)S(1)}, u32[]{:S(2)}, u32[]{:S(2)}) async-start(bf16[32,8,576]{2,1,0:T(8,128)(2,1)} %copy.137), calls=%async_computation.4 | async-start | bytes 655360 | tf_op jit(solution)/shard_map/all_to_all | solution.py:96
  104.2 16.1 %all-to-all-start.2 = ((bf16[32,8,576]{2,1,0:T(8,128)(2,1)}), bf16[32,8,576]{2,1,0:T(8,128)(2,1)S(1)}, u32[]{:S(2)}, u32[]{:S(2)}) async-start(bf16[32,8,576]{2,1,0:T(8,128)(2,1)} %copy.126), calls=%async_computation.2 | async-start | bytes 655360 | tf_op jit(solution)/shard_map/all_to_all | solution.py:96
  111.9 36.5 %collective-permute-start = (bf16[1,128,576]{1,2,0:T(8,128)(2,1)}, bf16[1,128,576]{1,2,0:T(8,128)(2,1)}, u32[]{:S(2)}, u32[]{:S(2)}) collective-permute-start(bf16[1,128,576]{1,2,0:T(8,128)(2,1)} %copy.139), channel_id=1, source_target_pairs={{0,496},{16,0},{32,16},{48,32},{64,48},{80,64},{96,80},{112,96},{1... | collective-permute-start | bytes 442376 | tf_op jit(solution)/shard_map/ppermute | solution.py:20
  120.3 16.4 %all-to-all-start.6 = ((bf16[32,8,576]{2,1,0:T(8,128)(2,1)}), bf16[32,8,576]{2,1,0:T(8,128)(2,1)S(1)}, u32[]{:S(2)}, u32[]{:S(2)}) async-start(bf16[32,8,576]{2,1,0:T(8,128)(2,1)} %copy.149), calls=%async_computation.6 | async-start | bytes 655360 | tf_op jit(solution)/shard_map/all_to_all | solution.py:96
  136.7 126.7 %all-to-all-start.1 = ((bf16[2,128,512]{2,0,1:T(2,128)(2,1)}), bf16[2,128,512]{2,0,1:T(2,128)(2,1)}, u32[]{:S(2)}, u32[]{:S(2)}) async-start(bf16[2,128,512]{2,0,1:T(2,128)(2,1)} %copy.203), calls=%async_computation.1 | async-start | bytes 524288 | tf_op jit(solution)/shard_map/all_to_all | solution.py:118
  141.0 12.8 %collective-permute-start.15 = (bf16[1,128,576]{1,2,0:T(8,128)(2,1)S(1)}, bf16[1,128,576]{1,2,0:T(8,128)(2,1)S(1)}, u32[]{:S(2)}, u32[]{:S(2)}) collective-permute-start(bf16[1,128,576]{1,2,0:T(8,128)(2,1)S(1)} %copy.151), channel_id=1, source_target_pairs={{0,496},{16,0},{32,16},{48,32},{64,48},{80,64},{96,80},{112,96},{1... | collective-permute-start | bytes 442376 | tf_op jit(solution)/shard_map/ppermute | solution.py:20
  164.9 10.3 %collective-permute-start.3 = (bf16[1,128,576]{1,2,0:T(8,128)(2,1)S(1)}, bf16[1,128,576]{1,2,0:T(8,128)(2,1)S(1)}, u32[]{:S(2)}, u32[]{:S(2)}) collective-permute-start(bf16[1,128,576]{1,2,0:T(8,128)(2,1)S(1)} %broadcast_select_fusion.15), channel_id=1, source_target_pairs={{0,384},{16,400},{32,416},{48,432},{64,448},{80,464},{96,480},{112... | collective-permute-start | bytes 442376 | tf_op jit(solution)/shard_map/ppermute | solution.py:20
  169.4 10.3 %collective-permute-start.18 = (bf16[1,128,576]{1,2,0:T(8,128)(2,1)S(1)}, bf16[1,128,576]{1,2,0:T(8,128)(2,1)S(1)}, u32[]{:S(2)}, u32[]{:S(2)}) collective-permute-start(bf16[1,128,576]{1,2,0:T(8,128)(2,1)S(1)} %broadcast_select_fusion.14), channel_id=1, source_target_pairs={{0,384},{16,400},{32,416},{48,432},{64,448},{80,464},{96,480},{112... | collective-permute-start | bytes 442376 | tf_op jit(solution)/shard_map/ppermute | solution.py:20
  179.7 16.9 %collective-permute-start.19 = (bf16[1,128,576]{1,2,0:T(8,128)(2,1)S(1)}, bf16[1,128,576]{1,2,0:T(8,128)(2,1)}, u32[]{:S(2)}, u32[]{:S(2)}) collective-permute-start(bf16[1,128,576]{1,2,0:T(8,128)(2,1)S(1)} %broadcast_select_fusion.16), channel_id=1, source_target_pairs={{0,256},{16,272},{32,288},{48,304},{64,320},{80,336},{96,352},{112... | collective-permute-start | bytes 442376 | tf_op jit(solution)/shard_map/ppermute | solution.py:20
  204.3 11.9 %collective-permute-start.10 = (bf16[1,128,512]{2,0,1:T(2,128)(2,1)S(1)}, bf16[1,128,512]{2,0,1:T(2,128)(2,1)S(1)}, u32[]{:S(2)}, u32[]{:S(2)}) collective-permute-start(bf16[1,128,512]{2,0,1:T(2,128)(2,1)S(1)} %bitcast.182), channel_id=1, source_target_pairs={{0,16},{16,32},{32,48},{48,64},{64,80},{80,96},{96,112},{112,128},... | collective-permute-start | bytes 393224 | tf_op jit(solution)/shard_map/ppermute | solution.py:20
  208.3 15.1 %collective-permute-start.25 = (bf16[1,128,512]{2,0,1:T(2,128)(2,1)S(1)}, bf16[1,128,512]{2,0,1:T(2,128)(2,1)S(1)}, u32[]{:S(2)}, u32[]{:S(2)}) collective-permute-start(bf16[1,128,512]{2,0,1:T(2,128)(2,1)S(1)} %bitcast.183), channel_id=1, source_target_pairs={{0,16},{16,32},{32,48},{48,64},{64,80},{80,96},{96,112},{112,128},... | collective-permute-start | bytes 393224 | tf_op jit(solution)/shard_map/ppermute | solution.py:20
  216.8 11.1 %collective-permute-start.11 = (bf16[1,128,512]{2,0,1:T(2,128)(2,1)S(1)}, bf16[1,128,512]{2,0,1:T(2,128)(2,1)S(1)}, u32[]{:S(2)}, u32[]{:S(2)}) collective-permute-start(bf16[1,128,512]{2,0,1:T(2,128)(2,1)S(1)} %get-tuple-element.603), channel_id=1, source_target_pairs={{0,32},{16,48},{32,64},{48,80},{64,96},{80,112},{96,128},{112,144}... | collective-permute-start | bytes 393224 | tf_op jit(solution)/shard_map/ppermute | solution.py:20
  224.0 10.7 %collective-permute-start.26 = (bf16[1,128,512]{2,0,1:T(2,128)(2,1)S(1)}, bf16[1,128,512]{2,0,1:T(2,128)(2,1)S(1)}, u32[]{:S(2)}, u32[]{:S(2)}) collective-permute-start(bf16[1,128,512]{2,0,1:T(2,128)(2,1)S(1)} %get-tuple-element.605), channel_id=1, source_target_pairs={{0,32},{16,48},{32,64},{48,80},{64,96},{80,112},{96,128},{112,144}... | collective-permute-start | bytes 393224 | tf_op jit(solution)/shard_map/ppermute | solution.py:20
  239.0 11.0 %collective-permute-start.13 = (bf16[1,128,512]{2,0,1:T(2,128)(2,1)S(1)}, bf16[1,128,512]{2,0,1:T(2,128)(2,1)S(1)}, u32[]{:S(2)}, u32[]{:S(2)}) collective-permute-start(bf16[1,128,512]{2,0,1:T(2,128)(2,1)S(1)} %broadcast_select_fusion.5), channel_id=1, source_target_pairs={{0,128},{16,144},{32,160},{48,176},{64,192},{80,208},{96,224},{112... | collective-permute-start | bytes 393224 | tf_op jit(solution)/shard_map/ppermute | solution.py:20
  244.2 45.7 %collective-permute-start.28 = (bf16[1,128,512]{2,0,1:T(2,128)(2,1)S(1)}, bf16[1,128,512]{2,0,1:T(2,128)(2,1)S(1)}, u32[]{:S(2)}, u32[]{:S(2)}) collective-permute-start(bf16[1,128,512]{2,0,1:T(2,128)(2,1)S(1)} %broadcast_select_fusion.4), channel_id=1, source_target_pairs={{0,128},{16,144},{32,160},{48,176},{64,192},{80,208},{96,224},{112... | collective-permute-start | bytes 393224 | tf_op jit(solution)/shard_map/ppermute | solution.py:20
  250.4 42.5 %collective-permute-start.14 = (bf16[1,128,512]{2,0,1:T(2,128)(2,1)S(1)}, bf16[1,128,512]{2,0,1:T(2,128)(2,1)S(1)}, u32[]{:S(2)}, u32[]{:S(2)}) collective-permute-start(bf16[1,128,512]{2,0,1:T(2,128)(2,1)S(1)} %broadcast_select_fusion.7), channel_id=1, source_target_pairs={{0,256},{16,272},{32,288},{48,304},{64,320},{80,336},{96,352},{112... | collective-permute-start | bytes 393224 | tf_op jit(solution)/shard_map/ppermute | solution.py:20
  263.4 38.6 %all-to-all-start.3 = ((bf16[2,128,512]{2,0,1:T(2,128)(2,1)}), bf16[2,128,512]{2,0,1:T(2,128)(2,1)S(1)}, u32[]{:S(2)}, u32[]{:S(2)}) async-start(bf16[2,128,512]{2,0,1:T(2,128)(2,1)} %copy.202), calls=%async_computation.3 | async-start | bytes 524288 | tf_op jit(solution)/shard_map/all_to_all | solution.py:118
  291.0 19.5 %collective-permute-start.29 = (bf16[1,128,512]{2,0,1:T(2,128)(2,1)}, bf16[1,128,512]{2,0,1:T(2,128)(2,1)}, u32[]{:S(2)}, u32[]{:S(2)}) collective-permute-start(bf16[1,128,512]{2,0,1:T(2,128)(2,1)} %broadcast_select_fusion.6), channel_id=1, source_target_pairs={{0,256},{16,272},{32,288},{48,304},{64,320},{80,336},{96,352},{112... | collective-permute-start | bytes 393224 | tf_op jit(solution)/shard_map/ppermute | solution.py:20
  302.0 14.2 %all-to-all-start.5 = ((bf16[2,128,512]{2,0,1:T(2,128)(2,1)}), bf16[2,128,512]{2,0,1:T(2,128)(2,1)S(1)}, u32[]{:S(2)}, u32[]{:S(2)}) async-start(bf16[2,128,512]{2,0,1:T(2,128)(2,1)} %pad_maximum_fusion.6), calls=%async_computation.5 | async-start | bytes 524288 | tf_op jit(solution)/shard_map/all_to_all | solution.py:118
  316.2 16.5 %all-to-all-start.7 = ((bf16[2,128,512]{2,0,1:T(2,128)(2,1)}), bf16[2,128,512]{2,0,1:T(2,128)(2,1)S(1)}, u32[]{:S(2)}, u32[]{:S(2)}) async-start(bf16[2,128,512]{2,0,1:T(2,128)(2,1)} %pad_maximum_fusion.7), calls=%async_computation.7 | async-start | bytes 524288 | tf_op jit(solution)/shard_map/all_to_all | solution.py:118
  (30 other events, 283.4 us)
where the time goes:
time: 338 us; the launch traced here: 334 us
  starting transfers between devices  180 us (53%)
  waiting for transfers between devices  84 us (25%)
  local copies, waits for them, and re-layouts  26.2 us (8%)
  matrix products  21.2 us (6%)
  other arithmetic  19.8 us (6%)
    ppermute x30, starting transfers between devices, passed_along(): return lax.ppermute(value, axis, pairs)  111 us
    ppermute x30, waiting for transfers between devices, passed_along(): return lax.ppermute(value, axis, pairs)  43.9 us
    all_to_all x4, starting transfers between devices, body(): lax.all_to_all(latent_out, 'head', split_axis=1, concat_axis=0, tiled=True)  39.1 us
    all_to_all x4, starting transfers between devices, body(): lax.all_to_all(query_rows, 'head', split_axis=0, concat_axis=1, tiled=True)  29.6 us
    all_to_all x4, waiting for transfers between devices, body(): lax.all_to_all(latent_out, 'head', split_axis=1, concat_axis=0, tiled=True)  20.9 us
    all_to_all x4, waiting for transfers between devices, body(): lax.all_to_all(query_rows, 'head', split_axis=0, concat_axis=1, tiled=True)  19.2 us
    dot_general x4, matrix products, score_tile(): jnp.einsum('rhc,rtc->rht', queries, key_rows, preferred_element_type=jnp....  7.88 us
  transfers between devices with their start and end apart: 38, of which 20 were waited for; matrix products, arithmetic and copies ran while one was open for 18% of the time, Pallas kernels for 0%

commit v1 on v0

v1 whole, which is shorter than its diff:
```python
import functools
import math

import jax
import jax.numpy as jnp
from jax import lax
from jax.experimental import pallas as pl
from jax.experimental.pallas import tpu as pltpu
from jax.sharding import PartitionSpec as P

HEAD_DIM = 128
ROPE = 64
LATENT = 512
LANES = 128
CHUNKS = LATENT // LANES
UNIT = 16
HIDDEN = -1e30

yarn_gain = (0.1 * math.log(40.0) + 1.0) ** 2
score_scale = yarn_gain / math.sqrt(HEAD_DIM + ROPE)


def split_places(rows, columns):
    wide = rows.astype(jnp.float32).reshape(columns, 2, 8, rows.shape[-1])
    return wide[:, 0], wide[:, 1]


def absorb_kernel(q_ref, r_ref, w_ref, held_ref, moved_ref):
    columns = held_ref.shape[0]
    heads = w_ref.shape[0]
    weights = w_ref[...].reshape(heads * HEAD_DIM, LATENT)
    lane_head = lax.broadcasted_iota(jnp.int32, (columns, UNIT, HEAD_DIM), 1) % heads
    nope = [split_places(q_ref[step], columns) for step in range(4)]
    rope = [split_places(r_ref[step], columns) for step in range(4)]

    def unit_of(parts, first, place):
        return jnp.concatenate([parts[first][place], parts[first + 1][place]], axis=1)

    units = [(2, 0), (0, 0), (0, 1), (2, 1)]
    for number, (first, place) in enumerate(units):
        rows = unit_of(nope, first, place)
        spread = jnp.concatenate(
            [
                jnp.where(lane_head == head, rows, 0.0)
                .astype(jnp.bfloat16)
                .reshape(columns * UNIT, HEAD_DIM)
                for head in range(heads)
            ],
            axis=1,
        )
        latent = jnp.dot(spread, weights, preferred_element_type=jnp.float32)
        latent = latent.astype(jnp.bfloat16).reshape(columns, UNIT, LATENT)
        for chunk in range(CHUNKS):
            piece = latent[:, :, chunk * LANES : (chunk + 1) * LANES]
            if number == 0:
                moved_ref[:, pl.ds(chunk * UNIT, UNIT), :] = piece
            else:
                at = ((number - 1) * CHUNKS + chunk) * UNIT
                held_ref[:, pl.ds(at, UNIT), :] = piece
    blank = jnp.zeros((columns, UNIT, ROPE), jnp.float32)
    at = 3 * CHUNKS * UNIT
    pair = jnp.concatenate([unit_of(rope, 0, 0), unit_of(rope, 0, 1)], axis=2)
    held_ref[:, pl.ds(at, UNIT), :] = pair.astype(jnp.bfloat16)
    single = jnp.concatenate([unit_of(rope, 2, 1), blank], axis=2)
    held_ref[:, pl.ds(at + UNIT, UNIT), :] = single.astype(jnp.bfloat16)
    single = jnp.concatenate([unit_of(rope, 2, 0), blank], axis=2)
    moved_ref[:, pl.ds(CHUNKS * UNIT, UNIT), :] = single.astype(jnp.bfloat16)


def absorb(q_nope, q_rope, w_absorb_k, columns):
    return pl.pallas_call(
        absorb_kernel,
        out_shape=(
            jax.ShapeDtypeStruct((columns, 14 * UNIT, LANES), jnp.bfloat16),
            jax.ShapeDtypeStruct((columns, 5 * UNIT, LANES), jnp.bfloat16),
        ),
        compiler_params=pltpu.CompilerParams(vmem_limit_bytes=32 * 1024 * 1024),
        cost_estimate=pl.CostEstimate(
            flops=1024 * 1024 * 512 * 2, bytes_accessed=3 * 1024 * 1024, transcendentals=0
        ),
        name="absorb",
    )(q_nope, q_rope, w_absorb_k)


def attend_unit(query, keys_ref, count, first_step):
    rows = query.shape[0]
    keys = keys_ref[...]
    capacity = keys.shape[0]
    scores = lax.dot_general(
        query, keys, (((1,), (1,)), ((), ())), preferred_element_type=jnp.float32
    )
    position = lax.broadcasted_iota(jnp.int32, (rows, capacity), 1)
    step = first_step + lax.broadcasted_iota(jnp.int32, (rows, 1), 0) % UNIT // 8
    scores = jnp.where(position < count + step + 1, scores * score_scale, HIDDEN)
    peak = jnp.max(scores, axis=1, keepdims=True)
    spread = jnp.exp(scores - peak)
    total = jnp.sum(spread, axis=1, keepdims=True)
    mixed = jnp.dot(
        spread.astype(jnp.bfloat16), keys[:, :LATENT], preferred_element_type=jnp.float32
    )
    return (mixed / total).astype(jnp.bfloat16)


def place_recent(keys_ref, recent, count):
    capacity = keys_ref.shape[0]
    start = jnp.minimum(count // UNIT * UNIT, capacity - 2 * UNIT)
    start = pl.multiple_of(start, UNIT)
    window = keys_ref[pl.ds(start, 2 * UNIT), :].astype(jnp.float32)
    row = start + lax.broadcasted_iota(jnp.int32, window.shape, 0)
    for step in range(recent.shape[0]):
        window = jnp.where(row == count + step, recent[step : step + 1], window)
    keys_ref[pl.ds(start, 2 * UNIT), :] = window.astype(jnp.bfloat16)


def unit_query(got_ref, at, rope):
    columns = got_ref.shape[0]
    parts = [
        got_ref[:, pl.ds(at + chunk * UNIT, UNIT), :].reshape(columns * UNIT, LANES)
        for chunk in range(CHUNKS)
    ]
    return jnp.concatenate(parts + [rope], axis=1)


def put_unit(out_ref, at, mixed):
    columns = out_ref.shape[0]
    mixed = mixed.reshape(columns, UNIT, LATENT)
    for chunk in range(CHUNKS):
        out_ref[:, pl.ds(at + chunk * UNIT, UNIT), :] = mixed[
            :, :, chunk * LANES : (chunk + 1) * LANES
        ]


def held_kernel(counts_ref, got_ref, cache_ref, recent_ref, out_ref, keys_ref, sems):
    columns = got_ref.shape[0]
    copies = [
        pltpu.make_async_copy(cache_ref.at[place], keys_ref.at[place], sems.at[place])
        for place in range(2)
    ]
    for copy in copies:
        copy.start()
    recent = recent_ref[...].astype(jnp.float32)
    ropes = got_ref[:, pl.ds(3 * CHUNKS * UNIT, UNIT), :].reshape(columns * UNIT, LANES)
    late = got_ref[:, pl.ds(3 * CHUNKS * UNIT + UNIT, UNIT), :].reshape(columns * UNIT, LANES)
    wide = [ropes[:, :ROPE], ropes[:, ROPE:], late[:, :ROPE]]
    for place in range(2):
        copies[place].wait()
        keys = keys_ref.at[place]
        count = counts_ref[place]
        place_recent(keys, recent[:, place], count)
        for unit, first_step in ([(0, 0)], [(1, 0), (2, 2)])[place]:
            at = unit * CHUNKS * UNIT
            mixed = attend_unit(unit_query(got_ref, at, wide[unit]), keys, count, first_step)
            put_unit(out_ref, at, mixed)


def moved_kernel(counts_ref, got_ref, cache_ref, recent_ref, out_ref, keys_ref, sem):
    columns = got_ref.shape[0]
    copy = pltpu.make_async_copy(cache_ref.at[0], keys_ref, sem)
    copy.start()
    recent = recent_ref[...].astype(jnp.float32)
    rope = got_ref[:, pl.ds(CHUNKS * UNIT, UNIT), :].reshape(columns * UNIT, LANES)[:, :ROPE]
    copy.wait()
    count = counts_ref[0]
    place_recent(keys_ref, recent, count)
    put_unit(out_ref, 0, attend_unit(unit_query(got_ref, 0, rope), keys_ref, count, 2))


def attend(kernel, got, cache, recent, counts, units, keys_shape, sem_shape, name):
    columns = got.shape[0]
    vmem = pl.BlockSpec(memory_space=pltpu.VMEM)
    return pl.pallas_call(
        kernel,
        out_shape=jax.ShapeDtypeStruct((columns, units * CHUNKS * UNIT, LANES), jnp.bfloat16),
        in_specs=[
            pl.BlockSpec(memory_space=pltpu.SMEM),
            vmem,
            pl.BlockSpec(memory_space=pl.ANY),
            vmem,
        ],
        out_specs=vmem,
        scratch_shapes=[
            pltpu.VMEM(keys_shape, jnp.bfloat16),
            pltpu.SemaphoreType.DMA(sem_shape),
        ],
        compiler_params=pltpu.CompilerParams(vmem_limit_bytes=32 * 1024 * 1024),
        cost_estimate=pl.CostEstimate(
            flops=units * 256 * 1024 * 1152 * 2,
            bytes_accessed=units * 2 * 1024 * 1024,
            transcendentals=units * 256 * 1024,
        ),
        name=name,
    )(counts, got, cache, recent)


def project_unit(got_ref, at, w_ref):
    columns = got_ref.shape[0]
    heads = w_ref.shape[0]
    parts = [
        got_ref[:, pl.ds(at + chunk * UNIT, UNIT), :].reshape(columns * UNIT, LANES)
        for chunk in range(CHUNKS)
    ]
    latent = jnp.concatenate(parts, axis=1)
    row_head = lax.broadcasted_iota(jnp.int32, (columns * UNIT, HEAD_DIM), 0) % heads
    result = jnp.zeros((columns * UNIT, HEAD_DIM), jnp.float32)
    for head in range(0, heads, 2):
        pair = jnp.concatenate([w_ref[head], w_ref[head + 1]], axis=1)
        product = jnp.dot(latent, pair, preferred_element_type=jnp.float32)
        result = jnp.where(row_head == head, product[:, :HEAD_DIM], result)
        result = jnp.where(row_head == head + 1, product[:, HEAD_DIM:], result)
    result = result.reshape(columns, 2, 8, HEAD_DIM)
    return result[:, 0], result[:, 1]


def project_kernel(held_ref, moved_ref, w_ref, out_ref):
    columns = held_ref.shape[0]
    span = CHUNKS * UNIT
    for first, (near_ref, near_at), (far_ref, far_at) in (
        (0, (held_ref, 0), (held_ref, span)),
        (2, (moved_ref, 0), (held_ref, 2 * span)),
    ):
        near = project_unit(near_ref, near_at, w_ref)
        far = project_unit(far_ref, far_at, w_ref)
        for step in range(2):
            rows = jnp.concatenate([near[step], far[step]], axis=1)
            out_ref[first + step] = rows.astype(jnp.bfloat16).reshape(
                columns * UNIT, HEAD_DIM
            )


def project(held, moved, w_absorb_v):
    columns = held.shape[0]
    return pl.pallas_call(
        project_kernel,
        out_shape=jax.ShapeDtypeStruct((4, columns * UNIT, HEAD_DIM), jnp.bfloat16),
        compiler_params=pltpu.CompilerParams(vmem_limit_bytes=32 * 1024 * 1024),
        cost_estimate=pl.CostEstimate(
            flops=1024 * 1024 * 512 * 2, bytes_accessed=3 * 1024 * 1024, transcendentals=0
        ),
        name="project",
    )(held, moved, w_absorb_v)


def shifted(value, shift, sign):
    count = lax.axis_size("grp")

    def along(steps):
        pairs = [(source, (source + steps) % count) for source in range(count)]
        return lambda given: lax.ppermute(given, "grp", pairs)

    branches = [along(sign * steps) for steps in range(1, count)]
    return lax.switch(shift - 1, branches, value)


def exchanged(value):
    return lax.all_to_all(value, "head", split_axis=0, concat_axis=0, tiled=True)


def body(q_nope, q_rope, w_absorb_k, w_absorb_v, latent_cache, new_latent, lengths, moves):
    steps, slots, heads, _ = q_nope.shape
    holders, capacity, entries = latent_cache.shape
    columns = lax.axis_size("head")
    shift = moves[0, 0]
    first_slot = (lax.axis_index("grp") * columns + lax.axis_index("head")) * holders
    counts = lax.dynamic_slice_in_dim(lengths, first_slot, holders)

    held_out, moved_out = absorb(
        q_nope.reshape(steps, slots * heads, HEAD_DIM),
        q_rope.reshape(steps, slots * heads, ROPE),
        w_absorb_k,
        columns,
    )
    moved_in = exchanged(moved_out)
    held_in = exchanged(held_out)
    fresh = shifted(new_latent[2:, 0], shift, -1)
    moved_in = shifted(moved_in, shift, -1)
    moved_recent = jnp.concatenate([new_latent[:2, 0], fresh], axis=0)
    moved_mixed = attend(
        moved_kernel, moved_in, latent_cache, moved_recent, counts, 1, (capacity, entries), (), "moved"
    )
    held_mixed = attend(
        held_kernel,
        held_in,
        latent_cache,
        new_latent,
        counts,
        3,
        (holders, capacity, entries),
        (2,),
        "held",
    )
    held_back = exchanged(held_mixed)
    moved_back = exchanged(shifted(moved_mixed, shift, 1))
    out = project(held_back, moved_back, w_absorb_v)
    return out.reshape(steps, slots, heads, HEAD_DIM)


def solution(mesh):
    placed = (
        P(None, "grp", "head", None),
        P(None, "grp", "head", None),
        P("head", None, None),
        P("head", None, None),
        P(("grp", "head"), None, None),
        P(None, ("grp", "head"), None),
        P(),
        P("head", None),
    )
    return jax.shard_map(
        body, mesh=mesh, in_specs=placed, out_specs=P(None, "grp", "head", None), check_vma=False
    )
```

time: 338 us -> 145 us (0.43)
  starting transfers between devices: 180 us -> 38.5 us
  waiting for transfers between devices: 84 us -> 32.3 us
  blocking collectives: 0 us -> 50.6 us
  matrix products: 21.2 us -> 0 us
  other arithmetic: 19.8 us -> 0.67 us
  local copies, waits for them, and re-layouts: 26.2 us -> 9.8 us
  Pallas kernels: 0 us -> 11.5 us
    ppermute x30 -> x3, starting transfers between devices: 111 us -> 10.9 us  [along(): return lambda given: lax.ppermute(given, 'grp', pairs)]
    all_to_all x0 -> x2, blocking collectives: none -> 50.6 us  [exchanged(): lax.all_to_all(value, 'head', split_axis=0, concat_axis=0, tiled=True)]
    all_to_all x8 -> x2, starting transfers between devices: 68.7 us -> 27.6 us  [exchanged(): lax.all_to_all(value, 'head', split_axis=0, concat_axis=0, tiled=True)]
    all_to_all x8 -> x2, waiting for transfers between devices: 40.1 us -> 6.09 us  [exchanged(): lax.all_to_all(value, 'head', split_axis=0, concat_axis=0, tiled=True)]
    dot_general x24 -> x0, matrix products: 21.2 us -> none  [the longest x4 7.88 us: score_tile(): jnp.einsum('rhc,rtc->rht', queries, key_rows, preferred_element_type=jnp....]
    ppermute x30 -> x3, waiting for transfers between devices: 43.9 us -> 26.2 us  [along(): return lambda given: lax.ppermute(given, 'grp', pairs)]
    pallas_call x0 -> x4, Pallas kernels: none -> 11.5 us  [the longest x2 6.42 us: attend(): pl.pallas_call(kernel, out_shape=jax.ShapeDtypeStruct((columns, units * C...]
    unnamed x34 -> x17, local copies, waits for them, and re-layouts: 1.14 us -> 9.03 us
  transfers between devices with their start and end apart: 38 -> 5, of which waited for: 20 -> 4; matrix products, arithmetic and copies ran while one was open for 18% -> 3% of each run, Pallas kernels for 0% -> 4%
where the time goes in v1:
time: 145 us; the launch traced here: 144 us
  blocking collectives  50.6 us (35%)
  starting transfers between devices  38.5 us (27%)
  waiting for transfers between devices  32.3 us (22%)
  Pallas kernels  11.5 us (8%)
  local copies, waits for them, and re-layouts  9.8 us (7%)
    all_to_all x2, blocking collectives, exchanged(): lax.all_to_all(value, 'head', split_axis=0, concat_axis=0, tiled=True)  50.6 us
    all_to_all x2, starting transfers between devices, exchanged(): lax.all_to_all(value, 'head', split_axis=0, concat_axis=0, tiled=True)  27.6 us
    ppermute x3, waiting for transfers between devices, along(): return lambda given: lax.ppermute(given, 'grp', pairs)  26.2 us
    ppermute x3, starting transfers between devices, along(): return lambda given: lax.ppermute(given, 'grp', pairs)  10.9 us
    unnamed x17, local copies, waits for them, and re-layouts  9.03 us
    pallas_call x2, Pallas kernels, attend(): pl.pallas_call(kernel, out_shape=jax.ShapeDtypeStruct((columns, units * C...  6.42 us
    all_to_all x2, waiting for transfers between devices, exchanged(): lax.all_to_all(value, 'head', split_axis=0, concat_axis=0, tiled=True)  6.09 us
    pallas_call x1, Pallas kernels, project(): pl.pallas_call(project_kernel, out_shape=jax.ShapeDtypeStruct((4, columns...  2.91 us
  transfers between devices with their start and end apart: 5, of which 4 were waited for; matrix products, arithmetic and copies ran while one was open for 3% of the time, Pallas kernels for 4%

profile of v1, /device:TPU:1, one launch (start us, length us, event | category | flops | bytes accessed | tf_op | source)
XLA Modules:
  0.0 144.2 jit_solution(3315014676241437742)
XLA Ops:
  0.0 1.2 copy-done.3
  1.2 0.9 copy-done.5
  2.2 0.9 copy-done.6
  3.1 2.2 %absorb.1 = (bf16[16,224,128]{2,1,0:T(8,128)(2,1)}, bf16[16,80,128]{2,1,0:T(8,128)(2,1)S(1)}) custom-call(bf16[4,256,128]{2,1,0:T(8,128)(2,1)S(1)} %bitcast.10, bf16[4,256,64]{2,1,0:T(8,128)(2,1)S(1)} %bitcast.11, bf16[8,128,512]{2,1,0:T(8,128)(2,1)S(1)} %copy-done.3), custom_call_target="tpu_custom_call" | custom-call | flops 1073741824 | bytes 3145728 | tf_op jit(solution)/shard_map/absorb/pallas_call | solution.py:71
  5.3 24.8 %all_to_all.113 = bf16[16,80,128]{2,1,0:T(8,128)(2,1)} all-to-all(bf16[16,80,128]{2,1,0:T(8,128)(2,1)S(1)} %get-tuple-element.197), channel_id=1, replica_groups=mesh['grp'=32,'head'=16] {'head'}, dimensions={0} | all-to-all | bytes 655360 | tf_op jit(solution)/shard_map/all_to_all | solution.py:255
  30.1 3.5 %all-to-all-start = ((bf16[16,224,128]{2,1,0:T(8,128)(2,1)}), bf16[16,224,128]{2,1,0:T(8,128)(2,1)S(1)}, u32[]{:S(2)}, u32[]{:S(2)}) async-start(bf16[16,224,128]{2,1,0:T(8,128)(2,1)} %get-tuple-element.196), calls=%async_computation | async-start | bytes 1835008 | tf_op jit(solution)/shard_map/all_to_all | solution.py:255
  33.6 3.1 %copy.9.cache_ref = bf16[2,1024,576]{2,1,0:T(8,128)(2,1)S(1)} copy(bf16[2,1024,576]{1,2,0:T(8,128)(2,1)} %param.105) | data formatting | bytes 4718592 | tf_op args[4]
  38.2 9.4 %conditional.4 = (bf16[2,576]{1,0:T(2,128)(2,1)}) conditional(s32[]{:T(128)} %bitcast.2, bf16[2,576]{1,0:T(2,128)(2,1)S(1)} %bitcast.28, bf16[2,576]{1,0:T(2,128)(2,1)S(1)} %bitcast.43, bf16[2,576]{1,0:T(2,128)(2,1)S(1)} %bitcast.15, bf16[2,576]{1,0:T(2,128)(2,1)S(1)} %bitcast.16, ...), branch_computations={%region_31.0_spmd, %region_32.0_spmd, %region_33.0_spmd, %region_3... | conditional | bytes 9264 | solution.py:251
  38.2 5.7 %collective-permute-start.56 = (bf16[2,576]{1,0:T(2,128)(2,1)S(1)}, bf16[2,576]{1,0:T(2,128)(2,1)}, u32[]{:S(2)}, u32[]{:S(2)}) collective-permute-start(bf16[2,576]{1,0:T(2,128)(2,1)S(1)} %param.56), channel_id=1, source_target_pairs={{0,96},{16,112},{32,128},{48,144},{64,160},{80,176},{96,192},{112,... | collective-permute-start | bytes 6920 | tf_op jit(solution)/shard_map/cond/branch_25_fun/ppermute | solution.py:248
  43.9 3.7 %collective-permute-done.56 = bf16[2,576]{1,0:T(2,128)(2,1)} collective-permute-done((bf16[2,576]{1,0:T(2,128)(2,1)S(1)}, bf16[2,576]{1,0:T(2,128)(2,1)}, u32[]{:S(2)}, u32[]{:S(2)}) %collective-permute-start.56) | collective-permute-done | bytes 2336 | tf_op jit(solution)/shard_map/cond/branch_25_fun/ppermute | solution.py:248
  48.3 18.1 %conditional.3 = (bf16[16,80,128]{2,1,0:T(8,128)(2,1)}) conditional(s32[]{:T(128)} %bitcast.2, bf16[16,80,128]{2,1,0:T(8,128)(2,1)} %all_to_all.113, bf16[16,80,128]{2,1,0:T(8,128)(2,1)} %all_to_all.113, bf16[16,80,128]{2,1,0:T(8,128)(2,1)} %all_to_all.113, bf16[16,80,128]{2,1,0:T(8,128)(2,1)} %all_to_all.113, ...), branch_computations={%region_0.0_spmd, %region_1.0_spmd, %region_2.0_spmd, %region_3.0_... | conditional | bytes 1310768 | solution.py:251
  48.3 3.3 %collective-permute-start.25 = (bf16[16,80,128]{2,1,0:T(8,128)(2,1)}, bf16[16,80,128]{2,1,0:T(8,128)(2,1)}, u32[]{:S(2)}, u32[]{:S(2)}) collective-permute-start(bf16[16,80,128]{2,1,0:T(8,128)(2,1)} %param.25), channel_id=1, source_target_pairs={{0,96},{16,112},{32,128},{48,144},{64,160},{80,176},{96,192},{112,... | collective-permute-start | bytes 983048 | tf_op jit(solution)/shard_map/cond/branch_25_fun/ppermute | solution.py:248
  51.6 14.8 %collective-permute-done.25 = bf16[16,80,128]{2,1,0:T(8,128)(2,1)} collective-permute-done((bf16[16,80,128]{2,1,0:T(8,128)(2,1)}, bf16[16,80,128]{2,1,0:T(8,128)(2,1)}, u32[]{:S(2)}, u32[]{:S(2)}) %collective-permute-start.25) | collective-permute-done | bytes 327712 | tf_op jit(solution)/shard_map/cond/branch_25_fun/ppermute | solution.py:248
  66.4 2.3 %moved.1 = bf16[16,64,128]{2,1,0:T(8,128)(2,1)S(1)} custom-call(s32[2]{0:T(128)S(1)} %dynamic_slice.3.counts_ref, bf16[16,80,128]{2,1,0:T(8,128)(2,1)} %get-tuple-element.200.got_ref, bf16[2,1024,576]{2,1,0:T(8,128)(2,1)S(1)} %copy.9.cache_ref, bf16[4,576]{1,0:T(4,128)(2,1)S(1)} %pad_maximum_fusion.recent_ref), custom_call_target="tpu_custom_call" | custom-call | flops 603979776 | bytes 2097152 | tf_op jit(solution)/shard_map/moved/pallas_call | solution.py:171
  68.7 9.7 %conditional.5 = (bf16[16,64,128]{2,1,0:T(8,128)(2,1)}) conditional(s32[]{:T(128)} %bitcast.2, bf16[16,64,128]{2,1,0:T(8,128)(2,1)S(1)} %moved.1, bf16[16,64,128]{2,1,0:T(8,128)(2,1)S(1)} %moved.1, bf16[16,64,128]{2,1,0:T(8,128)(2,1)S(1)} %moved.1, bf16[16,64,128]{2,1,0:T(8,128)(2,1)S(1)} %moved.1, ...), branch_computations={%region_62.0_spmd, %region_63.0_spmd, %region_64.0_spmd, %region_6... | conditional | bytes 1048624 | solution.py:251
  68.7 1.9 %collective-permute-start.87 = (bf16[16,64,128]{2,1,0:T(8,128)(2,1)S(1)}, bf16[16,64,128]{2,1,0:T(8,128)(2,1)}, u32[]{:S(2)}, u32[]{:S(2)}) collective-permute-start(bf16[16,64,128]{2,1,0:T(8,128)(2,1)S(1)} %param.87), channel_id=1, source_target_pairs={{0,416},{16,432},{32,448},{48,464},{64,480},{80,496},{96,0},{112,1... | collective-permute-start | bytes 786440 | tf_op jit(solution)/shard_map/cond/branch_25_fun/ppermute | solution.py:248
  70.7 7.7 %collective-permute-done.87 = bf16[16,64,128]{2,1,0:T(8,128)(2,1)} collective-permute-done((bf16[16,64,128]{2,1,0:T(8,128)(2,1)S(1)}, bf16[16,64,128]{2,1,0:T(8,128)(2,1)}, u32[]{:S(2)}, u32[]{:S(2)}) %collective-permute-start.87) | collective-permute-done | bytes 262176 | tf_op jit(solution)/shard_map/cond/branch_25_fun/ppermute | solution.py:248
  78.4 24.1 %all-to-all-start.3 = ((bf16[16,64,128]{2,1,0:T(8,128)(2,1)}), bf16[16,64,128]{2,1,0:T(8,128)(2,1)}, u32[]{:S(2)}, u32[]{:S(2)}) async-start(bf16[16,64,128]{2,1,0:T(8,128)(2,1)} %get-tuple-element.202), calls=%async_computation.3 | async-start | bytes 524288 | tf_op jit(solution)/shard_map/all_to_all | solution.py:255
  103.2 4.1 %held.1 = bf16[16,192,128]{2,1,0:T(8,128)(2,1)S(1)} custom-call(s32[2]{0:T(128)S(1)} %dynamic_slice.3.counts_ref, bf16[16,224,128]{2,1,0:T(8,128)(2,1)S(1)} %all-to-all-done.got_ref, bf16[2,1024,576]{2,1,0:T(8,128)(2,1)S(1)} %copy.9.cache_ref, bf16[4,2,576]{2,1,0:T(2,128)(2,1)S(1)} %copy-done.2), custom_call_target="tpu_custom_call" | custom-call | flops 1811939328 | bytes 6291456 | tf_op jit(solution)/shard_map/held/pallas_call | solution.py:171
  107.3 0.9 copy-done
  108.2 6.1 %all-to-all-done.3.moved_ref = bf16[16,64,128]{2,1,0:T(8,128)(2,1)} async-done(((bf16[16,64,128]{2,1,0:T(8,128)(2,1)}), bf16[16,64,128]{2,1,0:T(8,128)(2,1)}, u32[]{:S(2)}, u32[]{:S(2)}) %all-to-all-start.3) | async-done | bytes 262176 | tf_op jit(solution)/shard_map/all_to_all | solution.py:255
  114.3 25.8 %all_to_all.114.held_ref = bf16[16,192,128]{2,1,0:T(8,128)(2,1)S(1)} all-to-all(bf16[16,192,128]{2,1,0:T(8,128)(2,1)} %copy-done), channel_id=1, replica_groups=mesh['grp'=32,'head'=16] {'head'}, dimensions={0} | all-to-all | bytes 1572864 | tf_op jit(solution)/shard_map/all_to_all | solution.py:255
  140.1 1.2 copy-done.4
  141.3 2.9 %project.1 = bf16[4,256,128]{2,1,0:T(8,128)(2,1)} custom-call(bf16[16,192,128]{2,1,0:T(8,128)(2,1)S(1)} %all_to_all.114.held_ref, bf16[16,64,128]{2,1,0:T(8,128)(2,1)} %all-to-all-done.3.moved_ref, bf16[8,512,128]{2,1,0:T(8,128)(2,1)S(1)} %copy-done.4), custom_call_target="tpu_custom_call" | custom-call | flops 1073741824 | bytes 3145728 | tf_op jit(solution)/shard_map/project/pallas_call | solution.py:232
  (15 shorter events, 2.2 us)
Async XLA Ops:
  0.0 1.2 copy-start.3
  1.2 0.9 copy-start.5
  2.2 0.9 copy-start.6
  30.1 48.3 %all-to-all-start = ((bf16[16,224,128]{2,1,0:T(8,128)(2,1)}), bf16[16,224,128]{2,1,0:T(8,128)(2,1)S(1)}, u32[]{:S(2)}, u32[]{:S(2)}) async-start(bf16[16,224,128]{2,1,0:T(8,128)(2,1)} %get-tuple-element.196), calls=%async_computation | async-start | bytes 1835008 | tf_op jit(solution)/shard_map/all_to_all | solution.py:255
  33.6 3.8 %copy-start.1 = (bf16[4,2,576]{2,1,0:T(2,128)(2,1)S(1)}, bf16[4,2,576]{2,1,0:T(2,128)(2,1)}, u32[]{:S(2)}) copy-start(bf16[4,2,576]{2,1,0:T(2,128)(2,1)} %recent_ref.1) | copy-start | bytes 27652
  38.2 9.4 %collective-permute-start.56 = (bf16[2,576]{1,0:T(2,128)(2,1)S(1)}, bf16[2,576]{1,0:T(2,128)(2,1)}, u32[]{:S(2)}, u32[]{:S(2)}) collective-permute-start(bf16[2,576]{1,0:T(2,128)(2,1)S(1)} %param.56), channel_id=1, source_target_pairs={{0,96},{16,112},{32,128},{48,144},{64,160},{80,176},{96,192},{112,... | collective-permute-start | bytes 6920 | tf_op jit(solution)/shard_map/cond/branch_25_fun/ppermute | solution.py:248
  48.3 18.1 %collective-permute-start.25 = (bf16[16,80,128]{2,1,0:T(8,128)(2,1)}, bf16[16,80,128]{2,1,0:T(8,128)(2,1)}, u32[]{:S(2)}, u32[]{:S(2)}) collective-permute-start(bf16[16,80,128]{2,1,0:T(8,128)(2,1)} %param.25), channel_id=1, source_target_pairs={{0,96},{16,112},{32,128},{48,144},{64,160},{80,176},{96,192},{112,... | collective-permute-start | bytes 983048 | tf_op jit(solution)/shard_map/cond/branch_25_fun/ppermute | solution.py:248
  68.7 9.6 %collective-permute-start.87 = (bf16[16,64,128]{2,1,0:T(8,128)(2,1)S(1)}, bf16[16,64,128]{2,1,0:T(8,128)(2,1)}, u32[]{:S(2)}, u32[]{:S(2)}) collective-permute-start(bf16[16,64,128]{2,1,0:T(8,128)(2,1)S(1)} %param.87), channel_id=1, source_target_pairs={{0,416},{16,432},{32,448},{48,464},{64,480},{80,496},{96,0},{112,1... | collective-permute-start | bytes 786440 | tf_op jit(solution)/shard_map/cond/branch_25_fun/ppermute | solution.py:248
  78.4 35.9 %all-to-all-start.3 = ((bf16[16,64,128]{2,1,0:T(8,128)(2,1)}), bf16[16,64,128]{2,1,0:T(8,128)(2,1)}, u32[]{:S(2)}, u32[]{:S(2)}) async-start(bf16[16,64,128]{2,1,0:T(8,128)(2,1)} %get-tuple-element.202), calls=%async_computation.3 | async-start | bytes 524288 | tf_op jit(solution)/shard_map/all_to_all | solution.py:255
  102.5 0.7 copy-start.2
  107.3 0.9 copy-start
  140.1 1.2 copy-start.4

commit v2 on v1

v2 whole, which is shorter than its diff:
```python
import functools
import math

import jax
import jax.numpy as jnp
from jax import lax
from jax.experimental import pallas as pl
from jax.experimental.pallas import tpu as pltpu
from jax.sharding import PartitionSpec as P

HEAD_DIM = 128
ROPE = 64
LATENT = 512
LANES = 128
CHUNKS = LATENT // LANES
UNIT = 16
HIDDEN = -1e30

yarn_gain = (0.1 * math.log(40.0) + 1.0) ** 2
score_scale = yarn_gain / math.sqrt(HEAD_DIM + ROPE)


def split_places(rows, columns):
    wide = rows.astype(jnp.float32).reshape(columns, 2, 8, rows.shape[-1])
    return wide[:, 0], wide[:, 1]


def spread_heads(rows, heads):
    columns = rows.shape[0]
    lane_head = lax.broadcasted_iota(jnp.int32, rows.shape, 1) % heads
    pieces = [
        jnp.where(lane_head == head, rows, 0.0)
        .astype(jnp.bfloat16)
        .reshape(columns * UNIT, HEAD_DIM)
        for head in range(heads)
    ]
    return jnp.concatenate(pieces, axis=1)


def absorb_kernel(steps, units, q_hbm, r_hbm, w_hbm, out_ref, q_ref, r_ref, w_ref, sems):
    columns = out_ref.shape[0]
    heads = w_ref.shape[0]
    first = steps[0]
    copies = [
        pltpu.make_async_copy(q_hbm.at[pl.ds(first, len(steps))], q_ref, sems.at[0]),
        pltpu.make_async_copy(r_hbm.at[pl.ds(first, len(steps))], r_ref, sems.at[1]),
        pltpu.make_async_copy(w_hbm, w_ref, sems.at[2]),
    ]
    for copy in copies:
        copy.start()
    copies[0].wait()
    nope = {step: split_places(q_ref[step - first], columns) for step in steps}
    copies[1].wait()
    rope = {step: split_places(r_ref[step - first], columns) for step in steps}

    def unit_of(parts, begin, place):
        return jnp.concatenate([parts[begin][place], parts[begin + 1][place]], axis=1)

    blank = jnp.zeros((columns, UNIT, ROPE), jnp.float32)
    for number in range(0, len(units), 2):
        pair = [unit_of(rope, *unit) for unit in units[number : number + 2]] + [blank]
        at = (len(units) * CHUNKS + number // 2) * UNIT
        both = jnp.concatenate(pair[:2], axis=2).astype(jnp.bfloat16)
        out_ref[:, pl.ds(at, UNIT), :] = both
    copies[2].wait()
    weights = w_ref[...].reshape(heads * HEAD_DIM, LATENT)
    for number, unit in enumerate(units):
        spread = spread_heads(unit_of(nope, *unit), heads)
        latent = jnp.dot(spread, weights, preferred_element_type=jnp.float32)
        put_unit(out_ref, number * CHUNKS * UNIT, latent.astype(jnp.bfloat16))


def absorb(q_nope, q_rope, w_absorb_k, columns, steps, units, name):
    high = len(units) * CHUNKS + (len(units) + 1) // 2
    hbm = pl.BlockSpec(memory_space=pltpu.HBM)
    slots = q_nope.shape[1]
    return pl.pallas_call(
        functools.partial(absorb_kernel, steps, units),
        out_shape=pltpu.HBM((columns, high * UNIT, LANES), jnp.bfloat16),
        in_specs=[hbm] * 3,
        scratch_shapes=[
            pltpu.VMEM((len(steps), slots, HEAD_DIM), jnp.bfloat16),
            pltpu.VMEM((len(steps), slots, ROPE), jnp.bfloat16),
            pltpu.VMEM(w_absorb_k.shape, jnp.bfloat16),
            pltpu.SemaphoreType.DMA((3,)),
        ],
        compiler_params=pltpu.CompilerParams(vmem_limit_bytes=32 * 1024 * 1024),
        cost_estimate=pl.CostEstimate(
            flops=len(units) * 256 * 1024 * 512 * 2,
            bytes_accessed=3 * 1024 * 1024,
            transcendentals=0,
        ),
        name=name,
    )(*(pltpu.with_memory_space_constraint(x, pltpu.HBM) for x in (q_nope, q_rope, w_absorb_k)))


def attend_unit(query, keys_ref, count, first_step):
    rows = query.shape[0]
    keys = keys_ref[...]
    capacity = keys.shape[1]
    scores = jnp.dot(query, keys, preferred_element_type=jnp.float32)
    position = lax.broadcasted_iota(jnp.int32, (rows, capacity), 1)
    step = first_step + lax.broadcasted_iota(jnp.int32, (rows, 1), 0) % UNIT // 8
    scores = jnp.where(position < count + step + 1, scores * score_scale, HIDDEN)
    peak = jnp.max(scores, axis=1, keepdims=True)
    spread = jnp.exp(scores - peak)
    total = jnp.sum(spread, axis=1, keepdims=True)
    weights = (spread * (1.0 / total)).astype(jnp.bfloat16)
    mixed = lax.dot_general(
        weights, keys[:LATENT], (((1,), (1,)), ((), ())), preferred_element_type=jnp.float32
    )
    return mixed.astype(jnp.bfloat16)


def place_recent(keys_ref, recent, count):
    capacity = keys_ref.shape[1]
    start = jnp.minimum(count // LANES * LANES, capacity - 2 * LANES)
    start = pl.multiple_of(start, LANES)
    steps = recent.shape[0]
    lane = start + lax.broadcasted_iota(jnp.int32, (steps, 2 * LANES), 1)
    row = lax.broadcasted_iota(jnp.int32, (steps, 2 * LANES), 0)
    chosen = jnp.where(lane == count + row, 1.0, 0.0).astype(jnp.bfloat16)
    fresh = lax.dot_general(
        recent, chosen, (((0,), (0,)), ((), ())), preferred_element_type=jnp.float32
    )
    window = keys_ref[:, pl.ds(start, 2 * LANES)].astype(jnp.float32)
    lane = start + lax.broadcasted_iota(jnp.int32, window.shape, 1)
    window = jnp.where((lane >= count) & (lane < count + steps), fresh, window)
    keys_ref[:, pl.ds(start, 2 * LANES)] = window.astype(jnp.bfloat16)


def unit_rows(got_ref, at):
    columns = got_ref.shape[0]
    return got_ref[:, pl.ds(at, UNIT), :].reshape(columns * UNIT, LANES)


def unit_latent(got_ref, at):
    return [unit_rows(got_ref, at + chunk * UNIT) for chunk in range(CHUNKS)]


def put_unit(out_ref, at, mixed):
    columns = out_ref.shape[0]
    mixed = mixed.reshape(columns, UNIT, LATENT)
    for chunk in range(CHUNKS):
        out_ref[:, pl.ds(at + chunk * UNIT, UNIT), :] = mixed[
            :, :, chunk * LANES : (chunk + 1) * LANES
        ]


def attend_kernel(plan, counts_ref, got_ref, cache_ref, recent_ref, out_ref, keys_ref, sems):
    units = sum(len(group) for group in plan)
    copies = [
        pltpu.make_async_copy(cache_ref.at[place], keys_ref.at[place], sems.at[place])
        for place in range(len(plan))
    ]
    for copy in copies:
        copy.start()
    for place, group in enumerate(plan):
        copies[place].wait()
        count = counts_ref[place]
        keys = keys_ref.at[place]
        place_recent(keys, recent_ref[place], count)
        for unit, first_step in group:
            at = unit * CHUNKS * UNIT
            rope = unit_rows(got_ref, (units * CHUNKS + unit // 2) * UNIT)
            rope = rope[:, unit % 2 * ROPE : unit % 2 * ROPE + ROPE]
            query = jnp.concatenate(unit_latent(got_ref, at) + [rope], axis=1)
            put_unit(out_ref, at, attend_unit(query, keys, count, first_step))


def attend(got, cache, recent, counts, plan, name):
    columns = got.shape[0]
    units = sum(len(group) for group in plan)
    places = len(plan)
    vmem = pl.BlockSpec(memory_space=pltpu.VMEM)
    return pl.pallas_call(
        functools.partial(attend_kernel, plan),
        out_shape=pltpu.HBM((columns, units * CHUNKS * UNIT, LANES), jnp.bfloat16),
        in_specs=[
            pl.BlockSpec(memory_space=pltpu.SMEM),
            vmem,
            pl.BlockSpec(memory_space=pltpu.HBM),
            vmem,
        ],
        out_specs=vmem,
        scratch_shapes=[
            pltpu.VMEM((places,) + cache.shape[1:], jnp.bfloat16),
            pltpu.SemaphoreType.DMA((places,)),
        ],
        compiler_params=pltpu.CompilerParams(vmem_limit_bytes=32 * 1024 * 1024),
        cost_estimate=pl.CostEstimate(
            flops=units * 256 * 1024 * 1152 * 2,
            bytes_accessed=units * 2 * 1024 * 1024,
            transcendentals=units * 256 * 1024,
        ),
        name=name,
    )(counts, got, cache, recent)


def project_unit(got_ref, at, w_ref):
    columns = got_ref.shape[0]
    heads = w_ref.shape[0]
    latent = jnp.concatenate(unit_latent(got_ref, at), axis=1)
    row_head = lax.broadcasted_iota(jnp.int32, (columns * UNIT, HEAD_DIM), 0) % heads
    result = jnp.zeros((columns * UNIT, HEAD_DIM), jnp.float32)
    for head in range(0, heads, 2):
        pair = jnp.concatenate([w_ref[head], w_ref[head + 1]], axis=1)
        product = jnp.dot(latent, pair, preferred_element_type=jnp.float32)
        result = jnp.where(row_head == head, product[:, :HEAD_DIM], result)
        result = jnp.where(row_head == head + 1, product[:, HEAD_DIM:], result)
    result = result.reshape(columns, 2, 8, HEAD_DIM)
    return result[:, 0], result[:, 1]


def join_places(near, far):
    rows = jnp.concatenate([near, far], axis=1).astype(jnp.bfloat16)
    return rows.reshape(rows.shape[0] * UNIT, HEAD_DIM)


def project_held_kernel(got_ref, w_ref, out_ref):
    span = CHUNKS * UNIT
    near = project_unit(got_ref, 0, w_ref)
    far = project_unit(got_ref, span, w_ref)
    late = project_unit(got_ref, 2 * span, w_ref)
    for step in range(2):
        out_ref[step] = join_places(near[step], far[step])
        out_ref[2 + step] = join_places(jnp.zeros_like(late[step]), late[step])


def project_moved_kernel(got_ref, w_ref, part_ref, out_ref):
    columns = got_ref.shape[0]
    near = project_unit(got_ref, 0, w_ref)
    for step in range(2):
        far = split_places(part_ref[2 + step], columns)[1]
        out_ref[step] = part_ref[step]
        out_ref[2 + step] = join_places(near[step], far)


def project(kernel, operands, units, name):
    columns = operands[0].shape[0]
    return pl.pallas_call(
        kernel,
        out_shape=jax.ShapeDtypeStruct((4, columns * UNIT, HEAD_DIM), jnp.bfloat16),
        compiler_params=pltpu.CompilerParams(vmem_limit_bytes=16 * 1024 * 1024),
        cost_estimate=pl.CostEstimate(
            flops=units * 256 * 1024 * 512 * 2, bytes_accessed=2 * 1024 * 1024, transcendentals=0
        ),
        name=name,
    )(*operands)


def shifted(value, shift, sign):
    count = lax.axis_size("grp")

    def along(steps):
        pairs = [(source, (source + steps) % count) for source in range(count)]
        return lambda given: lax.ppermute(given, "grp", pairs)

    branches = [along(sign * steps) for steps in range(1, count)]
    return lax.switch(shift - 1, branches, value)


def exchanged(value):
    return lax.all_to_all(value, "head", split_axis=0, concat_axis=0, tiled=True)


def body(q_nope, q_rope, w_absorb_k, w_absorb_v, latent_cache, new_latent, lengths, moves):
    steps, slots, heads, _ = q_nope.shape
    holders, capacity, entries = latent_cache.shape
    columns = lax.axis_size("head")
    shift = moves[0, 0]
    first_slot = (lax.axis_index("grp") * columns + lax.axis_index("head")) * holders
    counts = lax.dynamic_slice_in_dim(lengths, first_slot, holders)

    q_nope = q_nope.reshape(steps, slots * heads, HEAD_DIM)
    q_rope = q_rope.reshape(steps, slots * heads, ROPE)
    cache = jnp.swapaxes(latent_cache, 1, 2)
    recent = jnp.swapaxes(new_latent, 0, 1)

    moved_out = absorb(q_nope, q_rope, w_absorb_k, columns, (2, 3), [(2, 0)], "absorb_moved")
    held_out = absorb(
        q_nope, q_rope, w_absorb_k, columns, (0, 1, 2, 3), [(0, 0), (0, 1), (2, 1)], "absorb_held"
    )
    moved_in = exchanged(moved_out)
    fresh = shifted(new_latent[2:, 0], shift, -1)
    held_out, fresh = lax.optimization_barrier((held_out, fresh))
    held_in = exchanged(held_out)
    moved_recent = jnp.concatenate([recent[:1, :2], fresh[None]], axis=1)
    moved_in = shifted(moved_in, shift, -1)
    moved_mixed = attend(moved_in, cache, moved_recent, counts, [[(0, 2)]], "attend_moved")
    held_mixed = attend(
        held_in, cache, recent, counts, [[(0, 0)], [(1, 0), (2, 2)]], "attend_held"
    )
    held_mixed, moved_mixed = lax.optimization_barrier((held_mixed, moved_mixed))
    held_back = exchanged(held_mixed)
    moved_back = shifted(moved_mixed, shift, 1)
    moved_back = exchanged(moved_back)
    part = project(project_held_kernel, (held_back, w_absorb_v), 3, "project_held")
    out = project(project_moved_kernel, (moved_back, w_absorb_v, part), 1, "project_moved")
    return out.reshape(steps, slots, heads, HEAD_DIM)


def solution(mesh):
    placed = (
        P(None, "grp", "head", None),
        P(None, "grp", "head", None),
        P("head", None, None),
        P("head", None, None),
        P(("grp", "head"), None, None),
        P(None, ("grp", "head"), None),
        P(),
        P("head", None),
    )
    return jax.shard_map(
        body, mesh=mesh, in_specs=placed, out_specs=P(None, "grp", "head", None), check_vma=False
    )
```

time: 145 us -> 122 us (0.84)
  blocking collectives: 50.6 us -> 0 us
  starting transfers between devices: 38.5 us -> 58.1 us
  waiting for transfers between devices: 32.3 us -> 42.1 us
  local copies, waits for them, and re-layouts: 9.8 us -> 0.8 us
  Pallas kernels: 11.5 us -> 18.4 us
    all_to_all x2 -> x0, blocking collectives: 50.6 us -> none  [exchanged(): lax.all_to_all(value, 'head', split_axis=0, concat_axis=0, tiled=True)]
    ppermute x3, starting transfers between devices: 10.9 us -> 22 us  [along(): return lambda given: lax.ppermute(given, 'grp', pairs)]
    all_to_all x2 -> x4, waiting for transfers between devices: 6.09 us -> 16.1 us  [exchanged(): lax.all_to_all(value, 'head', split_axis=0, concat_axis=0, tiled=True)]
    unnamed x17 -> x7, local copies, waits for them, and re-layouts: 9.03 us -> 0.02 us
    all_to_all x2 -> x4, starting transfers between devices: 27.6 us -> 36.1 us  [exchanged(): lax.all_to_all(value, 'head', split_axis=0, concat_axis=0, tiled=True)]
    pallas_call x4 -> x6, Pallas kernels: 11.5 us -> 18.4 us  [the longest x2 10.2 us: attend(): pl.pallas_call(functools.partial(attend_kernel, plan), out_shape=pltpu.HB...]
  transfers between devices with their start and end apart: 5 -> 7, of which waited for: 4 -> 6; matrix products, arithmetic and copies ran while one was open for 3% -> 1% of each run, Pallas kernels for 4% -> 7%
where the time goes in v2:
time: 122 us; the launch traced here: 121 us
  starting transfers between devices  58.1 us (48%)
  waiting for transfers between devices  42.1 us (35%)
  Pallas kernels  18.4 us (15%)
    all_to_all x4, starting transfers between devices, exchanged(): lax.all_to_all(value, 'head', split_axis=0, concat_axis=0, tiled=True)  36.1 us
    ppermute x3, waiting for transfers between devices, along(): return lambda given: lax.ppermute(given, 'grp', pairs)  26 us
    ppermute x3, starting transfers between devices, along(): return lambda given: lax.ppermute(given, 'grp', pairs)  22 us
    all_to_all x4, waiting for transfers between devices, exchanged(): lax.all_to_all(value, 'head', split_axis=0, concat_axis=0, tiled=True)  16.1 us
    pallas_call x2, Pallas kernels, attend(): pl.pallas_call(functools.partial(attend_kernel, plan), out_shape=pltpu.HB...  10.2 us
    pallas_call x2, Pallas kernels, absorb(): pl.pallas_call(functools.partial(absorb_kernel, steps, units), out_shape=...  6.06 us
  transfers between devices with their start and end apart: 7, of which 6 were waited for; matrix products, arithmetic and copies ran while one was open for 1% of the time, Pallas kernels for 7%

profile of v2, /device:TPU:1, one launch (start us, length us, event | category | flops | bytes accessed | tf_op | source)
XLA Modules:
  0.0 120.9 jit_solution(10896285694029208280)
XLA Ops:
  0.0 2.6 %absorb_moved.1 = bf16[16,80,128]{2,1,0:T(8,128)(2,1)} custom-call(bf16[4,256,128]{2,1,0:T(8,128)(2,1)} %bitcast.15, bf16[4,256,64]{2,1,0:T(8,128)(2,1)} %bitcast.17, bf16[8,128,512]{2,1,0:T(8,128)(2,1)} %w_hbm.3), custom_call_target="tpu_custom_call" | custom-call | flops 268435456 | bytes 3145728 | tf_op jit(solution)/shard_map/absorb_moved/pallas_call | solution.py:77
  2.6 11.8 %all-to-all-start.1 = ((bf16[16,80,128]{2,1,0:T(8,128)(2,1)}), bf16[16,80,128]{2,1,0:T(8,128)(2,1)S(1)}, u32[]{:S(2)}, u32[]{:S(2)}) async-start(bf16[16,80,128]{2,1,0:T(8,128)(2,1)} %absorb_moved.1), calls=%async_computation.1 | async-start | bytes 655360 | tf_op jit(solution)/shard_map/all_to_all | solution.py:264
  15.1 10.4 %conditional.3 = (bf16[2,576]{1,0:T(2,128)(2,1)}) conditional(s32[]{:T(128)} %bitcast, bf16[2,576]{1,0:T(2,128)(2,1)S(1)} %slice_bitcast_fusion, bf16[2,576]{1,0:T(2,128)(2,1)S(1)} %slice_bitcast_fusion, bf16[2,576]{1,0:T(2,128)(2,1)S(1)} %slice_bitcast_fusion, bf16[2,576]{1,0:T(2,128)(2,1)S(1)} %slice_bitcast_fusion, ...), branch_computations={%region_0.0_spmd, %region_1.0_spmd, %region_2.0_spmd, %region_3.0_... | conditional | bytes 9264 | solution.py:260
  15.2 9.6 %collective-permute-start.12 = (bf16[2,576]{1,0:T(2,128)(2,1)S(1)}, bf16[2,576]{1,0:T(2,128)(2,1)}, u32[]{:S(2)}, u32[]{:S(2)}) collective-permute-start(bf16[2,576]{1,0:T(2,128)(2,1)S(1)} %param.12), channel_id=1, source_target_pairs={{0,304},{16,320},{32,336},{48,352},{64,368},{80,384},{96,400},{112... | collective-permute-start | bytes 6920 | tf_op jit(solution)/shard_map/cond/branch_12_fun/ppermute | solution.py:257
  24.8 0.7 collective-permute-done.12
  25.5 3.5 %absorb_held.1 = bf16[16,224,128]{2,1,0:T(8,128)(2,1)} custom-call(bf16[4,256,128]{2,1,0:T(8,128)(2,1)} %bitcast.16, bf16[4,256,64]{2,1,0:T(8,128)(2,1)} %bitcast.18, bf16[8,128,512]{2,1,0:T(8,128)(2,1)} %w_hbm.3), custom_call_target="tpu_custom_call" | custom-call | flops 805306368 | bytes 3145728 | tf_op jit(solution)/shard_map/absorb_held/pallas_call | solution.py:77
  29.0 5.6 %all-to-all-start = ((bf16[16,224,128]{2,1,0:T(8,128)(2,1)}), bf16[16,224,128]{2,1,0:T(8,128)(2,1)}, u32[]{:S(2)}, u32[]{:S(2)}) async-start(bf16[16,224,128]{2,1,0:T(8,128)(2,1)} %absorb_held.1), calls=%async_computation | async-start | bytes 1835008 | tf_op jit(solution)/shard_map/all_to_all | solution.py:264
  34.6 0.8 dynamic_slice.3.counts_ref
  35.4 0.7 pad_maximum_fusion.recent_ref
  36.1 17.6 %conditional.4 = (bf16[16,80,128]{2,1,0:T(8,128)(2,1)}) conditional(s32[]{:T(128)} %bitcast, bf16[16,80,128]{2,1,0:T(8,128)(2,1)S(1)} %all-to-all-done.1, bf16[16,80,128]{2,1,0:T(8,128)(2,1)S(1)} %all-to-all-done.1, bf16[16,80,128]{2,1,0:T(8,128)(2,1)S(1)} %all-to-all-done.1, ...), branch_computations={%region_31.0_spmd, %region_32.0_spmd, %region_33.0_spmd, %region_3... | conditional | bytes 1310768 | solution.py:260
  36.1 8.4 %collective-permute-start.43 = (bf16[16,80,128]{2,1,0:T(8,128)(2,1)S(1)}, bf16[16,80,128]{2,1,0:T(8,128)(2,1)}, u32[]{:S(2)}, u32[]{:S(2)}) collective-permute-start(bf16[16,80,128]{2,1,0:T(8,128)(2,1)S(1)} %param.43), channel_id=1, source_target_pairs={{0,304},{16,320},{32,336},{48,352},{64,368},{80,384},{96,400},{112... | collective-permute-start | bytes 983048 | tf_op jit(solution)/shard_map/cond/branch_12_fun/ppermute | solution.py:257
  44.5 9.2 %collective-permute-done.43 = bf16[16,80,128]{2,1,0:T(8,128)(2,1)} collective-permute-done((bf16[16,80,128]{2,1,0:T(8,128)(2,1)S(1)}, bf16[16,80,128]{2,1,0:T(8,128)(2,1)}, u32[]{:S(2)}, u32[]{:S(2)}) %collective-permute-start.43) | collective-permute-done | bytes 327712 | tf_op jit(solution)/shard_map/cond/branch_12_fun/ppermute | solution.py:257
  53.7 3.5 %attend_moved.1 = bf16[16,64,128]{2,1,0:T(8,128)(2,1)} custom-call(s32[2]{0:T(128)S(1)} %dynamic_slice.3.counts_ref, bf16[16,80,128]{2,1,0:T(8,128)(2,1)} %get-tuple-element.205.got_ref, bf16[2,576,1024]{2,1,0:T(8,128)(2,1)S(1)} %bitcast.11, bf16[1,4,576]{2,1,0:T(4,128)(2,1)S(1)} %pad_maximum_fusion.recent_ref), custom_call_target="tpu_custom_call" | custom-call | flops 603979776 | bytes 2097152 | tf_op jit(solution)/shard_map/attend_moved/pallas_call | solution.py:176
  57.2 2.8 %all-to-all-done.got_ref = bf16[16,224,128]{2,1,0:T(8,128)(2,1)} async-done(((bf16[16,224,128]{2,1,0:T(8,128)(2,1)}), bf16[16,224,128]{2,1,0:T(8,128)(2,1)}, u32[]{:S(2)}, u32[]{:S(2)}) %all-to-all-start) | async-done | bytes 917536 | tf_op jit(solution)/shard_map/all_to_all | solution.py:264
  60.0 6.7 %attend_held.1 = bf16[16,192,128]{2,1,0:T(8,128)(2,1)} custom-call(s32[2]{0:T(128)S(1)} %dynamic_slice.3.counts_ref, bf16[16,224,128]{2,1,0:T(8,128)(2,1)} %all-to-all-done.got_ref, bf16[2,576,1024]{2,1,0:T(8,128)(2,1)S(1)} %bitcast.12, bf16[2,4,576]{2,1,0:T(4,128)(2,1)S(1)} %bitcast.14), custom_call_target="tpu_custom_call" | custom-call | flops 1811939328 | bytes 6291456 | tf_op jit(solution)/shard_map/attend_held/pallas_call | solution.py:176
  66.7 12.9 %all-to-all-start.3 = ((bf16[16,192,128]{2,1,0:T(8,128)(2,1)}), bf16[16,192,128]{2,1,0:T(8,128)(2,1)S(1)}, u32[]{:S(2)}, u32[]{:S(2)}) async-start(bf16[16,192,128]{2,1,0:T(8,128)(2,1)} %attend_held.1), calls=%async_computation.3 | async-start | bytes 1572864 | tf_op jit(solution)/shard_map/all_to_all | solution.py:264
  79.6 20.1 %conditional.5 = (bf16[16,64,128]{2,1,0:T(8,128)(2,1)}) conditional(s32[]{:T(128)} %bitcast, bf16[16,64,128]{2,1,0:T(8,128)(2,1)} %attend_moved.1, bf16[16,64,128]{2,1,0:T(8,128)(2,1)} %attend_moved.1, bf16[16,64,128]{2,1,0:T(8,128)(2,1)} %attend_moved.1, bf16[16,64,128]{2,1,0:T(8,128)(2,1)} %attend_moved.1, ...), branch_computations={%region_62.0_spmd, %region_63.0_spmd, %region_64.0_spmd, %region_6... | conditional | bytes 1048624 | solution.py:260
  79.6 4.0 %collective-permute-start.74 = (bf16[16,64,128]{2,1,0:T(8,128)(2,1)}, bf16[16,64,128]{2,1,0:T(8,128)(2,1)}, u32[]{:S(2)}, u32[]{:S(2)}) collective-permute-start(bf16[16,64,128]{2,1,0:T(8,128)(2,1)} %param.74), channel_id=1, source_target_pairs={{0,208},{16,224},{32,240},{48,256},{64,272},{80,288},{96,304},{112... | collective-permute-start | bytes 786440 | tf_op jit(solution)/shard_map/cond/branch_12_fun/ppermute | solution.py:257
  83.6 16.1 %collective-permute-done.74 = bf16[16,64,128]{2,1,0:T(8,128)(2,1)} collective-permute-done((bf16[16,64,128]{2,1,0:T(8,128)(2,1)}, bf16[16,64,128]{2,1,0:T(8,128)(2,1)}, u32[]{:S(2)}, u32[]{:S(2)}) %collective-permute-start.74) | collective-permute-done | bytes 262176 | tf_op jit(solution)/shard_map/cond/branch_12_fun/ppermute | solution.py:257
  99.7 2.6 %all-to-all-done.3.got_ref = bf16[16,192,128]{2,1,0:T(8,128)(2,1)S(1)} async-done(((bf16[16,192,128]{2,1,0:T(8,128)(2,1)}), bf16[16,192,128]{2,1,0:T(8,128)(2,1)S(1)}, u32[]{:S(2)}, u32[]{:S(2)}) %all-to-all-start.3) | async-done | bytes 786464 | tf_op jit(solution)/shard_map/all_to_all | solution.py:264
  102.3 5.8 %all-to-all-start.2 = ((bf16[16,64,128]{2,1,0:T(8,128)(2,1)}), bf16[16,64,128]{2,1,0:T(8,128)(2,1)S(1)}, u32[]{:S(2)}, u32[]{:S(2)}) async-start(bf16[16,64,128]{2,1,0:T(8,128)(2,1)} %get-tuple-element.206), calls=%async_computation.2 | async-start | bytes 524288 | tf_op jit(solution)/shard_map/all_to_all | solution.py:264
  108.1 1.0 project_held.1.part_ref
  109.1 10.7 %all-to-all-done.2.got_ref = bf16[16,64,128]{2,1,0:T(8,128)(2,1)S(1)} async-done(((bf16[16,64,128]{2,1,0:T(8,128)(2,1)}), bf16[16,64,128]{2,1,0:T(8,128)(2,1)S(1)}, u32[]{:S(2)}, u32[]{:S(2)}) %all-to-all-start.2) | async-done | bytes 262176 | tf_op jit(solution)/shard_map/all_to_all | solution.py:264
  119.8 1.2 project_moved.1
  (10 shorter events, 0.0 us)
Async XLA Ops:
  0.0 15.1 %copy-start.2 = (bf16[4,2,576]{2,1,0:T(2,128)(2,1)S(1)}, bf16[4,2,576]{2,1,0:T(2,128)(2,1)}, u32[]{:S(2)}) copy-start(bf16[4,2,576]{2,1,0:T(2,128)(2,1)} %param.106) | copy-start | bytes 27652
  2.6 26.4 %all-to-all-start.1 = ((bf16[16,80,128]{2,1,0:T(8,128)(2,1)}), bf16[16,80,128]{2,1,0:T(8,128)(2,1)S(1)}, u32[]{:S(2)}, u32[]{:S(2)}) async-start(bf16[16,80,128]{2,1,0:T(8,128)(2,1)} %absorb_moved.1), calls=%async_computation.1 | async-start | bytes 655360 | tf_op jit(solution)/shard_map/all_to_all | solution.py:264
  15.2 10.4 %collective-permute-start.12 = (bf16[2,576]{1,0:T(2,128)(2,1)S(1)}, bf16[2,576]{1,0:T(2,128)(2,1)}, u32[]{:S(2)}, u32[]{:S(2)}) collective-permute-start(bf16[2,576]{1,0:T(2,128)(2,1)S(1)} %param.12), channel_id=1, source_target_pairs={{0,304},{16,320},{32,336},{48,352},{64,368},{80,384},{96,400},{112... | collective-permute-start | bytes 6920 | tf_op jit(solution)/shard_map/cond/branch_12_fun/ppermute | solution.py:257
  25.5 28.2 %copy-start = (bf16[2,1024,576]{1,2,0:T(8,128)(2,1)S(1)}, bf16[2,1024,576]{1,2,0:T(8,128)(2,1)}, u32[]{:S(2)}) copy-start(bf16[2,1024,576]{1,2,0:T(8,128)(2,1)} %param.105) | copy-start | bytes 7077892
  29.0 31.0 %all-to-all-start = ((bf16[16,224,128]{2,1,0:T(8,128)(2,1)}), bf16[16,224,128]{2,1,0:T(8,128)(2,1)}, u32[]{:S(2)}, u32[]{:S(2)}) async-start(bf16[16,224,128]{2,1,0:T(8,128)(2,1)} %absorb_held.1), calls=%async_computation | async-start | bytes 1835008 | tf_op jit(solution)/shard_map/all_to_all | solution.py:264
  36.1 17.6 %collective-permute-start.43 = (bf16[16,80,128]{2,1,0:T(8,128)(2,1)S(1)}, bf16[16,80,128]{2,1,0:T(8,128)(2,1)}, u32[]{:S(2)}, u32[]{:S(2)}) collective-permute-start(bf16[16,80,128]{2,1,0:T(8,128)(2,1)S(1)} %param.43), channel_id=1, source_target_pairs={{0,304},{16,320},{32,336},{48,352},{64,368},{80,384},{96,400},{112... | collective-permute-start | bytes 983048 | tf_op jit(solution)/shard_map/cond/branch_12_fun/ppermute | solution.py:257
  57.2 50.9 %copy-start.1 = (bf16[8,512,128]{2,1,0:T(8,128)(2,1)S(1)}, bf16[8,512,128]{2,1,0:T(8,128)(2,1)}, u32[]{:S(2)}) copy-start(bf16[8,512,128]{2,1,0:T(8,128)(2,1)} %w_ref.3) | copy-start | bytes 3145732
  66.7 35.6 %all-to-all-start.3 = ((bf16[16,192,128]{2,1,0:T(8,128)(2,1)}), bf16[16,192,128]{2,1,0:T(8,128)(2,1)S(1)}, u32[]{:S(2)}, u32[]{:S(2)}) async-start(bf16[16,192,128]{2,1,0:T(8,128)(2,1)} %attend_held.1), calls=%async_computation.3 | async-start | bytes 1572864 | tf_op jit(solution)/shard_map/all_to_all | solution.py:264
  79.6 20.1 %collective-permute-start.74 = (bf16[16,64,128]{2,1,0:T(8,128)(2,1)}, bf16[16,64,128]{2,1,0:T(8,128)(2,1)}, u32[]{:S(2)}, u32[]{:S(2)}) collective-permute-start(bf16[16,64,128]{2,1,0:T(8,128)(2,1)} %param.74), channel_id=1, source_target_pairs={{0,208},{16,224},{32,240},{48,256},{64,272},{80,288},{96,304},{112... | collective-permute-start | bytes 786440 | tf_op jit(solution)/shard_map/cond/branch_12_fun/ppermute | solution.py:257
  102.3 17.5 %all-to-all-start.2 = ((bf16[16,64,128]{2,1,0:T(8,128)(2,1)}), bf16[16,64,128]{2,1,0:T(8,128)(2,1)S(1)}, u32[]{:S(2)}, u32[]{:S(2)}) async-start(bf16[16,64,128]{2,1,0:T(8,128)(2,1)} %get-tuple-element.206), calls=%async_computation.2 | async-start | bytes 524288 | tf_op jit(solution)/shard_map/all_to_all | solution.py:264

commit v3 on v2

--- a/solution.py
+++ b/solution.py
@@ -14,7 +14,9 @@
 LANES = 128
 CHUNKS = LATENT // LANES
 UNIT = 16
+MOVED_ROWS = CHUNKS * UNIT + UNIT // 2
 HIDDEN = -1e30
+LOG2_E = 1.4426950408889634
 
 yarn_gain = (0.1 * math.log(40.0) + 1.0) ** 2
 score_scale = yarn_gain / math.sqrt(HEAD_DIM + ROPE)
@@ -57,7 +59,11 @@
         return jnp.concatenate([parts[begin][place], parts[begin + 1][place]], axis=1)
 
     blank = jnp.zeros((columns, UNIT, ROPE), jnp.float32)
-    for number in range(0, len(units), 2):
+    if len(units) == 1:
+        begin, place = units[0]
+        both = jnp.concatenate([rope[begin][place], rope[begin + 1][place]], axis=2)
+        out_ref[:, pl.ds(CHUNKS * UNIT, UNIT // 2), :] = both.astype(jnp.bfloat16)
+    for number in range(0, len(units) if len(units) > 1 else 0, 2):
         pair = [unit_of(rope, *unit) for unit in units[number : number + 2]] + [blank]
         at = (len(units) * CHUNKS + number // 2) * UNIT
         both = jnp.concatenate(pair[:2], axis=2).astype(jnp.bfloat16)
@@ -71,12 +77,12 @@
 
 
 def absorb(q_nope, q_rope, w_absorb_k, columns, steps, units, name):
-    high = len(units) * CHUNKS + (len(units) + 1) // 2
+    high = MOVED_ROWS if len(units) == 1 else (len(units) * CHUNKS + (len(units) + 1) // 2) * UNIT
     hbm = pl.BlockSpec(memory_space=pltpu.HBM)
     slots = q_nope.shape[1]
     return pl.pallas_call(
         functools.partial(absorb_kernel, steps, units),
-        out_shape=pltpu.HBM((columns, high * UNIT, LANES), jnp.bfloat16),
+        out_shape=pltpu.HBM((columns, high, LANES), jnp.bfloat16),
         in_specs=[hbm] * 3,
         scratch_shapes=[
             pltpu.VMEM((len(steps), slots, HEAD_DIM), jnp.bfloat16),
@@ -91,42 +97,33 @@
             transcendentals=0,
         ),
         name=name,
-    )(*(pltpu.with_memory_space_constraint(x, pltpu.HBM) for x in (q_nope, q_rope, w_absorb_k)))
-
-
-def attend_unit(query, keys_ref, count, first_step):
-    rows = query.shape[0]
-    keys = keys_ref[...]
-    capacity = keys.shape[1]
-    scores = jnp.dot(query, keys, preferred_element_type=jnp.float32)
-    position = lax.broadcasted_iota(jnp.int32, (rows, capacity), 1)
-    step = first_step + lax.broadcasted_iota(jnp.int32, (rows, 1), 0) % UNIT // 8
-    scores = jnp.where(position < count + step + 1, scores * score_scale, HIDDEN)
+    )(in_hbm(q_nope), in_hbm(q_rope), in_hbm(w_absorb_k))
+
+
+def attend_unit(query, keys, live):
+    scores = lax.dot_general(
+        query, keys, (((1,), (1,)), ((), ())), preferred_element_type=jnp.float32
+    )
+    position = lax.broadcasted_iota(jnp.int32, scores.shape, 1)
+    scores = jnp.where(position < live, scores, HIDDEN)
     peak = jnp.max(scores, axis=1, keepdims=True)
-    spread = jnp.exp(scores - peak)
+    spread = jnp.exp2((scores - peak) * (score_scale * LOG2_E))
     total = jnp.sum(spread, axis=1, keepdims=True)
-    weights = (spread * (1.0 / total)).astype(jnp.bfloat16)
-    mixed = lax.dot_general(
-        weights, keys[:LATENT], (((1,), (1,)), ((), ())), preferred_element_type=jnp.float32
-    )
-    return mixed.astype(jnp.bfloat16)
+    mixed = jnp.dot(
+        spread.astype(jnp.bfloat16), keys[:, :LATENT], preferred_element_type=jnp.float32
+    )
+    return (mixed * (1.0 / total)).astype(jnp.bfloat16)
 
 
 def place_recent(keys_ref, recent, count):
-    capacity = keys_ref.shape[1]
-    start = jnp.minimum(count // LANES * LANES, capacity - 2 * LANES)
-    start = pl.multiple_of(start, LANES)
-    steps = recent.shape[0]
-    lane = start + lax.broadcasted_iota(jnp.int32, (steps, 2 * LANES), 1)
-    row = lax.broadcasted_iota(jnp.int32, (steps, 2 * LANES), 0)
-    chosen = jnp.where(lane == count + row, 1.0, 0.0).astype(jnp.bfloat16)
-    fresh = lax.dot_general(
-        recent, chosen, (((0,), (0,)), ((), ())), preferred_element_type=jnp.float32
-    )
-    window = keys_ref[:, pl.ds(start, 2 * LANES)].astype(jnp.float32)
-    lane = start + lax.broadcasted_iota(jnp.int32, window.shape, 1)
-    window = jnp.where((lane >= count) & (lane < count + steps), fresh, window)
-    keys_ref[:, pl.ds(start, 2 * LANES)] = window.astype(jnp.bfloat16)
+    capacity = keys_ref.shape[0]
+    start = jnp.minimum(count // UNIT * UNIT, capacity - 2 * UNIT)
+    start = pl.multiple_of(start, UNIT)
+    window = keys_ref[pl.ds(start, 2 * UNIT), :].astype(jnp.float32)
+    row = start + lax.broadcasted_iota(jnp.int32, window.shape, 0)
+    for step in range(recent.shape[0]):
+        window = jnp.where(row == count + step, recent[step : step + 1], window)
+    keys_ref[pl.ds(start, 2 * UNIT), :] = window.astype(jnp.bfloat16)
 
 
 def unit_rows(got_ref, at):
@@ -147,54 +144,108 @@
         ]
 
 
-def attend_kernel(plan, counts_ref, got_ref, cache_ref, recent_ref, out_ref, keys_ref, sems):
-    units = sum(len(group) for group in plan)
-    copies = [
-        pltpu.make_async_copy(cache_ref.at[place], keys_ref.at[place], sems.at[place])
-        for place in range(len(plan))
-    ]
-    for copy in copies:
-        copy.start()
-    for place, group in enumerate(plan):
-        copies[place].wait()
-        count = counts_ref[place]
-        keys = keys_ref.at[place]
-        place_recent(keys, recent_ref[place], count)
-        for unit, first_step in group:
-            at = unit * CHUNKS * UNIT
-            rope = unit_rows(got_ref, (units * CHUNKS + unit // 2) * UNIT)
-            rope = rope[:, unit % 2 * ROPE : unit % 2 * ROPE + ROPE]
-            query = jnp.concatenate(unit_latent(got_ref, at) + [rope], axis=1)
-            put_unit(out_ref, at, attend_unit(query, keys, count, first_step))
-
-
-def attend(got, cache, recent, counts, plan, name):
-    columns = got.shape[0]
-    units = sum(len(group) for group in plan)
-    places = len(plan)
+def prepare_kernel(counts_ref, cache_ref, recent_ref, keys_ref, fresh_ref):
+    for place in range(cache_ref.shape[0]):
+        for at in range(0, cache_ref.shape[2], LANES):
+            keys_ref[place, pl.ds(at, LANES), :] = cache_ref[place, :, pl.ds(at, LANES)].T
+        recent = recent_ref[place].astype(jnp.float32)
+        place_recent(keys_ref.at[place], recent, counts_ref[place])
+        if place == 0:
+            late = jnp.concatenate([recent[2:], jnp.zeros((6, recent.shape[1]))], axis=0)
+            rope = jnp.concatenate([late[:, LATENT:], jnp.zeros((8, ROPE))], axis=1)
+            pieces = [late[:, at : at + LANES] for at in range(0, LATENT, LANES)] + [rope]
+            pieces.append(jnp.zeros((MOVED_ROWS - 8 * len(pieces), LANES)))
+            fresh_ref[0] = jnp.concatenate(pieces, axis=0).astype(jnp.bfloat16)
+
+
+def prepare(counts, cache, recent):
+    places, entries, capacity = cache.shape
     vmem = pl.BlockSpec(memory_space=pltpu.VMEM)
     return pl.pallas_call(
-        functools.partial(attend_kernel, plan),
-        out_shape=pltpu.HBM((columns, units * CHUNKS * UNIT, LANES), jnp.bfloat16),
-        in_specs=[
-            pl.BlockSpec(memory_space=pltpu.SMEM),
-            vmem,
-            pl.BlockSpec(memory_space=pltpu.HBM),
-            vmem,
-        ],
-        out_specs=vmem,
-        scratch_shapes=[
-            pltpu.VMEM((places,) + cache.shape[1:], jnp.bfloat16),
-            pltpu.SemaphoreType.DMA((places,)),
-        ],
-        compiler_params=pltpu.CompilerParams(vmem_limit_bytes=32 * 1024 * 1024),
+        prepare_kernel,
+        out_shape=(
+            pltpu.VMEM((places, capacity, entries), jnp.bfloat16),
+            pltpu.HBM((1, MOVED_ROWS, LANES), jnp.bfloat16),
+        ),
+        in_specs=[pl.BlockSpec(memory_space=pltpu.SMEM), vmem, vmem],
+        out_specs=(vmem, vmem),
+        compiler_params=pltpu.CompilerParams(vmem_limit_bytes=24 * 1024 * 1024),
+        cost_estimate=pl.CostEstimate(
+            flops=1024 * 1024, bytes_accessed=8 * 1024 * 1024, transcendentals=0
+        ),
+        name="prepare",
+    )(counts, cache, recent)
+
+
+def step_of_row(rows, first_step):
+    return first_step + lax.broadcasted_iota(jnp.int32, (rows, 1), 0) % UNIT // 8
+
+
+def attend_held_kernel(counts_ref, got_ref, keys, out_hbm, out_ref, sems):
+    span = CHUNKS * UNIT
+    sends = []
+    for unit, (place, first_step) in enumerate([(0, 0), (1, 0), (1, 2)]):
+        rope = unit_rows(got_ref, (3 * CHUNKS + unit // 2) * UNIT)
+        rope = rope[:, unit % 2 * ROPE : unit % 2 * ROPE + ROPE]
+        latent = unit_latent(got_ref, unit * span)
+        query = jnp.concatenate(latent + [rope], axis=1)
+        live = counts_ref[place] + step_of_row(query.shape[0], first_step) + 1
+        put_unit(out_ref, unit * span, attend_unit(query, keys[place], live))
+        send = pltpu.make_async_copy(
+            out_ref.at[:, pl.ds(unit * span, span), :],
+            out_hbm.at[:, pl.ds(unit * span, span), :],
+            sems.at[unit],
+        )
+        send.start()
+        sends.append(send)
+    for send in sends:
+        send.wait()
+
+
+def attend_moved_kernel(counts_ref, got_ref, keys_ref, out_ref, keys, sems):
+    columns = out_ref.shape[0]
+    copy = pltpu.make_async_copy(keys_ref.at[0], keys.at[0], sems.at[0])
+    copy.start()
+    rows = got_ref.at[pl.ds(0, columns)]
+    both = rows[:, pl.ds(CHUNKS * UNIT, UNIT // 2), :].astype(jnp.float32)
+    rope = jnp.concatenate([both[:, :, :ROPE], both[:, :, ROPE:]], axis=1)
+    rope = rope.reshape(columns * UNIT, ROPE).astype(jnp.bfloat16)
+    query = jnp.concatenate(unit_latent(rows, 0) + [rope], axis=1)
+    fresh = got_ref[columns].astype(jnp.float32)
+    pieces = [fresh[8 * chunk : 8 * chunk + 8] for chunk in range(CHUNKS + 1)]
+    fresh = jnp.concatenate(pieces[:CHUNKS] + [pieces[CHUNKS][:, :ROPE]], axis=1)
+    count = counts_ref[0]
+    live = count + step_of_row(query.shape[0], 2) + 1
+    copy.wait()
+    place_recent(keys.at[0], fresh[:2], count + 2)
+    put_unit(out_ref, 0, attend_unit(query, keys[0], live))
+
+
+def in_hbm(value):
+    return pltpu.with_memory_space_constraint(value, pltpu.HBM)
+
+
+def attend(kernel, counts, got, keys, columns, units, name):
+    vmem = pl.BlockSpec(memory_space=pltpu.VMEM)
+    shape = (columns, units * CHUNKS * UNIT, LANES)
+    if units > 1:
+        out_spec, scratch = pl.BlockSpec(memory_space=pltpu.HBM), pltpu.VMEM(shape, jnp.bfloat16)
+    else:
+        out_spec, scratch = vmem, pltpu.VMEM((1,) + keys.shape[1:], jnp.bfloat16)
+    return pl.pallas_call(
+        kernel,
+        out_shape=pltpu.HBM(shape, jnp.bfloat16),
+        in_specs=[pl.BlockSpec(memory_space=pltpu.SMEM), vmem, vmem],
+        out_specs=out_spec,
+        scratch_shapes=[scratch, pltpu.SemaphoreType.DMA((units,))],
+        compiler_params=pltpu.CompilerParams(vmem_limit_bytes=28 * 1024 * 1024),
         cost_estimate=pl.CostEstimate(
             flops=units * 256 * 1024 * 1152 * 2,
             bytes_accessed=units * 2 * 1024 * 1024,
             transcendentals=units * 256 * 1024,
         ),
         name=name,
-    )(counts, got, cache, recent)
+    )(counts, got, keys)
 
 
 def project_unit(got_ref, at, w_ref):
@@ -276,25 +327,25 @@
     q_rope = q_rope.reshape(steps, slots * heads, ROPE)
     cache = jnp.swapaxes(latent_cache, 1, 2)
     recent = jnp.swapaxes(new_latent, 0, 1)
-
     moved_out = absorb(q_nope, q_rope, w_absorb_k, columns, (2, 3), [(2, 0)], "absorb_moved")
     held_out = absorb(
         q_nope, q_rope, w_absorb_k, columns, (0, 1, 2, 3), [(0, 0), (0, 1), (2, 1)], "absorb_held"
     )
     moved_in = exchanged(moved_out)
-    fresh = shifted(new_latent[2:, 0], shift, -1)
-    held_out, fresh = lax.optimization_barrier((held_out, fresh))
+    keys, fresh = prepare(counts, cache, recent)
+    moved_in = jnp.concatenate([moved_in, fresh], axis=0)
+    held_out, keys, moved_in = lax.optimization_barrier((held_out, keys, moved_in))
     held_in = exchanged(held_out)
-    moved_recent = jnp.concatenate([recent[:1, :2], fresh[None]], axis=1)
     moved_in = shifted(moved_in, shift, -1)
-    moved_mixed = attend(moved_in, cache, moved_recent, counts, [[(0, 2)]], "attend_moved")
     held_mixed = attend(
-        held_in, cache, recent, counts, [[(0, 0)], [(1, 0), (2, 2)]], "attend_held"
-    )
-    held_mixed, moved_mixed = lax.optimization_barrier((held_mixed, moved_mixed))
+        attend_held_kernel, counts, held_in, keys, columns, 3, "attend_held"
+    )
+    moved_in, held_mixed = lax.optimization_barrier((moved_in, held_mixed))
     held_back = exchanged(held_mixed)
-    moved_back = shifted(moved_mixed, shift, 1)
-    moved_back = exchanged(moved_back)
+    moved_mixed = attend(
+        attend_moved_kernel, counts, moved_in, keys, columns, 1, "attend_moved"
+    )
+    moved_back = exchanged(shifted(moved_mixed, shift, 1))
     part = project(project_held_kernel, (held_back, w_absorb_v), 3, "project_held")
     out = project(project_moved_kernel, (moved_back, w_absorb_v, part), 1, "project_moved")
     return out.reshape(steps, slots, heads, HEAD_DIM)

time: 122 us -> 110 us (0.902)
  starting transfers between devices: 58.1 us -> 43 us
  local copies, waits for them, and re-layouts: 0.8 us -> 4.36 us
    all_to_all x4, starting transfers between devices: 36.1 us -> 27.3 us  [exchanged(): lax.all_to_all(value, 'head', split_axis=0, concat_axis=0, tiled=True)]
    ppermute x3 -> x2, starting transfers between devices: 22 us -> 15.7 us  [along(): return lambda given: lax.ppermute(given, 'grp', pairs)]
    ppermute x3 -> x2, waiting for transfers between devices: 26 us -> 21.1 us  [along(): return lambda given: lax.ppermute(given, 'grp', pairs)]
    all_to_all x4, waiting for transfers between devices: 16.1 us -> 20.6 us  [exchanged(): lax.all_to_all(value, 'head', split_axis=0, concat_axis=0, tiled=True)]
    unnamed x7 -> x9, local copies, waits for them, and re-layouts: 0.02 us -> 3.6 us
    pallas_call x2 -> x3, Pallas kernels: 10.2 us -> 9.29 us  [the longest x2 7.44 us: attend(): pl.pallas_call(kernel, out_shape=pltpu.HBM(shape, jnp.bfloat16), in_specs...]
  transfers between devices with their start and end apart: 7 -> 6, of which waited for: 6 -> 6; matrix products, arithmetic and copies ran while one was open for 1% -> 1% of each run, Pallas kernels for 7% -> 9%
where the time goes in v3:
time: 110 us; the launch traced here: 108 us
  starting transfers between devices  43 us (39%)
  waiting for transfers between devices  41.7 us (38%)
  Pallas kernels  17.3 us (16%)
  local copies, waits for them, and re-layouts  4.36 us (4%)
    all_to_all x4, starting transfers between devices, exchanged(): lax.all_to_all(value, 'head', split_axis=0, concat_axis=0, tiled=True)  27.3 us
    ppermute x2, waiting for transfers between devices, along(): return lambda given: lax.ppermute(given, 'grp', pairs)  21.1 us
    all_to_all x4, waiting for transfers between devices, exchanged(): lax.all_to_all(value, 'head', split_axis=0, concat_axis=0, tiled=True)  20.6 us
    ppermute x2, starting transfers between devices, along(): return lambda given: lax.ppermute(given, 'grp', pairs)  15.7 us
    pallas_call x2, Pallas kernels, attend(): pl.pallas_call(kernel, out_shape=pltpu.HBM(shape, jnp.bfloat16), in_specs...  7.44 us
    pallas_call x2, Pallas kernels, absorb(): pl.pallas_call(functools.partial(absorb_kernel, steps, units), out_shape=...  5.9 us
    unnamed x9, local copies, waits for them, and re-layouts  3.6 us
  transfers between devices with their start and end apart: 6, of which 6 were waited for; matrix products, arithmetic and copies ran while one was open for 1% of the time, Pallas kernels for 9%

profile of v3, /device:TPU:1, one launch (start us, length us, event | category | flops | bytes accessed | tf_op | source)
XLA Modules:
  0.0 107.9 jit_solution(10760239448122518907)
XLA Ops:
  0.0 2.5 %absorb_moved.1 = bf16[16,72,128]{2,1,0:T(8,128)(2,1)} custom-call(bf16[4,256,128]{2,1,0:T(8,128)(2,1)} %bitcast.10, bf16[4,256,64]{2,1,0:T(8,128)(2,1)} %bitcast.12, bf16[8,128,512]{2,1,0:T(8,128)(2,1)} %w_hbm.3), custom_call_target="tpu_custom_call" | custom-call | flops 268435456 | bytes 3145728 | tf_op jit(solution)/shard_map/absorb_moved/pallas_call | solution.py:83
  2.5 11.8 %all-to-all-start = ((bf16[16,72,128]{2,1,0:T(8,128)(2,1)}), bf16[16,72,128]{2,1,0:T(8,128)(2,1)S(1)}, u32[]{:S(2)}, u32[]{:S(2)}) async-start(bf16[16,72,128]{2,1,0:T(8,128)(2,1)} %absorb_moved.1), calls=%async_computation | async-start | bytes 589824 | tf_op jit(solution)/shard_map/all_to_all | solution.py:315
  15.1 0.8 dynamic_slice.3.counts_ref
  15.9 1.7 %copy-done = bf16[2,1024,576]{1,2,0:T(8,128)(2,1)S(1)} copy-done((bf16[2,1024,576]{1,2,0:T(8,128)(2,1)S(1)}, bf16[2,1024,576]{1,2,0:T(8,128)(2,1)}, u32[]{:S(2)}) %copy-start) | copy-done | bytes 2359320
  17.5 1.8 %prepare.1 = (bf16[2,1024,576]{2,1,0:T(8,128)(2,1)S(1)}, bf16[1,72,128]{2,1,0:T(8,128)(2,1)}) custom-call(s32[2]{0:T(128)S(1)} %dynamic_slice.3.counts_ref, bf16[2,576,1024]{2,1,0:T(8,128)(2,1)S(1)} %bitcast.8, bf16[2,4,576]{2,1,0:T(4,128)(2,1)S(1)} %bitcast.9), custom_call_target="tpu_custom_call" | custom-call | flops 1048576 | bytes 8388608 | tf_op jit(solution)/shard_map/prepare/pallas_call | solution.py:164
  19.4 3.4 %absorb_held.1 = bf16[16,224,128]{2,1,0:T(8,128)(2,1)} custom-call(bf16[4,256,128]{2,1,0:T(8,128)(2,1)} %bitcast.11, bf16[4,256,64]{2,1,0:T(8,128)(2,1)} %bitcast.13, bf16[8,128,512]{2,1,0:T(8,128)(2,1)} %w_hbm.3), custom_call_target="tpu_custom_call" | custom-call | flops 805306368 | bytes 3145728 | tf_op jit(solution)/shard_map/absorb_held/pallas_call | solution.py:83
  22.7 4.0 %all-to-all-done = bf16[16,72,128]{2,1,0:T(8,128)(2,1)S(1)} async-done(((bf16[16,72,128]{2,1,0:T(8,128)(2,1)}), bf16[16,72,128]{2,1,0:T(8,128)(2,1)S(1)}, u32[]{:S(2)}, u32[]{:S(2)}) %all-to-all-start) | async-done | bytes 294944 | tf_op jit(solution)/shard_map/all_to_all | solution.py:315
  27.5 3.5 %all-to-all-start.1 = ((bf16[16,224,128]{2,1,0:T(8,128)(2,1)}), bf16[16,224,128]{2,1,0:T(8,128)(2,1)S(1)}, u32[]{:S(2)}, u32[]{:S(2)}) async-start(bf16[16,224,128]{2,1,0:T(8,128)(2,1)} %absorb_held.1), calls=%async_computation.1 | async-start | bytes 1835008 | tf_op jit(solution)/shard_map/all_to_all | solution.py:315
  31.7 19.8 %conditional.2 = (bf16[17,72,128]{2,1,0:T(8,128)(2,1)}) conditional(s32[]{:T(128)} %bitcast, bf16[17,72,128]{2,1,0:T(8,128)(2,1)} %pad_maximum_fusion, bf16[17,72,128]{2,1,0:T(8,128)(2,1)} %pad_maximum_fusion, bf16[17,72,128]{2,1,0:T(8,128)(2,1)} %pad_maximum_fusion, ...), branch_computations={%region_0.0_spmd, %region_1.0_spmd, %region_2.0_spmd, %region_3.0_... | conditional | bytes 1253424 | solution.py:311
  31.7 8.4 %collective-permute-start.14 = (bf16[17,72,128]{2,1,0:T(8,128)(2,1)}, bf16[17,72,128]{2,1,0:T(8,128)(2,1)}, u32[]{:S(2)}, u32[]{:S(2)}) collective-permute-start(bf16[17,72,128]{2,1,0:T(8,128)(2,1)} %param.14), channel_id=1, source_target_pairs={{0,272},{16,288},{32,304},{48,320},{64,336},{80,352},{96,368},{112... | collective-permute-start | bytes 940040 | tf_op jit(solution)/shard_map/cond/branch_14_fun/ppermute | solution.py:308
  40.1 11.4 %collective-permute-done.14 = bf16[17,72,128]{2,1,0:T(8,128)(2,1)} collective-permute-done((bf16[17,72,128]{2,1,0:T(8,128)(2,1)}, bf16[17,72,128]{2,1,0:T(8,128)(2,1)}, u32[]{:S(2)}, u32[]{:S(2)}) %collective-permute-start.14) | collective-permute-done | bytes 313376 | tf_op jit(solution)/shard_map/cond/branch_14_fun/ppermute | solution.py:308
  51.5 4.5 %all-to-all-done.1.got_ref = bf16[16,224,128]{2,1,0:T(8,128)(2,1)S(1)} async-done(((bf16[16,224,128]{2,1,0:T(8,128)(2,1)}), bf16[16,224,128]{2,1,0:T(8,128)(2,1)S(1)}, u32[]{:S(2)}, u32[]{:S(2)}) %all-to-all-start.1) | async-done | bytes 917536 | tf_op jit(solution)/shard_map/all_to_all | solution.py:315
  56.0 4.4 %attend_held.1 = bf16[16,192,128]{2,1,0:T(8,128)(2,1)} custom-call(s32[2]{0:T(128)S(1)} %dynamic_slice.3.counts_ref, bf16[16,224,128]{2,1,0:T(8,128)(2,1)S(1)} %all-to-all-done.1.got_ref, bf16[2,1024,576]{2,1,0:T(8,128)(2,1)S(1)} %get-tuple-element.142.keys.keys_ref), custom_call_target="tpu_custom_call" | custom-call | flops 1811939328 | bytes 6291456 | tf_op jit(solution)/shard_map/attend_held/pallas_call | solution.py:235
  60.5 4.5 %all-to-all-start.3 = ((bf16[16,192,128]{2,1,0:T(8,128)(2,1)}), bf16[16,192,128]{2,1,0:T(8,128)(2,1)S(1)}, u32[]{:S(2)}, u32[]{:S(2)}) async-start(bf16[16,192,128]{2,1,0:T(8,128)(2,1)} %attend_held.1), calls=%async_computation.3 | async-start | bytes 1572864 | tf_op jit(solution)/shard_map/all_to_all | solution.py:315
  64.9 3.0 %attend_moved.1 = bf16[16,64,128]{2,1,0:T(8,128)(2,1)} custom-call(s32[2]{0:T(128)S(1)} %dynamic_slice.3.counts_ref, bf16[17,72,128]{2,1,0:T(8,128)(2,1)} %get-tuple-element.145.got_ref, bf16[2,1024,576]{2,1,0:T(8,128)(2,1)S(1)} %get-tuple-element.142.keys.keys_ref), custom_call_target="tpu_custom_call" | custom-call | flops 603979776 | bytes 2097152 | tf_op jit(solution)/shard_map/attend_moved/pallas_call | solution.py:235
  68.0 17.1 %conditional.3 = (bf16[16,64,128]{2,1,0:T(8,128)(2,1)}) conditional(s32[]{:T(128)} %bitcast, bf16[16,64,128]{2,1,0:T(8,128)(2,1)} %attend_moved.1, bf16[16,64,128]{2,1,0:T(8,128)(2,1)} %attend_moved.1, bf16[16,64,128]{2,1,0:T(8,128)(2,1)} %attend_moved.1, bf16[16,64,128]{2,1,0:T(8,128)(2,1)} %attend_moved.1, ...), branch_computations={%region_31.0_spmd, %region_32.0_spmd, %region_33.0_spmd, %region_3... | conditional | bytes 1048624 | solution.py:311
  68.0 7.3 %collective-permute-start.45 = (bf16[16,64,128]{2,1,0:T(8,128)(2,1)}, bf16[16,64,128]{2,1,0:T(8,128)(2,1)}, u32[]{:S(2)}, u32[]{:S(2)}) collective-permute-start(bf16[16,64,128]{2,1,0:T(8,128)(2,1)} %param.45), channel_id=1, source_target_pairs={{0,240},{16,256},{32,272},{48,288},{64,304},{80,320},{96,336},{112... | collective-permute-start | bytes 786440 | tf_op jit(solution)/shard_map/cond/branch_14_fun/ppermute | solution.py:308
  75.3 9.7 %collective-permute-done.45 = bf16[16,64,128]{2,1,0:T(8,128)(2,1)} collective-permute-done((bf16[16,64,128]{2,1,0:T(8,128)(2,1)}, bf16[16,64,128]{2,1,0:T(8,128)(2,1)}, u32[]{:S(2)}, u32[]{:S(2)}) %collective-permute-start.45) | collective-permute-done | bytes 262176 | tf_op jit(solution)/shard_map/cond/branch_14_fun/ppermute | solution.py:308
  85.0 2.6 %all-to-all-done.3.got_ref = bf16[16,192,128]{2,1,0:T(8,128)(2,1)S(1)} async-done(((bf16[16,192,128]{2,1,0:T(8,128)(2,1)}), bf16[16,192,128]{2,1,0:T(8,128)(2,1)S(1)}, u32[]{:S(2)}, u32[]{:S(2)}) %all-to-all-start.3) | async-done | bytes 786464 | tf_op jit(solution)/shard_map/all_to_all | solution.py:315
  87.6 7.5 %all-to-all-start.2 = ((bf16[16,64,128]{2,1,0:T(8,128)(2,1)}), bf16[16,64,128]{2,1,0:T(8,128)(2,1)S(1)}, u32[]{:S(2)}, u32[]{:S(2)}) async-start(bf16[16,64,128]{2,1,0:T(8,128)(2,1)} %get-tuple-element.146), calls=%async_computation.2 | async-start | bytes 524288 | tf_op jit(solution)/shard_map/all_to_all | solution.py:315
  95.1 1.2 %copy-done.1 = bf16[8,512,128]{2,1,0:T(8,128)(2,1)S(1)} copy-done((bf16[8,512,128]{2,1,0:T(8,128)(2,1)S(1)}, bf16[8,512,128]{2,1,0:T(8,128)(2,1)}, u32[]{:S(2)}) %copy-start.1) | copy-done | bytes 1048600
  96.3 1.0 project_held.1.part_ref
  97.3 9.5 %all-to-all-done.2.got_ref = bf16[16,64,128]{2,1,0:T(8,128)(2,1)S(1)} async-done(((bf16[16,64,128]{2,1,0:T(8,128)(2,1)}), bf16[16,64,128]{2,1,0:T(8,128)(2,1)S(1)}, u32[]{:S(2)}, u32[]{:S(2)}) %all-to-all-start.2) | async-done | bytes 262176 | tf_op jit(solution)/shard_map/all_to_all | solution.py:315
  106.8 1.1 %project_moved.1 = bf16[4,256,128]{2,1,0:T(8,128)(2,1)} custom-call(bf16[16,64,128]{2,1,0:T(8,128)(2,1)S(1)} %all-to-all-done.2.got_ref, bf16[8,512,128]{2,1,0:T(8,128)(2,1)S(1)} %copy-done.2, bf16[4,256,128]{2,1,0:T(8,128)(2,1)S(1)} %project_held.1.part_ref), custom_call_target="tpu_custom_call" | custom-call | flops 268435456 | bytes 2097152 | tf_op jit(solution)/shard_map/project_moved/pallas_call | solution.py:292
  (8 shorter events, 1.5 us)
Async XLA Ops:
  2.5 24.2 %all-to-all-start = ((bf16[16,72,128]{2,1,0:T(8,128)(2,1)}), bf16[16,72,128]{2,1,0:T(8,128)(2,1)S(1)}, u32[]{:S(2)}, u32[]{:S(2)}) async-start(bf16[16,72,128]{2,1,0:T(8,128)(2,1)} %absorb_moved.1), calls=%async_computation | async-start | bytes 589824 | tf_op jit(solution)/shard_map/all_to_all | solution.py:315
  15.9 1.7 %copy-start = (bf16[2,1024,576]{1,2,0:T(8,128)(2,1)S(1)}, bf16[2,1024,576]{1,2,0:T(8,128)(2,1)}, u32[]{:S(2)}) copy-start(bf16[2,1024,576]{1,2,0:T(8,128)(2,1)} %param.74) | copy-start | bytes 7077892
  19.4 7.4 %copy-start.3 = (bf16[1,72,128]{2,1,0:T(8,128)(2,1)S(1)}, bf16[1,72,128]{2,1,0:T(8,128)(2,1)}, u32[]{:S(2)}) copy-start(bf16[1,72,128]{2,1,0:T(8,128)(2,1)} %get-tuple-element.139) | copy-start | bytes 55300
  27.5 28.5 %all-to-all-start.1 = ((bf16[16,224,128]{2,1,0:T(8,128)(2,1)}), bf16[16,224,128]{2,1,0:T(8,128)(2,1)S(1)}, u32[]{:S(2)}, u32[]{:S(2)}) async-start(bf16[16,224,128]{2,1,0:T(8,128)(2,1)} %absorb_held.1), calls=%async_computation.1 | async-start | bytes 1835008 | tf_op jit(solution)/shard_map/all_to_all | solution.py:315
  31.7 19.8 %collective-permute-start.14 = (bf16[17,72,128]{2,1,0:T(8,128)(2,1)}, bf16[17,72,128]{2,1,0:T(8,128)(2,1)}, u32[]{:S(2)}, u32[]{:S(2)}) collective-permute-start(bf16[17,72,128]{2,1,0:T(8,128)(2,1)} %param.14), channel_id=1, source_target_pairs={{0,272},{16,288},{32,304},{48,320},{64,336},{80,352},{96,368},{112... | collective-permute-start | bytes 940040 | tf_op jit(solution)/shard_map/cond/branch_14_fun/ppermute | solution.py:308
  60.5 27.1 %all-to-all-start.3 = ((bf16[16,192,128]{2,1,0:T(8,128)(2,1)}), bf16[16,192,128]{2,1,0:T(8,128)(2,1)S(1)}, u32[]{:S(2)}, u32[]{:S(2)}) async-start(bf16[16,192,128]{2,1,0:T(8,128)(2,1)} %attend_held.1), calls=%async_computation.3 | async-start | bytes 1572864 | tf_op jit(solution)/shard_map/all_to_all | solution.py:315
  68.0 17.0 %collective-permute-start.45 = (bf16[16,64,128]{2,1,0:T(8,128)(2,1)}, bf16[16,64,128]{2,1,0:T(8,128)(2,1)}, u32[]{:S(2)}, u32[]{:S(2)}) collective-permute-start(bf16[16,64,128]{2,1,0:T(8,128)(2,1)} %param.45), channel_id=1, source_target_pairs={{0,240},{16,256},{32,272},{48,288},{64,304},{80,320},{96,336},{112... | collective-permute-start | bytes 786440 | tf_op jit(solution)/shard_map/cond/branch_14_fun/ppermute | solution.py:308
  87.6 19.2 %all-to-all-start.2 = ((bf16[16,64,128]{2,1,0:T(8,128)(2,1)}), bf16[16,64,128]{2,1,0:T(8,128)(2,1)S(1)}, u32[]{:S(2)}, u32[]{:S(2)}) async-start(bf16[16,64,128]{2,1,0:T(8,128)(2,1)} %get-tuple-element.146), calls=%async_computation.2 | async-start | bytes 524288 | tf_op jit(solution)/shard_map/all_to_all | solution.py:315
  95.1 1.2 %copy-start.1 = (bf16[8,512,128]{2,1,0:T(8,128)(2,1)S(1)}, bf16[8,512,128]{2,1,0:T(8,128)(2,1)}, u32[]{:S(2)}) copy-start(bf16[8,512,128]{2,1,0:T(8,128)(2,1)} %w_ref.3) | copy-start | bytes 3145732
  96.3 10.5 %copy-start.2 = (bf16[8,512,128]{2,1,0:T(8,128)(2,1)S(1)}, bf16[8,512,128]{2,1,0:T(8,128)(2,1)}, u32[]{:S(2)}) copy-start(bf16[8,512,128]{2,1,0:T(8,128)(2,1)} %w_ref.3) | copy-start | bytes 3145732

commit v4 on v3

--- a/solution.py
+++ b/solution.py
@@ -15,6 +15,7 @@
 CHUNKS = LATENT // LANES
 UNIT = 16
 MOVED_ROWS = CHUNKS * UNIT + UNIT // 2
+PARTS = 4
 HIDDEN = -1e30
 LOG2_E = 1.4426950408889634
 
@@ -46,8 +47,13 @@
     copies = [
         pltpu.make_async_copy(q_hbm.at[pl.ds(first, len(steps))], q_ref, sems.at[0]),
         pltpu.make_async_copy(r_hbm.at[pl.ds(first, len(steps))], r_ref, sems.at[1]),
-        pltpu.make_async_copy(w_hbm, w_ref, sems.at[2]),
     ]
+    step = heads // PARTS
+    for part in range(PARTS):
+        piece = pl.ds(part * step, step)
+        copies.append(
+            pltpu.make_async_copy(w_hbm.at[piece], w_ref.at[piece], sems.at[2 + part])
+        )
     for copy in copies:
         copy.start()
     copies[0].wait()
@@ -58,26 +64,33 @@
     def unit_of(parts, begin, place):
         return jnp.concatenate([parts[begin][place], parts[begin + 1][place]], axis=1)
 
-    blank = jnp.zeros((columns, UNIT, ROPE), jnp.float32)
-    if len(units) == 1:
-        begin, place = units[0]
-        both = jnp.concatenate([rope[begin][place], rope[begin + 1][place]], axis=2)
-        out_ref[:, pl.ds(CHUNKS * UNIT, UNIT // 2), :] = both.astype(jnp.bfloat16)
-    for number in range(0, len(units) if len(units) > 1 else 0, 2):
-        pair = [unit_of(rope, *unit) for unit in units[number : number + 2]] + [blank]
-        at = (len(units) * CHUNKS + number // 2) * UNIT
-        both = jnp.concatenate(pair[:2], axis=2).astype(jnp.bfloat16)
+    at = len(units) * CHUNKS * UNIT
+    if len(units) > 1:
+        pair = [unit_of(rope, *unit) for unit in units[:2]]
+        both = jnp.concatenate(pair, axis=2).astype(jnp.bfloat16)
         out_ref[:, pl.ds(at, UNIT), :] = both
-    copies[2].wait()
-    weights = w_ref[...].reshape(heads * HEAD_DIM, LATENT)
-    for number, unit in enumerate(units):
-        spread = spread_heads(unit_of(nope, *unit), heads)
-        latent = jnp.dot(spread, weights, preferred_element_type=jnp.float32)
-        put_unit(out_ref, number * CHUNKS * UNIT, latent.astype(jnp.bfloat16))
+        at += UNIT
+    begin, place = units[-1]
+    both = jnp.concatenate([rope[begin][place], rope[begin + 1][place]], axis=2)
+    out_ref[:, pl.ds(at, UNIT // 2), :] = both.astype(jnp.bfloat16)
+    spreads = [spread_heads(unit_of(nope, *unit), heads) for unit in units]
+    spread = jnp.concatenate(spreads, axis=0)
+    latent = None
+    step = heads // PARTS
+    for part in range(PARTS):
+        copies[2 + part].wait()
+        weights = w_ref[pl.ds(part * step, step)].reshape(step * HEAD_DIM, LATENT)
+        rows = spread[:, part * step * HEAD_DIM : (part + 1) * step * HEAD_DIM]
+        term = jnp.dot(rows, weights, preferred_element_type=jnp.float32)
+        latent = term if latent is None else latent + term
+    latent = latent.astype(jnp.bfloat16)
+    for number in range(len(units)):
+        rows = latent[number * columns * UNIT : (number + 1) * columns * UNIT]
+        put_unit(out_ref, number * CHUNKS * UNIT, rows)
 
 
 def absorb(q_nope, q_rope, w_absorb_k, columns, steps, units, name):
-    high = MOVED_ROWS if len(units) == 1 else (len(units) * CHUNKS + (len(units) + 1) // 2) * UNIT
+    high = len(units) * (CHUNKS * UNIT + UNIT // 2)
     hbm = pl.BlockSpec(memory_space=pltpu.HBM)
     slots = q_nope.shape[1]
     return pl.pallas_call(
@@ -88,7 +101,7 @@
             pltpu.VMEM((len(steps), slots, HEAD_DIM), jnp.bfloat16),
             pltpu.VMEM((len(steps), slots, ROPE), jnp.bfloat16),
             pltpu.VMEM(w_absorb_k.shape, jnp.bfloat16),
-            pltpu.SemaphoreType.DMA((3,)),
+            pltpu.SemaphoreType.DMA((2 + PARTS,)),
         ],
         compiler_params=pltpu.CompilerParams(vmem_limit_bytes=32 * 1024 * 1024),
         cost_estimate=pl.CostEstimate(
@@ -181,23 +194,37 @@
     return first_step + lax.broadcasted_iota(jnp.int32, (rows, 1), 0) % UNIT // 8
 
 
+def packed_rope(got_ref, at):
+    columns = got_ref.shape[0]
+    both = got_ref[:, pl.ds(at, UNIT // 2), :].astype(jnp.float32)
+    rope = jnp.concatenate([both[:, :, :ROPE], both[:, :, ROPE:]], axis=1)
+    return rope.reshape(columns * UNIT, ROPE).astype(jnp.bfloat16)
+
+
 def attend_held_kernel(counts_ref, got_ref, keys, out_hbm, out_ref, sems):
     span = CHUNKS * UNIT
+    pair = unit_rows(got_ref, 3 * span)
+    ropes = [pair[:, :ROPE], pair[:, ROPE:], packed_rope(got_ref, 3 * span + UNIT)]
     sends = []
-    for unit, (place, first_step) in enumerate([(0, 0), (1, 0), (1, 2)]):
-        rope = unit_rows(got_ref, (3 * CHUNKS + unit // 2) * UNIT)
-        rope = rope[:, unit % 2 * ROPE : unit % 2 * ROPE + ROPE]
-        latent = unit_latent(got_ref, unit * span)
-        query = jnp.concatenate(latent + [rope], axis=1)
-        live = counts_ref[place] + step_of_row(query.shape[0], first_step) + 1
-        put_unit(out_ref, unit * span, attend_unit(query, keys[place], live))
-        send = pltpu.make_async_copy(
-            out_ref.at[:, pl.ds(unit * span, span), :],
-            out_hbm.at[:, pl.ds(unit * span, span), :],
-            sems.at[unit],
-        )
-        send.start()
-        sends.append(send)
+    for place, units in enumerate([[(0, 0)], [(1, 0), (2, 2)]]):
+        queries = []
+        lives = []
+        for unit, first_step in units:
+            latent = unit_latent(got_ref, unit * span)
+            queries.append(jnp.concatenate(latent + [ropes[unit]], axis=1))
+            rows = queries[-1].shape[0]
+            lives.append(counts_ref[place] + step_of_row(rows, first_step) + 1)
+        query = jnp.concatenate(queries, axis=0)
+        mixed = attend_unit(query, keys[place], jnp.concatenate(lives, axis=0))
+        for number, (unit, _) in enumerate(units):
+            put_unit(out_ref, unit * span, mixed[number * rows : (number + 1) * rows])
+            send = pltpu.make_async_copy(
+                out_ref.at[:, pl.ds(unit * span, span), :],
+                out_hbm.at[:, pl.ds(unit * span, span), :],
+                sems.at[unit],
+            )
+            send.start()
+            sends.append(send)
     for send in sends:
         send.wait()
 
@@ -207,10 +234,7 @@
     copy = pltpu.make_async_copy(keys_ref.at[0], keys.at[0], sems.at[0])
     copy.start()
     rows = got_ref.at[pl.ds(0, columns)]
-    both = rows[:, pl.ds(CHUNKS * UNIT, UNIT // 2), :].astype(jnp.float32)
-    rope = jnp.concatenate([both[:, :, :ROPE], both[:, :, ROPE:]], axis=1)
-    rope = rope.reshape(columns * UNIT, ROPE).astype(jnp.bfloat16)
-    query = jnp.concatenate(unit_latent(rows, 0) + [rope], axis=1)
+    query = jnp.concatenate(unit_latent(rows, 0) + [packed_rope(rows, CHUNKS * UNIT)], axis=1)
     fresh = got_ref[columns].astype(jnp.float32)
     pieces = [fresh[8 * chunk : 8 * chunk + 8] for chunk in range(CHUNKS + 1)]
     fresh = jnp.concatenate(pieces[:CHUNKS] + [pieces[CHUNKS][:, :ROPE]], axis=1)

time: 110 us -> 107 us (0.973)
  starting transfers between devices: 43 us -> 34.9 us
  waiting for transfers between devices: 41.7 us -> 46.6 us
    ppermute x2, starting transfers between devices: 15.7 us -> 10.1 us  [along(): return lambda given: lax.ppermute(given, 'grp', pairs)]
    all_to_all x4, waiting for transfers between devices: 20.6 us -> 24.8 us  [exchanged(): lax.all_to_all(value, 'head', split_axis=0, concat_axis=0, tiled=True)]
    all_to_all x4, starting transfers between devices: 27.3 us -> 24.8 us  [exchanged(): lax.all_to_all(value, 'head', split_axis=0, concat_axis=0, tiled=True)]
where the time goes in v4:
time: 107 us; the launch traced here: 104 us
  waiting for transfers between devices  46.6 us (44%)
  starting transfers between devices  34.9 us (33%)
  Pallas kernels  17.1 us (16%)
  local copies, waits for them, and re-layouts  4.36 us (4%)
    all_to_all x4, waiting for transfers between devices, exchanged(): lax.all_to_all(value, 'head', split_axis=0, concat_axis=0, tiled=True)  24.8 us
    all_to_all x4, starting transfers between devices, exchanged(): lax.all_to_all(value, 'head', split_axis=0, concat_axis=0, tiled=True)  24.8 us
    ppermute x2, waiting for transfers between devices, along(): return lambda given: lax.ppermute(given, 'grp', pairs)  21.8 us
    ppermute x2, starting transfers between devices, along(): return lambda given: lax.ppermute(given, 'grp', pairs)  10.1 us
    pallas_call x2, Pallas kernels, attend(): pl.pallas_call(kernel, out_shape=pltpu.HBM(shape, jnp.bfloat16), in_specs...  7.31 us
    pallas_call x2, Pallas kernels, absorb(): pl.pallas_call(functools.partial(absorb_kernel, steps, units), out_shape=...  5.77 us
    unnamed x9, local copies, waits for them, and re-layouts  3.6 us
    pallas_call x2, Pallas kernels, project(): pl.pallas_call(kernel, out_shape=jax.ShapeDtypeStruct((4, columns * UNIT,...  2.15 us
  transfers between devices with their start and end apart: 6, of which 6 were waited for; matrix products, arithmetic and copies ran while one was open for 1% of the time, Pallas kernels for 9%

profile of v4, /device:TPU:1, one launch (start us, length us, event | category | flops | bytes accessed | tf_op | source)
XLA Modules:
  0.0 104.5 jit_solution(6595132032310983625)
XLA Ops:
  0.0 2.5 %absorb_moved.1 = bf16[16,72,128]{2,1,0:T(8,128)(2,1)} custom-call(bf16[4,256,128]{2,1,0:T(8,128)(2,1)} %bitcast.10, bf16[4,256,64]{2,1,0:T(8,128)(2,1)} %bitcast.12, bf16[8,128,512]{2,1,0:T(8,128)(2,1)} %w_hbm.3), custom_call_target="tpu_custom_call" | custom-call | flops 268435456 | bytes 3145728 | tf_op jit(solution)/shard_map/absorb_moved/pallas_call | solution.py:96
  2.5 11.8 %all-to-all-start = ((bf16[16,72,128]{2,1,0:T(8,128)(2,1)}), bf16[16,72,128]{2,1,0:T(8,128)(2,1)S(1)}, u32[]{:S(2)}, u32[]{:S(2)}) async-start(bf16[16,72,128]{2,1,0:T(8,128)(2,1)} %absorb_moved.1), calls=%async_computation | async-start | bytes 589824 | tf_op jit(solution)/shard_map/all_to_all | solution.py:339
  15.8 1.7 %copy-done = bf16[2,1024,576]{1,2,0:T(8,128)(2,1)S(1)} copy-done((bf16[2,1024,576]{1,2,0:T(8,128)(2,1)S(1)}, bf16[2,1024,576]{1,2,0:T(8,128)(2,1)}, u32[]{:S(2)}) %copy-start) | copy-done | bytes 2359320
  17.5 1.8 %prepare.1 = (bf16[2,1024,576]{2,1,0:T(8,128)(2,1)S(1)}, bf16[1,72,128]{2,1,0:T(8,128)(2,1)}) custom-call(s32[2]{0:T(128)S(1)} %dynamic_slice.3.counts_ref, bf16[2,576,1024]{2,1,0:T(8,128)(2,1)S(1)} %bitcast.8, bf16[2,4,576]{2,1,0:T(4,128)(2,1)S(1)} %bitcast.9), custom_call_target="tpu_custom_call" | custom-call | flops 1048576 | bytes 8388608 | tf_op jit(solution)/shard_map/prepare/pallas_call | solution.py:177
  19.3 3.3 %absorb_held.1 = bf16[16,216,128]{2,1,0:T(8,128)(2,1)} custom-call(bf16[4,256,128]{2,1,0:T(8,128)(2,1)} %bitcast.11, bf16[4,256,64]{2,1,0:T(8,128)(2,1)} %bitcast.13, bf16[8,128,512]{2,1,0:T(8,128)(2,1)} %w_hbm.3), custom_call_target="tpu_custom_call" | custom-call | flops 805306368 | bytes 3145728 | tf_op jit(solution)/shard_map/absorb_held/pallas_call | solution.py:96
  22.6 4.1 %all-to-all-done = bf16[16,72,128]{2,1,0:T(8,128)(2,1)S(1)} async-done(((bf16[16,72,128]{2,1,0:T(8,128)(2,1)}), bf16[16,72,128]{2,1,0:T(8,128)(2,1)S(1)}, u32[]{:S(2)}, u32[]{:S(2)}) %all-to-all-start) | async-done | bytes 294944 | tf_op jit(solution)/shard_map/all_to_all | solution.py:339
  26.7 0.8 pad_maximum_fusion
  27.5 3.5 %all-to-all-start.1 = ((bf16[16,216,128]{2,1,0:T(8,128)(2,1)}), bf16[16,216,128]{2,1,0:T(8,128)(2,1)S(1)}, u32[]{:S(2)}, u32[]{:S(2)}) async-start(bf16[16,216,128]{2,1,0:T(8,128)(2,1)} %absorb_held.1), calls=%async_computation.1 | async-start | bytes 1769472 | tf_op jit(solution)/shard_map/all_to_all | solution.py:339
  31.7 16.5 %conditional.2 = (bf16[17,72,128]{2,1,0:T(8,128)(2,1)}) conditional(s32[]{:T(128)} %bitcast, bf16[17,72,128]{2,1,0:T(8,128)(2,1)} %pad_maximum_fusion, bf16[17,72,128]{2,1,0:T(8,128)(2,1)} %pad_maximum_fusion, bf16[17,72,128]{2,1,0:T(8,128)(2,1)} %pad_maximum_fusion, ...), branch_computations={%region_0.0_spmd, %region_1.0_spmd, %region_2.0_spmd, %region_3.0_... | conditional | bytes 1253424 | solution.py:335
  31.7 5.2 %collective-permute-start.19 = (bf16[17,72,128]{2,1,0:T(8,128)(2,1)}, bf16[17,72,128]{2,1,0:T(8,128)(2,1)}, u32[]{:S(2)}, u32[]{:S(2)}) collective-permute-start(bf16[17,72,128]{2,1,0:T(8,128)(2,1)} %param.19), channel_id=1, source_target_pairs={{0,192},{16,208},{32,224},{48,240},{64,256},{80,272},{96,288},{112... | collective-permute-start | bytes 940040 | tf_op jit(solution)/shard_map/cond/branch_19_fun/ppermute | solution.py:332
  36.9 11.2 %collective-permute-done.19 = bf16[17,72,128]{2,1,0:T(8,128)(2,1)} collective-permute-done((bf16[17,72,128]{2,1,0:T(8,128)(2,1)}, bf16[17,72,128]{2,1,0:T(8,128)(2,1)}, u32[]{:S(2)}, u32[]{:S(2)}) %collective-permute-start.19) | collective-permute-done | bytes 313376 | tf_op jit(solution)/shard_map/cond/branch_19_fun/ppermute | solution.py:332
  48.2 7.1 %all-to-all-done.1.got_ref = bf16[16,216,128]{2,1,0:T(8,128)(2,1)S(1)} async-done(((bf16[16,216,128]{2,1,0:T(8,128)(2,1)}), bf16[16,216,128]{2,1,0:T(8,128)(2,1)S(1)}, u32[]{:S(2)}, u32[]{:S(2)}) %all-to-all-start.1) | async-done | bytes 884768 | tf_op jit(solution)/shard_map/all_to_all | solution.py:339
  55.2 4.3 %attend_held.1 = bf16[16,192,128]{2,1,0:T(8,128)(2,1)} custom-call(s32[2]{0:T(128)S(1)} %dynamic_slice.3.counts_ref, bf16[16,216,128]{2,1,0:T(8,128)(2,1)S(1)} %all-to-all-done.1.got_ref, bf16[2,1024,576]{2,1,0:T(8,128)(2,1)S(1)} %get-tuple-element.142.keys.keys_ref), custom_call_target="tpu_custom_call" | custom-call | flops 1811939328 | bytes 6291456 | tf_op jit(solution)/shard_map/attend_held/pallas_call | solution.py:259
  59.5 5.4 %all-to-all-start.3 = ((bf16[16,192,128]{2,1,0:T(8,128)(2,1)}), bf16[16,192,128]{2,1,0:T(8,128)(2,1)S(1)}, u32[]{:S(2)}, u32[]{:S(2)}) async-start(bf16[16,192,128]{2,1,0:T(8,128)(2,1)} %attend_held.1), calls=%async_computation.3 | async-start | bytes 1572864 | tf_op jit(solution)/shard_map/all_to_all | solution.py:339
  64.9 3.0 %attend_moved.1 = bf16[16,64,128]{2,1,0:T(8,128)(2,1)} custom-call(s32[2]{0:T(128)S(1)} %dynamic_slice.3.counts_ref, bf16[17,72,128]{2,1,0:T(8,128)(2,1)} %get-tuple-element.145.got_ref, bf16[2,1024,576]{2,1,0:T(8,128)(2,1)S(1)} %get-tuple-element.142.keys.keys_ref), custom_call_target="tpu_custom_call" | custom-call | flops 603979776 | bytes 2097152 | tf_op jit(solution)/shard_map/attend_moved/pallas_call | solution.py:259
  68.0 15.4 %conditional.3 = (bf16[16,64,128]{2,1,0:T(8,128)(2,1)}) conditional(s32[]{:T(128)} %bitcast, bf16[16,64,128]{2,1,0:T(8,128)(2,1)} %attend_moved.1, bf16[16,64,128]{2,1,0:T(8,128)(2,1)} %attend_moved.1, bf16[16,64,128]{2,1,0:T(8,128)(2,1)} %attend_moved.1, bf16[16,64,128]{2,1,0:T(8,128)(2,1)} %attend_moved.1, ...), branch_computations={%region_31.0_spmd, %region_32.0_spmd, %region_33.0_spmd, %region_3... | conditional | bytes 1048624 | solution.py:335
  68.0 4.8 %collective-permute-start.50 = (bf16[16,64,128]{2,1,0:T(8,128)(2,1)}, bf16[16,64,128]{2,1,0:T(8,128)(2,1)}, u32[]{:S(2)}, u32[]{:S(2)}) collective-permute-start(bf16[16,64,128]{2,1,0:T(8,128)(2,1)} %param.50), channel_id=1, source_target_pairs={{0,320},{16,336},{32,352},{48,368},{64,384},{80,400},{96,416},{112... | collective-permute-start | bytes 786440 | tf_op jit(solution)/shard_map/cond/branch_19_fun/ppermute | solution.py:332
  72.8 10.6 %collective-permute-done.50 = bf16[16,64,128]{2,1,0:T(8,128)(2,1)} collective-permute-done((bf16[16,64,128]{2,1,0:T(8,128)(2,1)}, bf16[16,64,128]{2,1,0:T(8,128)(2,1)}, u32[]{:S(2)}, u32[]{:S(2)}) %collective-permute-start.50) | collective-permute-done | bytes 262176 | tf_op jit(solution)/shard_map/cond/branch_19_fun/ppermute | solution.py:332
  83.4 4.2 %all-to-all-done.3.got_ref = bf16[16,192,128]{2,1,0:T(8,128)(2,1)S(1)} async-done(((bf16[16,192,128]{2,1,0:T(8,128)(2,1)}), bf16[16,192,128]{2,1,0:T(8,128)(2,1)S(1)}, u32[]{:S(2)}, u32[]{:S(2)}) %all-to-all-start.3) | async-done | bytes 786464 | tf_op jit(solution)/shard_map/all_to_all | solution.py:339
  87.6 4.0 %all-to-all-start.2 = ((bf16[16,64,128]{2,1,0:T(8,128)(2,1)}), bf16[16,64,128]{2,1,0:T(8,128)(2,1)S(1)}, u32[]{:S(2)}, u32[]{:S(2)}) async-start(bf16[16,64,128]{2,1,0:T(8,128)(2,1)} %get-tuple-element.146), calls=%async_computation.2 | async-start | bytes 524288 | tf_op jit(solution)/shard_map/all_to_all | solution.py:339
  91.6 1.2 %copy-done.1 = bf16[8,512,128]{2,1,0:T(8,128)(2,1)S(1)} copy-done((bf16[8,512,128]{2,1,0:T(8,128)(2,1)S(1)}, bf16[8,512,128]{2,1,0:T(8,128)(2,1)}, u32[]{:S(2)}) %copy-start.1) | copy-done | bytes 1048600
  92.9 1.0 project_held.1.part_ref
  93.9 9.5 %all-to-all-done.2.got_ref = bf16[16,64,128]{2,1,0:T(8,128)(2,1)S(1)} async-done(((bf16[16,64,128]{2,1,0:T(8,128)(2,1)}), bf16[16,64,128]{2,1,0:T(8,128)(2,1)S(1)}, u32[]{:S(2)}, u32[]{:S(2)}) %all-to-all-start.2) | async-done | bytes 262176 | tf_op jit(solution)/shard_map/all_to_all | solution.py:339
  103.3 1.1 %project_moved.1 = bf16[4,256,128]{2,1,0:T(8,128)(2,1)} custom-call(bf16[16,64,128]{2,1,0:T(8,128)(2,1)S(1)} %all-to-all-done.2.got_ref, bf16[8,512,128]{2,1,0:T(8,128)(2,1)S(1)} %copy-done.2, bf16[4,256,128]{2,1,0:T(8,128)(2,1)S(1)} %project_held.1.part_ref), custom_call_target="tpu_custom_call" | custom-call | flops 268435456 | bytes 2097152 | tf_op jit(solution)/shard_map/project_moved/pallas_call | solution.py:316
  (8 shorter events, 1.5 us)
Async XLA Ops:
  2.5 24.2 %all-to-all-start = ((bf16[16,72,128]{2,1,0:T(8,128)(2,1)}), bf16[16,72,128]{2,1,0:T(8,128)(2,1)S(1)}, u32[]{:S(2)}, u32[]{:S(2)}) async-start(bf16[16,72,128]{2,1,0:T(8,128)(2,1)} %absorb_moved.1), calls=%async_computation | async-start | bytes 589824 | tf_op jit(solution)/shard_map/all_to_all | solution.py:339
  15.8 1.7 %copy-start = (bf16[2,1024,576]{1,2,0:T(8,128)(2,1)S(1)}, bf16[2,1024,576]{1,2,0:T(8,128)(2,1)}, u32[]{:S(2)}) copy-start(bf16[2,1024,576]{1,2,0:T(8,128)(2,1)} %param.74) | copy-start | bytes 7077892
  19.3 7.4 %copy-start.3 = (bf16[1,72,128]{2,1,0:T(8,128)(2,1)S(1)}, bf16[1,72,128]{2,1,0:T(8,128)(2,1)}, u32[]{:S(2)}) copy-start(bf16[1,72,128]{2,1,0:T(8,128)(2,1)} %get-tuple-element.139) | copy-start | bytes 55300
  27.5 27.8 %all-to-all-start.1 = ((bf16[16,216,128]{2,1,0:T(8,128)(2,1)}), bf16[16,216,128]{2,1,0:T(8,128)(2,1)S(1)}, u32[]{:S(2)}, u32[]{:S(2)}) async-start(bf16[16,216,128]{2,1,0:T(8,128)(2,1)} %absorb_held.1), calls=%async_computation.1 | async-start | bytes 1769472 | tf_op jit(solution)/shard_map/all_to_all | solution.py:339
  31.7 16.5 %collective-permute-start.19 = (bf16[17,72,128]{2,1,0:T(8,128)(2,1)}, bf16[17,72,128]{2,1,0:T(8,128)(2,1)}, u32[]{:S(2)}, u32[]{:S(2)}) collective-permute-start(bf16[17,72,128]{2,1,0:T(8,128)(2,1)} %param.19), channel_id=1, source_target_pairs={{0,192},{16,208},{32,224},{48,240},{64,256},{80,272},{96,288},{112... | collective-permute-start | bytes 940040 | tf_op jit(solution)/shard_map/cond/branch_19_fun/ppermute | solution.py:332
  59.5 28.1 %all-to-all-start.3 = ((bf16[16,192,128]{2,1,0:T(8,128)(2,1)}), bf16[16,192,128]{2,1,0:T(8,128)(2,1)S(1)}, u32[]{:S(2)}, u32[]{:S(2)}) async-start(bf16[16,192,128]{2,1,0:T(8,128)(2,1)} %attend_held.1), calls=%async_computation.3 | async-start | bytes 1572864 | tf_op jit(solution)/shard_map/all_to_all | solution.py:339
  68.0 15.4 %collective-permute-start.50 = (bf16[16,64,128]{2,1,0:T(8,128)(2,1)}, bf16[16,64,128]{2,1,0:T(8,128)(2,1)}, u32[]{:S(2)}, u32[]{:S(2)}) collective-permute-start(bf16[16,64,128]{2,1,0:T(8,128)(2,1)} %param.50), channel_id=1, source_target_pairs={{0,320},{16,336},{32,352},{48,368},{64,384},{80,400},{96,416},{112... | collective-permute-start | bytes 786440 | tf_op jit(solution)/shard_map/cond/branch_19_fun/ppermute | solution.py:332
  87.6 15.7 %all-to-all-start.2 = ((bf16[16,64,128]{2,1,0:T(8,128)(2,1)}), bf16[16,64,128]{2,1,0:T(8,128)(2,1)S(1)}, u32[]{:S(2)}, u32[]{:S(2)}) async-start(bf16[16,64,128]{2,1,0:T(8,128)(2,1)} %get-tuple-element.146), calls=%async_computation.2 | async-start | bytes 524288 | tf_op jit(solution)/shard_map/all_to_all | solution.py:339
  91.6 1.2 %copy-start.1 = (bf16[8,512,128]{2,1,0:T(8,128)(2,1)S(1)}, bf16[8,512,128]{2,1,0:T(8,128)(2,1)}, u32[]{:S(2)}) copy-start(bf16[8,512,128]{2,1,0:T(8,128)(2,1)} %w_ref.3) | copy-start | bytes 3145732
  92.9 10.5 %copy-start.2 = (bf16[8,512,128]{2,1,0:T(8,128)(2,1)S(1)}, bf16[8,512,128]{2,1,0:T(8,128)(2,1)}, u32[]{:S(2)}) copy-start(bf16[8,512,128]{2,1,0:T(8,128)(2,1)} %w_ref.3) | copy-start | bytes 3145732

commit v5 on v4

--- a/solution.py
+++ b/solution.py
@@ -113,10 +113,15 @@
     )(in_hbm(q_nope), in_hbm(q_rope), in_hbm(w_absorb_k))
 
 
-def attend_unit(query, keys, live):
-    scores = lax.dot_general(
+def scores_of(query, keys):
+    return lax.dot_general(
         query, keys, (((1,), (1,)), ((), ())), preferred_element_type=jnp.float32
     )
+
+
+def attend_unit(query, keys, live, scores=None):
+    if scores is None:
+        scores = scores_of(query, keys)
     position = lax.broadcasted_iota(jnp.int32, scores.shape, 1)
     scores = jnp.where(position < live, scores, HIDDEN)
     peak = jnp.max(scores, axis=1, keepdims=True)
@@ -206,6 +211,7 @@
     pair = unit_rows(got_ref, 3 * span)
     ropes = [pair[:, :ROPE], pair[:, ROPE:], packed_rope(got_ref, 3 * span + UNIT)]
     sends = []
+    jobs = []
     for place, units in enumerate([[(0, 0)], [(1, 0), (2, 2)]]):
         queries = []
         lives = []
@@ -215,7 +221,9 @@
             rows = queries[-1].shape[0]
             lives.append(counts_ref[place] + step_of_row(rows, first_step) + 1)
         query = jnp.concatenate(queries, axis=0)
-        mixed = attend_unit(query, keys[place], jnp.concatenate(lives, axis=0))
+        jobs.append((place, units, query, jnp.concatenate(lives, axis=0), scores_of(query, keys[place])))
+    for place, units, query, live, scores in jobs:
+        mixed = attend_unit(query, keys[place], live, scores)
         for number, (unit, _) in enumerate(units):
             put_unit(out_ref, unit * span, mixed[number * rows : (number + 1) * rows])
             send = pltpu.make_async_copy(

time: 107 us -> 107 us (level); the launches traced: 104 us -> 106 us
  starting transfers between devices: 34.9 us -> 36.4 us
    all_to_all x4, waiting for transfers between devices: 24.8 us -> 34.8 us  [exchanged(): lax.all_to_all(value, 'head', split_axis=0, concat_axis=0, tiled=True)]
    ppermute x2, waiting for transfers between devices: 21.8 us -> 12.1 us  [along(): return lambda given: lax.ppermute(given, 'grp', pairs)]
    all_to_all x4, starting transfers between devices: 24.8 us -> 26.6 us  [exchanged(): lax.all_to_all(value, 'head', split_axis=0, concat_axis=0, tiled=True)]
where the time goes in v5:
time: 107 us; the launch traced here: 106 us
  waiting for transfers between devices  46.9 us (44%)
  starting transfers between devices  36.4 us (34%)
  Pallas kernels  16.9 us (16%)
  local copies, waits for them, and re-layouts  4.36 us (4%)
    all_to_all x4, waiting for transfers between devices, exchanged(): lax.all_to_all(value, 'head', split_axis=0, concat_axis=0, tiled=True)  34.8 us
    all_to_all x4, starting transfers between devices, exchanged(): lax.all_to_all(value, 'head', split_axis=0, concat_axis=0, tiled=True)  26.6 us
    ppermute x2, waiting for transfers between devices, along(): return lambda given: lax.ppermute(given, 'grp', pairs)  12.1 us
    ppermute x2, starting transfers between devices, along(): return lambda given: lax.ppermute(given, 'grp', pairs)  9.81 us
    pallas_call x2, Pallas kernels, attend(): pl.pallas_call(kernel, out_shape=pltpu.HBM(shape, jnp.bfloat16), in_specs...  7.09 us
    pallas_call x2, Pallas kernels, absorb(): pl.pallas_call(functools.partial(absorb_kernel, steps, units), out_shape=...  5.77 us
    unnamed x9, local copies, waits for them, and re-layouts  3.6 us
    pallas_call x2, Pallas kernels, project(): pl.pallas_call(kernel, out_shape=jax.ShapeDtypeStruct((4, columns * UNIT,...  2.15 us
  transfers between devices with their start and end apart: 6, of which 6 were waited for; matrix products, arithmetic and copies ran while one was open for 1% of the time, Pallas kernels for 9%

profile of v5, /device:TPU:1, one launch (start us, length us, event | category | flops | bytes accessed | tf_op | source)
XLA Modules:
  0.0 106.1 jit_solution(7830889537959167601)
XLA Ops:
  0.0 2.5 %absorb_moved.1 = bf16[16,72,128]{2,1,0:T(8,128)(2,1)} custom-call(bf16[4,256,128]{2,1,0:T(8,128)(2,1)} %bitcast.10, bf16[4,256,64]{2,1,0:T(8,128)(2,1)} %bitcast.12, bf16[8,128,512]{2,1,0:T(8,128)(2,1)} %w_hbm.3), custom_call_target="tpu_custom_call" | custom-call | flops 268435456 | bytes 3145728 | tf_op jit(solution)/shard_map/absorb_moved/pallas_call | solution.py:96
  2.5 11.8 %all-to-all-start = ((bf16[16,72,128]{2,1,0:T(8,128)(2,1)}), bf16[16,72,128]{2,1,0:T(8,128)(2,1)S(1)}, u32[]{:S(2)}, u32[]{:S(2)}) async-start(bf16[16,72,128]{2,1,0:T(8,128)(2,1)} %absorb_moved.1), calls=%async_computation | async-start | bytes 589824 | tf_op jit(solution)/shard_map/all_to_all | solution.py:347
  15.8 1.7 %copy-done = bf16[2,1024,576]{1,2,0:T(8,128)(2,1)S(1)} copy-done((bf16[2,1024,576]{1,2,0:T(8,128)(2,1)S(1)}, bf16[2,1024,576]{1,2,0:T(8,128)(2,1)}, u32[]{:S(2)}) %copy-start) | copy-done | bytes 2359320
  17.5 1.8 %prepare.1 = (bf16[2,1024,576]{2,1,0:T(8,128)(2,1)S(1)}, bf16[1,72,128]{2,1,0:T(8,128)(2,1)}) custom-call(s32[2]{0:T(128)S(1)} %dynamic_slice.3.counts_ref, bf16[2,576,1024]{2,1,0:T(8,128)(2,1)S(1)} %bitcast.8, bf16[2,4,576]{2,1,0:T(4,128)(2,1)S(1)} %bitcast.9), custom_call_target="tpu_custom_call" | custom-call | flops 1048576 | bytes 8388608 | tf_op jit(solution)/shard_map/prepare/pallas_call | solution.py:182
  19.3 3.3 %absorb_held.1 = bf16[16,216,128]{2,1,0:T(8,128)(2,1)} custom-call(bf16[4,256,128]{2,1,0:T(8,128)(2,1)} %bitcast.11, bf16[4,256,64]{2,1,0:T(8,128)(2,1)} %bitcast.13, bf16[8,128,512]{2,1,0:T(8,128)(2,1)} %w_hbm.3), custom_call_target="tpu_custom_call" | custom-call | flops 805306368 | bytes 3145728 | tf_op jit(solution)/shard_map/absorb_held/pallas_call | solution.py:96
  22.6 4.1 %all-to-all-done = bf16[16,72,128]{2,1,0:T(8,128)(2,1)S(1)} async-done(((bf16[16,72,128]{2,1,0:T(8,128)(2,1)}), bf16[16,72,128]{2,1,0:T(8,128)(2,1)S(1)}, u32[]{:S(2)}, u32[]{:S(2)}) %all-to-all-start) | async-done | bytes 294944 | tf_op jit(solution)/shard_map/all_to_all | solution.py:347
  26.7 0.8 pad_maximum_fusion
  27.5 3.5 %all-to-all-start.1 = ((bf16[16,216,128]{2,1,0:T(8,128)(2,1)}), bf16[16,216,128]{2,1,0:T(8,128)(2,1)S(1)}, u32[]{:S(2)}, u32[]{:S(2)}) async-start(bf16[16,216,128]{2,1,0:T(8,128)(2,1)} %absorb_held.1), calls=%async_computation.1 | async-start | bytes 1769472 | tf_op jit(solution)/shard_map/all_to_all | solution.py:347
  31.7 12.1 %conditional.2 = (bf16[17,72,128]{2,1,0:T(8,128)(2,1)}) conditional(s32[]{:T(128)} %bitcast, bf16[17,72,128]{2,1,0:T(8,128)(2,1)} %pad_maximum_fusion, bf16[17,72,128]{2,1,0:T(8,128)(2,1)} %pad_maximum_fusion, bf16[17,72,128]{2,1,0:T(8,128)(2,1)} %pad_maximum_fusion, ...), branch_computations={%region_0.0_spmd, %region_1.0_spmd, %region_2.0_spmd, %region_3.0_... | conditional | bytes 1253424 | solution.py:343
  31.7 6.0 %collective-permute-start.2 = (bf16[17,72,128]{2,1,0:T(8,128)(2,1)}, bf16[17,72,128]{2,1,0:T(8,128)(2,1)}, u32[]{:S(2)}, u32[]{:S(2)}) collective-permute-start(bf16[17,72,128]{2,1,0:T(8,128)(2,1)} %param.2), channel_id=1, source_target_pairs={{0,464},{16,480},{32,496},{48,0},{64,16},{80,32},{96,48},{112,64},... | collective-permute-start | bytes 940040 | tf_op jit(solution)/shard_map/cond/branch_2_fun/ppermute | solution.py:340
  37.7 6.0 %collective-permute-done.2 = bf16[17,72,128]{2,1,0:T(8,128)(2,1)} collective-permute-done((bf16[17,72,128]{2,1,0:T(8,128)(2,1)}, bf16[17,72,128]{2,1,0:T(8,128)(2,1)}, u32[]{:S(2)}, u32[]{:S(2)}) %collective-permute-start.2) | collective-permute-done | bytes 313376 | tf_op jit(solution)/shard_map/cond/branch_2_fun/ppermute | solution.py:340
  43.8 11.5 %all-to-all-done.1.got_ref = bf16[16,216,128]{2,1,0:T(8,128)(2,1)S(1)} async-done(((bf16[16,216,128]{2,1,0:T(8,128)(2,1)}), bf16[16,216,128]{2,1,0:T(8,128)(2,1)S(1)}, u32[]{:S(2)}, u32[]{:S(2)}) %all-to-all-start.1) | async-done | bytes 884768 | tf_op jit(solution)/shard_map/all_to_all | solution.py:347
  55.3 4.1 %attend_held.1 = bf16[16,192,128]{2,1,0:T(8,128)(2,1)} custom-call(s32[2]{0:T(128)S(1)} %dynamic_slice.3.counts_ref, bf16[16,216,128]{2,1,0:T(8,128)(2,1)S(1)} %all-to-all-done.1.got_ref, bf16[2,1024,576]{2,1,0:T(8,128)(2,1)S(1)} %get-tuple-element.142.keys.keys_ref), custom_call_target="tpu_custom_call" | custom-call | flops 1811939328 | bytes 6291456 | tf_op jit(solution)/shard_map/attend_held/pallas_call | solution.py:267
  59.3 4.1 %all-to-all-start.3 = ((bf16[16,192,128]{2,1,0:T(8,128)(2,1)}), bf16[16,192,128]{2,1,0:T(8,128)(2,1)S(1)}, u32[]{:S(2)}, u32[]{:S(2)}) async-start(bf16[16,192,128]{2,1,0:T(8,128)(2,1)} %attend_held.1), calls=%async_computation.3 | async-start | bytes 1572864 | tf_op jit(solution)/shard_map/all_to_all | solution.py:347
  63.5 3.0 %attend_moved.1 = bf16[16,64,128]{2,1,0:T(8,128)(2,1)} custom-call(s32[2]{0:T(128)S(1)} %dynamic_slice.3.counts_ref, bf16[17,72,128]{2,1,0:T(8,128)(2,1)} %get-tuple-element.145.got_ref, bf16[2,1024,576]{2,1,0:T(8,128)(2,1)S(1)} %get-tuple-element.142.keys.keys_ref), custom_call_target="tpu_custom_call" | custom-call | flops 603979776 | bytes 2097152 | tf_op jit(solution)/shard_map/attend_moved/pallas_call | solution.py:267
  66.5 9.9 %conditional.3 = (bf16[16,64,128]{2,1,0:T(8,128)(2,1)}) conditional(s32[]{:T(128)} %bitcast, bf16[16,64,128]{2,1,0:T(8,128)(2,1)} %attend_moved.1, bf16[16,64,128]{2,1,0:T(8,128)(2,1)} %attend_moved.1, bf16[16,64,128]{2,1,0:T(8,128)(2,1)} %attend_moved.1, bf16[16,64,128]{2,1,0:T(8,128)(2,1)} %attend_moved.1, ...), branch_computations={%region_31.0_spmd, %region_32.0_spmd, %region_33.0_spmd, %region_3... | conditional | bytes 1048624 | solution.py:343
  66.5 3.8 %collective-permute-start.33 = (bf16[16,64,128]{2,1,0:T(8,128)(2,1)}, bf16[16,64,128]{2,1,0:T(8,128)(2,1)}, u32[]{:S(2)}, u32[]{:S(2)}) collective-permute-start(bf16[16,64,128]{2,1,0:T(8,128)(2,1)} %param.33), channel_id=1, source_target_pairs={{0,48},{16,64},{32,80},{48,96},{64,112},{80,128},{96,144},{112,160... | collective-permute-start | bytes 786440 | tf_op jit(solution)/shard_map/cond/branch_2_fun/ppermute | solution.py:340
  70.3 6.0 %collective-permute-done.33 = bf16[16,64,128]{2,1,0:T(8,128)(2,1)} collective-permute-done((bf16[16,64,128]{2,1,0:T(8,128)(2,1)}, bf16[16,64,128]{2,1,0:T(8,128)(2,1)}, u32[]{:S(2)}, u32[]{:S(2)}) %collective-permute-start.33) | collective-permute-done | bytes 262176 | tf_op jit(solution)/shard_map/cond/branch_2_fun/ppermute | solution.py:340
  76.4 9.8 %all-to-all-done.3.got_ref = bf16[16,192,128]{2,1,0:T(8,128)(2,1)S(1)} async-done(((bf16[16,192,128]{2,1,0:T(8,128)(2,1)}), bf16[16,192,128]{2,1,0:T(8,128)(2,1)S(1)}, u32[]{:S(2)}, u32[]{:S(2)}) %all-to-all-start.3) | async-done | bytes 786464 | tf_op jit(solution)/shard_map/all_to_all | solution.py:347
  86.1 7.1 %all-to-all-start.2 = ((bf16[16,64,128]{2,1,0:T(8,128)(2,1)}), bf16[16,64,128]{2,1,0:T(8,128)(2,1)S(1)}, u32[]{:S(2)}, u32[]{:S(2)}) async-start(bf16[16,64,128]{2,1,0:T(8,128)(2,1)} %get-tuple-element.146), calls=%async_computation.2 | async-start | bytes 524288 | tf_op jit(solution)/shard_map/all_to_all | solution.py:347
  93.3 1.2 %copy-done.1 = bf16[8,512,128]{2,1,0:T(8,128)(2,1)S(1)} copy-done((bf16[8,512,128]{2,1,0:T(8,128)(2,1)S(1)}, bf16[8,512,128]{2,1,0:T(8,128)(2,1)}, u32[]{:S(2)}) %copy-start.1) | copy-done | bytes 1048600
  94.5 1.0 project_held.1.part_ref
  95.5 9.5 %all-to-all-done.2.got_ref = bf16[16,64,128]{2,1,0:T(8,128)(2,1)S(1)} async-done(((bf16[16,64,128]{2,1,0:T(8,128)(2,1)}), bf16[16,64,128]{2,1,0:T(8,128)(2,1)S(1)}, u32[]{:S(2)}, u32[]{:S(2)}) %all-to-all-start.2) | async-done | bytes 262176 | tf_op jit(solution)/shard_map/all_to_all | solution.py:347
  105.0 1.1 %project_moved.1 = bf16[4,256,128]{2,1,0:T(8,128)(2,1)} custom-call(bf16[16,64,128]{2,1,0:T(8,128)(2,1)S(1)} %all-to-all-done.2.got_ref, bf16[8,512,128]{2,1,0:T(8,128)(2,1)S(1)} %copy-done.2, bf16[4,256,128]{2,1,0:T(8,128)(2,1)S(1)} %project_held.1.part_ref), custom_call_target="tpu_custom_call" | custom-call | flops 268435456 | bytes 2097152 | tf_op jit(solution)/shard_map/project_moved/pallas_call | solution.py:324
  (8 shorter events, 1.5 us)
Async XLA Ops:
  2.5 24.2 %all-to-all-start = ((bf16[16,72,128]{2,1,0:T(8,128)(2,1)}), bf16[16,72,128]{2,1,0:T(8,128)(2,1)S(1)}, u32[]{:S(2)}, u32[]{:S(2)}) async-start(bf16[16,72,128]{2,1,0:T(8,128)(2,1)} %absorb_moved.1), calls=%async_computation | async-start | bytes 589824 | tf_op jit(solution)/shard_map/all_to_all | solution.py:347
  15.8 1.7 %copy-start = (bf16[2,1024,576]{1,2,0:T(8,128)(2,1)S(1)}, bf16[2,1024,576]{1,2,0:T(8,128)(2,1)}, u32[]{:S(2)}) copy-start(bf16[2,1024,576]{1,2,0:T(8,128)(2,1)} %param.74) | copy-start | bytes 7077892
  19.3 7.4 %copy-start.3 = (bf16[1,72,128]{2,1,0:T(8,128)(2,1)S(1)}, bf16[1,72,128]{2,1,0:T(8,128)(2,1)}, u32[]{:S(2)}) copy-start(bf16[1,72,128]{2,1,0:T(8,128)(2,1)} %get-tuple-element.139) | copy-start | bytes 55300
  27.5 27.8 %all-to-all-start.1 = ((bf16[16,216,128]{2,1,0:T(8,128)(2,1)}), bf16[16,216,128]{2,1,0:T(8,128)(2,1)S(1)}, u32[]{:S(2)}, u32[]{:S(2)}) async-start(bf16[16,216,128]{2,1,0:T(8,128)(2,1)} %absorb_held.1), calls=%async_computation.1 | async-start | bytes 1769472 | tf_op jit(solution)/shard_map/all_to_all | solution.py:347
  31.7 12.1 %collective-permute-start.2 = (bf16[17,72,128]{2,1,0:T(8,128)(2,1)}, bf16[17,72,128]{2,1,0:T(8,128)(2,1)}, u32[]{:S(2)}, u32[]{:S(2)}) collective-permute-start(bf16[17,72,128]{2,1,0:T(8,128)(2,1)} %param.2), channel_id=1, source_target_pairs={{0,464},{16,480},{32,496},{48,0},{64,16},{80,32},{96,48},{112,64},... | collective-permute-start | bytes 940040 | tf_op jit(solution)/shard_map/cond/branch_2_fun/ppermute | solution.py:340
  59.3 26.8 %all-to-all-start.3 = ((bf16[16,192,128]{2,1,0:T(8,128)(2,1)}), bf16[16,192,128]{2,1,0:T(8,128)(2,1)S(1)}, u32[]{:S(2)}, u32[]{:S(2)}) async-start(bf16[16,192,128]{2,1,0:T(8,128)(2,1)} %attend_held.1), calls=%async_computation.3 | async-start | bytes 1572864 | tf_op jit(solution)/shard_map/all_to_all | solution.py:347
  66.5 9.8 %collective-permute-start.33 = (bf16[16,64,128]{2,1,0:T(8,128)(2,1)}, bf16[16,64,128]{2,1,0:T(8,128)(2,1)}, u32[]{:S(2)}, u32[]{:S(2)}) collective-permute-start(bf16[16,64,128]{2,1,0:T(8,128)(2,1)} %param.33), channel_id=1, source_target_pairs={{0,48},{16,64},{32,80},{48,96},{64,112},{80,128},{96,144},{112,160... | collective-permute-start | bytes 786440 | tf_op jit(solution)/shard_map/cond/branch_2_fun/ppermute | solution.py:340
  86.1 18.8 %all-to-all-start.2 = ((bf16[16,64,128]{2,1,0:T(8,128)(2,1)}), bf16[16,64,128]{2,1,0:T(8,128)(2,1)S(1)}, u32[]{:S(2)}, u32[]{:S(2)}) async-start(bf16[16,64,128]{2,1,0:T(8,128)(2,1)} %get-tuple-element.146), calls=%async_computation.2 | async-start | bytes 524288 | tf_op jit(solution)/shard_map/all_to_all | solution.py:347
  93.3 1.2 %copy-start.1 = (bf16[8,512,128]{2,1,0:T(8,128)(2,1)S(1)}, bf16[8,512,128]{2,1,0:T(8,128)(2,1)}, u32[]{:S(2)}) copy-start(bf16[8,512,128]{2,1,0:T(8,128)(2,1)} %w_ref.3) | copy-start | bytes 3145732
  94.5 10.5 %copy-start.2 = (bf16[8,512,128]{2,1,0:T(8,128)(2,1)S(1)}, bf16[8,512,128]{2,1,0:T(8,128)(2,1)}, u32[]{:S(2)}) copy-start(bf16[8,512,128]{2,1,0:T(8,128)(2,1)} %w_ref.3) | copy-start | bytes 3145732

commit v6 on v5

--- a/solution.py
+++ b/solution.py
@@ -369,14 +369,15 @@
     held_out, keys, moved_in = lax.optimization_barrier((held_out, keys, moved_in))
     held_in = exchanged(held_out)
     moved_in = shifted(moved_in, shift, -1)
+    moved_mixed = attend(
+        attend_moved_kernel, counts, moved_in, keys, columns, 1, "attend_moved"
+    )
+    keys, moved_mixed = lax.optimization_barrier((keys, moved_mixed))
     held_mixed = attend(
         attend_held_kernel, counts, held_in, keys, columns, 3, "attend_held"
     )
-    moved_in, held_mixed = lax.optimization_barrier((moved_in, held_mixed))
+    held_mixed, moved_mixed = lax.optimization_barrier((held_mixed, moved_mixed))
     held_back = exchanged(held_mixed)
-    moved_mixed = attend(
-        attend_moved_kernel, counts, moved_in, keys, columns, 1, "attend_moved"
-    )
     moved_back = exchanged(shifted(moved_mixed, shift, 1))
     part = project(project_held_kernel, (held_back, w_absorb_v), 3, "project_held")
     out = project(project_moved_kernel, (moved_back, w_absorb_v, part), 1, "project_moved")

time: 107 us -> 113 us (1.056)
  the two profiles are of different devices: /device:TPU:1 before, /device:TPU:9 now
where the time goes in v6:
time: 113 us; the launch traced here: 112 us
  waiting for transfers between devices  50.8 us (45%)
  starting transfers between devices  38.9 us (34%)
  Pallas kernels  16.8 us (15%)
  local copies, waits for them, and re-layouts  4.36 us (4%)
    all_to_all x4, waiting for transfers between devices, exchanged(): lax.all_to_all(value, 'head', split_axis=0, concat_axis=0, tiled=True)  33.2 us
    all_to_all x4, starting transfers between devices, exchanged(): lax.all_to_all(value, 'head', split_axis=0, concat_axis=0, tiled=True)  32.9 us
    ppermute x2, waiting for transfers between devices, along(): return lambda given: lax.ppermute(given, 'grp', pairs)  17.6 us
    pallas_call x2, Pallas kernels, attend(): pl.pallas_call(kernel, out_shape=pltpu.HBM(shape, jnp.bfloat16), in_specs...  7.09 us
    ppermute x2, starting transfers between devices, along(): return lambda given: lax.ppermute(given, 'grp', pairs)  5.98 us
    pallas_call x2, Pallas kernels, absorb(): pl.pallas_call(functools.partial(absorb_kernel, steps, units), out_shape=...  5.76 us
    unnamed x9, local copies, waits for them, and re-layouts  3.6 us
  transfers between devices with their start and end apart: 6, of which 6 were waited for; matrix products, arithmetic and copies ran while one was open for 1% of the time, Pallas kernels for 8%

profile of v6, /device:TPU:9, one launch (start us, length us, event | category | flops | bytes accessed | tf_op | source)
XLA Modules:
  0.0 112.4 jit_solution(9312799609829922442)
XLA Ops:
  0.0 2.5 %absorb_moved.1 = bf16[16,72,128]{2,1,0:T(8,128)(2,1)} custom-call(bf16[4,256,128]{2,1,0:T(8,128)(2,1)} %bitcast.10, bf16[4,256,64]{2,1,0:T(8,128)(2,1)} %bitcast.12, bf16[8,128,512]{2,1,0:T(8,128)(2,1)} %w_hbm.3), custom_call_target="tpu_custom_call" | custom-call | flops 268435456 | bytes 3145728 | tf_op jit(solution)/shard_map/absorb_moved/pallas_call | solution.py:96
  2.5 11.0 %all-to-all-start = ((bf16[16,72,128]{2,1,0:T(8,128)(2,1)}), bf16[16,72,128]{2,1,0:T(8,128)(2,1)S(1)}, u32[]{:S(2)}, u32[]{:S(2)}) async-start(bf16[16,72,128]{2,1,0:T(8,128)(2,1)} %absorb_moved.1), calls=%async_computation | async-start | bytes 589824 | tf_op jit(solution)/shard_map/all_to_all | solution.py:347
  15.0 1.7 %copy-done = bf16[2,1024,576]{1,2,0:T(8,128)(2,1)S(1)} copy-done((bf16[2,1024,576]{1,2,0:T(8,128)(2,1)S(1)}, bf16[2,1024,576]{1,2,0:T(8,128)(2,1)}, u32[]{:S(2)}) %copy-start) | copy-done | bytes 2359320
  16.6 1.8 %prepare.1 = (bf16[2,1024,576]{2,1,0:T(8,128)(2,1)S(1)}, bf16[1,72,128]{2,1,0:T(8,128)(2,1)}) custom-call(s32[2]{0:T(128)S(1)} %dynamic_slice.3.counts_ref, bf16[2,576,1024]{2,1,0:T(8,128)(2,1)S(1)} %bitcast.8, bf16[2,4,576]{2,1,0:T(4,128)(2,1)S(1)} %bitcast.9), custom_call_target="tpu_custom_call" | custom-call | flops 1048576 | bytes 8388608 | tf_op jit(solution)/shard_map/prepare/pallas_call | solution.py:182
  18.5 3.3 %absorb_held.1 = bf16[16,216,128]{2,1,0:T(8,128)(2,1)} custom-call(bf16[4,256,128]{2,1,0:T(8,128)(2,1)} %bitcast.11, bf16[4,256,64]{2,1,0:T(8,128)(2,1)} %bitcast.13, bf16[8,128,512]{2,1,0:T(8,128)(2,1)} %w_hbm.3), custom_call_target="tpu_custom_call" | custom-call | flops 805306368 | bytes 3145728 | tf_op jit(solution)/shard_map/absorb_held/pallas_call | solution.py:96
  21.8 4.1 %all-to-all-done = bf16[16,72,128]{2,1,0:T(8,128)(2,1)S(1)} async-done(((bf16[16,72,128]{2,1,0:T(8,128)(2,1)}), bf16[16,72,128]{2,1,0:T(8,128)(2,1)S(1)}, u32[]{:S(2)}, u32[]{:S(2)}) %all-to-all-start) | async-done | bytes 294944 | tf_op jit(solution)/shard_map/all_to_all | solution.py:347
  25.9 0.8 pad_maximum_fusion
  26.6 3.5 %all-to-all-start.1 = ((bf16[16,216,128]{2,1,0:T(8,128)(2,1)}), bf16[16,216,128]{2,1,0:T(8,128)(2,1)S(1)}, u32[]{:S(2)}, u32[]{:S(2)}) async-start(bf16[16,216,128]{2,1,0:T(8,128)(2,1)} %absorb_held.1), calls=%async_computation.1 | async-start | bytes 1769472 | tf_op jit(solution)/shard_map/all_to_all | solution.py:347
  30.8 13.6 %conditional.2 = (bf16[17,72,128]{2,1,0:T(8,128)(2,1)}) conditional(s32[]{:T(128)} %bitcast, bf16[17,72,128]{2,1,0:T(8,128)(2,1)} %pad_maximum_fusion, bf16[17,72,128]{2,1,0:T(8,128)(2,1)} %pad_maximum_fusion, bf16[17,72,128]{2,1,0:T(8,128)(2,1)} %pad_maximum_fusion, ...), branch_computations={%region_0.0_spmd, %region_1.0_spmd, %region_2.0_spmd, %region_3.0_... | conditional | bytes 1253424 | solution.py:343
  30.9 3.1 %collective-permute-start.30 = (bf16[17,72,128]{2,1,0:T(8,128)(2,1)}, bf16[17,72,128]{2,1,0:T(8,128)(2,1)}, u32[]{:S(2)}, u32[]{:S(2)}) collective-permute-start(bf16[17,72,128]{2,1,0:T(8,128)(2,1)} %param.30), channel_id=1, source_target_pairs={{0,16},{16,32},{32,48},{48,64},{64,80},{80,96},{96,112},{112,128},... | collective-permute-start | bytes 940040 | tf_op jit(solution)/shard_map/cond/branch_30_fun/ppermute | solution.py:340
  34.0 10.5 %collective-permute-done.30 = bf16[17,72,128]{2,1,0:T(8,128)(2,1)} collective-permute-done((bf16[17,72,128]{2,1,0:T(8,128)(2,1)}, bf16[17,72,128]{2,1,0:T(8,128)(2,1)}, u32[]{:S(2)}, u32[]{:S(2)}) %collective-permute-start.30) | collective-permute-done | bytes 313376 | tf_op jit(solution)/shard_map/cond/branch_30_fun/ppermute | solution.py:340
  44.4 3.0 %attend_moved.1 = bf16[16,64,128]{2,1,0:T(8,128)(2,1)} custom-call(s32[2]{0:T(128)S(1)} %dynamic_slice.3.counts_ref, bf16[17,72,128]{2,1,0:T(8,128)(2,1)} %get-tuple-element.149.got_ref, bf16[2,1024,576]{2,1,0:T(8,128)(2,1)S(1)} %get-tuple-element.145.keys_ref.keys), custom_call_target="tpu_custom_call" | custom-call | flops 603979776 | bytes 2097152 | tf_op jit(solution)/shard_map/attend_moved/pallas_call | solution.py:267
  47.5 6.9 %all-to-all-done.1.got_ref = bf16[16,216,128]{2,1,0:T(8,128)(2,1)S(1)} async-done(((bf16[16,216,128]{2,1,0:T(8,128)(2,1)}), bf16[16,216,128]{2,1,0:T(8,128)(2,1)S(1)}, u32[]{:S(2)}, u32[]{:S(2)}) %all-to-all-start.1) | async-done | bytes 884768 | tf_op jit(solution)/shard_map/all_to_all | solution.py:347
  54.4 4.1 %attend_held.1 = bf16[16,192,128]{2,1,0:T(8,128)(2,1)} custom-call(s32[2]{0:T(128)S(1)} %dynamic_slice.3.counts_ref, bf16[16,216,128]{2,1,0:T(8,128)(2,1)S(1)} %all-to-all-done.1.got_ref, bf16[2,1024,576]{2,1,0:T(8,128)(2,1)S(1)} %get-tuple-element.145.keys_ref.keys), custom_call_target="tpu_custom_call" | custom-call | flops 1811939328 | bytes 6291456 | tf_op jit(solution)/shard_map/attend_held/pallas_call | solution.py:267
  58.5 12.8 %all-to-all-start.3 = ((bf16[16,192,128]{2,1,0:T(8,128)(2,1)}), bf16[16,192,128]{2,1,0:T(8,128)(2,1)S(1)}, u32[]{:S(2)}, u32[]{:S(2)}) async-start(bf16[16,192,128]{2,1,0:T(8,128)(2,1)} %attend_held.1), calls=%async_computation.3 | async-start | bytes 1572864 | tf_op jit(solution)/shard_map/all_to_all | solution.py:347
  71.3 10.0 %conditional.3 = (bf16[16,64,128]{2,1,0:T(8,128)(2,1)}) conditional(s32[]{:T(128)} %bitcast, bf16[16,64,128]{2,1,0:T(8,128)(2,1)} %attend_moved.1, bf16[16,64,128]{2,1,0:T(8,128)(2,1)} %attend_moved.1, bf16[16,64,128]{2,1,0:T(8,128)(2,1)} %attend_moved.1, bf16[16,64,128]{2,1,0:T(8,128)(2,1)} %attend_moved.1, ...), branch_computations={%region_31.0_spmd, %region_32.0_spmd, %region_33.0_spmd, %region_3... | conditional | bytes 1048624 | solution.py:343
  71.3 2.9 %collective-permute-start.61 = (bf16[16,64,128]{2,1,0:T(8,128)(2,1)}, bf16[16,64,128]{2,1,0:T(8,128)(2,1)}, u32[]{:S(2)}, u32[]{:S(2)}) collective-permute-start(bf16[16,64,128]{2,1,0:T(8,128)(2,1)} %param.61), channel_id=1, source_target_pairs={{0,496},{16,0},{32,16},{48,32},{64,48},{80,64},{96,80},{112,96},{1... | collective-permute-start | bytes 786440 | tf_op jit(solution)/shard_map/cond/branch_30_fun/ppermute | solution.py:340
  74.2 7.1 %collective-permute-done.61 = bf16[16,64,128]{2,1,0:T(8,128)(2,1)} collective-permute-done((bf16[16,64,128]{2,1,0:T(8,128)(2,1)}, bf16[16,64,128]{2,1,0:T(8,128)(2,1)}, u32[]{:S(2)}, u32[]{:S(2)}) %collective-permute-start.61) | collective-permute-done | bytes 262176 | tf_op jit(solution)/shard_map/cond/branch_30_fun/ppermute | solution.py:340
  81.3 12.7 %all-to-all-done.3.got_ref = bf16[16,192,128]{2,1,0:T(8,128)(2,1)S(1)} async-done(((bf16[16,192,128]{2,1,0:T(8,128)(2,1)}), bf16[16,192,128]{2,1,0:T(8,128)(2,1)S(1)}, u32[]{:S(2)}, u32[]{:S(2)}) %all-to-all-start.3) | async-done | bytes 786464 | tf_op jit(solution)/shard_map/all_to_all | solution.py:347
  94.0 5.6 %all-to-all-start.2 = ((bf16[16,64,128]{2,1,0:T(8,128)(2,1)}), bf16[16,64,128]{2,1,0:T(8,128)(2,1)S(1)}, u32[]{:S(2)}, u32[]{:S(2)}) async-start(bf16[16,64,128]{2,1,0:T(8,128)(2,1)} %get-tuple-element.150), calls=%async_computation.2 | async-start | bytes 524288 | tf_op jit(solution)/shard_map/all_to_all | solution.py:347
  99.5 1.2 %copy-done.1 = bf16[8,512,128]{2,1,0:T(8,128)(2,1)S(1)} copy-done((bf16[8,512,128]{2,1,0:T(8,128)(2,1)S(1)}, bf16[8,512,128]{2,1,0:T(8,128)(2,1)}, u32[]{:S(2)}) %copy-start.1) | copy-done | bytes 1048600
  100.8 1.0 project_held.1.part_ref
  101.7 9.5 %all-to-all-done.2.got_ref = bf16[16,64,128]{2,1,0:T(8,128)(2,1)S(1)} async-done(((bf16[16,64,128]{2,1,0:T(8,128)(2,1)}), bf16[16,64,128]{2,1,0:T(8,128)(2,1)S(1)}, u32[]{:S(2)}, u32[]{:S(2)}) %all-to-all-start.2) | async-done | bytes 262176 | tf_op jit(solution)/shard_map/all_to_all | solution.py:347
  111.2 1.1 %project_moved.1 = bf16[4,256,128]{2,1,0:T(8,128)(2,1)} custom-call(bf16[16,64,128]{2,1,0:T(8,128)(2,1)S(1)} %all-to-all-done.2.got_ref, bf16[8,512,128]{2,1,0:T(8,128)(2,1)S(1)} %copy-done.2, bf16[4,256,128]{2,1,0:T(8,128)(2,1)S(1)} %project_held.1.part_ref), custom_call_target="tpu_custom_call" | custom-call | flops 268435456 | bytes 2097152 | tf_op jit(solution)/shard_map/project_moved/pallas_call | solution.py:324
  (8 shorter events, 1.5 us)
Async XLA Ops:
  2.5 23.4 %all-to-all-start = ((bf16[16,72,128]{2,1,0:T(8,128)(2,1)}), bf16[16,72,128]{2,1,0:T(8,128)(2,1)S(1)}, u32[]{:S(2)}, u32[]{:S(2)}) async-start(bf16[16,72,128]{2,1,0:T(8,128)(2,1)} %absorb_moved.1), calls=%async_computation | async-start | bytes 589824 | tf_op jit(solution)/shard_map/all_to_all | solution.py:347
  15.0 1.7 %copy-start = (bf16[2,1024,576]{1,2,0:T(8,128)(2,1)S(1)}, bf16[2,1024,576]{1,2,0:T(8,128)(2,1)}, u32[]{:S(2)}) copy-start(bf16[2,1024,576]{1,2,0:T(8,128)(2,1)} %param.74) | copy-start | bytes 7077892
  18.5 7.4 %copy-start.3 = (bf16[1,72,128]{2,1,0:T(8,128)(2,1)S(1)}, bf16[1,72,128]{2,1,0:T(8,128)(2,1)}, u32[]{:S(2)}) copy-start(bf16[1,72,128]{2,1,0:T(8,128)(2,1)} %get-tuple-element.141) | copy-start | bytes 55300
  26.6 27.8 %all-to-all-start.1 = ((bf16[16,216,128]{2,1,0:T(8,128)(2,1)}), bf16[16,216,128]{2,1,0:T(8,128)(2,1)S(1)}, u32[]{:S(2)}, u32[]{:S(2)}) async-start(bf16[16,216,128]{2,1,0:T(8,128)(2,1)} %absorb_held.1), calls=%async_computation.1 | async-start | bytes 1769472 | tf_op jit(solution)/shard_map/all_to_all | solution.py:347
  30.9 13.6 %collective-permute-start.30 = (bf16[17,72,128]{2,1,0:T(8,128)(2,1)}, bf16[17,72,128]{2,1,0:T(8,128)(2,1)}, u32[]{:S(2)}, u32[]{:S(2)}) collective-permute-start(bf16[17,72,128]{2,1,0:T(8,128)(2,1)} %param.30), channel_id=1, source_target_pairs={{0,16},{16,32},{32,48},{48,64},{64,80},{80,96},{96,112},{112,128},... | collective-permute-start | bytes 940040 | tf_op jit(solution)/shard_map/cond/branch_30_fun/ppermute | solution.py:340
  58.5 52.7 %copy-start.2 = (bf16[8,512,128]{2,1,0:T(8,128)(2,1)S(1)}, bf16[8,512,128]{2,1,0:T(8,128)(2,1)}, u32[]{:S(2)}) copy-start(bf16[8,512,128]{2,1,0:T(8,128)(2,1)} %w_ref.3) | copy-start | bytes 3145732
  58.5 35.4 %all-to-all-start.3 = ((bf16[16,192,128]{2,1,0:T(8,128)(2,1)}), bf16[16,192,128]{2,1,0:T(8,128)(2,1)S(1)}, u32[]{:S(2)}, u32[]{:S(2)}) async-start(bf16[16,192,128]{2,1,0:T(8,128)(2,1)} %attend_held.1), calls=%async_computation.3 | async-start | bytes 1572864 | tf_op jit(solution)/shard_map/all_to_all | solution.py:347
  71.3 10.0 %collective-permute-start.61 = (bf16[16,64,128]{2,1,0:T(8,128)(2,1)}, bf16[16,64,128]{2,1,0:T(8,128)(2,1)}, u32[]{:S(2)}, u32[]{:S(2)}) collective-permute-start(bf16[16,64,128]{2,1,0:T(8,128)(2,1)} %param.61), channel_id=1, source_target_pairs={{0,496},{16,0},{32,16},{48,32},{64,48},{80,64},{96,80},{112,96},{1... | collective-permute-start | bytes 786440 | tf_op jit(solution)/shard_map/cond/branch_30_fun/ppermute | solution.py:340
  94.0 17.3 %all-to-all-start.2 = ((bf16[16,64,128]{2,1,0:T(8,128)(2,1)}), bf16[16,64,128]{2,1,0:T(8,128)(2,1)S(1)}, u32[]{:S(2)}, u32[]{:S(2)}) async-start(bf16[16,64,128]{2,1,0:T(8,128)(2,1)} %get-tuple-element.150), calls=%async_computation.2 | async-start | bytes 524288 | tf_op jit(solution)/shard_map/all_to_all | solution.py:347
  99.5 1.2 %copy-start.1 = (bf16[8,512,128]{2,1,0:T(8,128)(2,1)S(1)}, bf16[8,512,128]{2,1,0:T(8,128)(2,1)}, u32[]{:S(2)}) copy-start(bf16[8,512,128]{2,1,0:T(8,128)(2,1)} %w_ref.3) | copy-start | bytes 3145732
